TPU v7x, 32 devices: a whole 2x2x4 slice. The times are simulated.
32 devices in a mesh: groups: 2 (over y), wide: 8 (over z, x), narrow: 2 (over core).
Axes of the slice: x: 2, y: 2, z: 4, core: 2. Of those that a mesh axis runs over, the one named last changes fastest.
Arguments:
- tokens: bfloat16 [4, 32, 18432], P(None, 'groups', ('narrow', 'wide')), parts along dimension 1, may hold values from -6 to 6
- norm_gain: bfloat16 [18432], P(('narrow', 'wide')), may hold values from 0.099609375 to 1.8984375
- w_query: bfloat16 [18432, 12288], P('narrow', 'wide'), may hold values from -0.046875 to 0.046875
- w_keyval: bfloat16 [18432, 512], P(('narrow', 'wide')), may hold values from -0.046875 to 0.046875
- w_out: bfloat16 [12288, 18432], P(None, ('narrow', 'wide')), may hold values from -0.0546875 to 0.0546875
- cache_keys: bfloat16 [32, 2048, 256], P(('groups', 'narrow', 'wide')), parts along dimension 0, may hold values from -3000 to 3000, as said below
- cache_values: bfloat16 [32, 2048, 256], P(('groups', 'narrow', 'wide')), parts along dimension 0, may hold values from -12 to 12
- lengths: int32 [32], P(('groups', 'narrow', 'wide')), parts along dimension 0, may hold values from 1 to 2044, as said below
Outputs:
- attended: bfloat16 [4, 32, 18432], P(None, 'groups', ('narrow', 'wide')), parts along dimension 1
There are 2 independent parts, one for each index of `groups`. A program takes and returns all parts, laid end to end along the dimension named above; an argument that names none is the same for every part. Nothing has to cross between parts.
Inputs may be any that keep to these rules, and one draw needn't show every extreme that they name: `cache_keys`: keys of cached tokens, already rotated; slots at or beyond a sequence's length hold data that is not read. `lengths`: in every part one sequence holds exactly 2044 valid tokens and one holds exactly 1.
All inputs are finite; a program needn't handle non-finite values.
Results may differ from a plain program's by a relative error of at most 0.0065.
The roundings to bfloat16 on the way count: a program that leaves them out, or rounds other values in their place, can miss the bound.
Values may be sent and summed in bfloat16 or wider, within the bound.
No kernel may reach another device: no remote copies, remote signals or barrier semaphores. Data moves between devices by JAX's collectives and lax.ppermute only.
A program may use at most 128 MiB of HBM per device.

v0:
```python
import jax
import jax.numpy as jnp
from jax import lax
from jax.sharding import PartitionSpec as P

H = 48
DH = 256
STEPS = 4


epsilon = 1e-06


def rotate(vectors, positions):
    half_size = vectors.shape[-1] // 2
    ladder = jnp.arange(half_size, dtype=jnp.float32)
    frequency = jnp.exp(ladder * (-2.0 / vectors.shape[-1]) * jnp.log(10000.0))
    angles = positions[..., None] * frequency
    cosine = jnp.cos(angles)
    sine = jnp.sin(angles)
    first_half = vectors[..., :half_size]
    second_half = vectors[..., half_size:]
    return jnp.concatenate(
        [first_half * cosine - second_half * sine, second_half * cosine + first_half * sine],
        axis=-1,
    )


def attend(rot_query, cache_keys, cache_values, new_keys, new_values, lengths):
    score_scale = 1.0 / jnp.sqrt(jnp.float32(DH))
    cache_scores = (
        jnp.einsum("bhd,bsd->bhs", rot_query, cache_keys, preferred_element_type=jnp.float32)
        * score_scale
    )
    valid = jnp.arange(cache_keys.shape[1])[None, None, :] < lengths[:, None, None]
    masked = jnp.where(valid, cache_scores, -1e30)
    fresh = (
        jnp.einsum("bhd,bjd->bhj", rot_query, new_keys, preferred_element_type=jnp.float32)
        * score_scale
    )
    highest = jnp.maximum(jnp.max(masked, axis=-1), jnp.max(fresh, axis=-1))[..., None]
    cache_weights = jnp.where(valid, jnp.exp(masked - highest), 0.0)
    fresh_weights = jnp.exp(fresh - highest)
    total = jnp.sum(cache_weights, axis=-1, keepdims=True) + jnp.sum(
        fresh_weights, axis=-1, keepdims=True
    )
    cache_probs = (cache_weights / total).astype(jnp.bfloat16)
    fresh_probs = (fresh_weights / total).astype(jnp.bfloat16)
    context = jnp.einsum(
        "bhs,bsd->bhd", cache_probs, cache_values, preferred_element_type=jnp.float32
    )
    context = context + jnp.einsum(
        "bhj,bjd->bhd", fresh_probs, new_values, preferred_element_type=jnp.float32
    )
    return context.astype(jnp.bfloat16)


def local(tokens, norm_gain, w_query, w_keyval, w_out, cache_keys, cache_values, lengths):
    wide_count = lax.axis_size("wide")
    narrow_count = lax.axis_size("narrow")
    batch = tokens.shape[1]
    width_total = tokens.shape[2] * wide_count * narrow_count
    local_batch = lengths.shape[0]
    gain_values = norm_gain.astype(jnp.float32)
    fresh_keys = []
    fresh_values = []
    results = []
    for step in range(STEPS):
        rows = tokens[step]
        rows_float = rows.astype(jnp.float32)
        row_sum, row_squares = lax.psum(
            (jnp.sum(rows_float, axis=1), jnp.sum(rows_float * rows_float, axis=1)),
            ("wide", "narrow"),
        )
        average = (row_sum / width_total)[:, None]
        spread = (row_squares / width_total)[:, None] - average * average
        normed = ((rows_float - average) * lax.rsqrt(spread + epsilon) * gain_values).astype(
            jnp.bfloat16
        )
        query_total = jnp.dot(
            lax.all_gather(normed, "wide", axis=1, tiled=True),
            w_query,
            preferred_element_type=jnp.float32,
        )
        keyval_part = jnp.dot(normed, w_keyval, preferred_element_type=jnp.float32)
        query_half, keyval_half = (
            lax.psum_scatter(query_total, "narrow", scatter_dimension=0, tiled=True),
            lax.psum_scatter(keyval_part, "narrow", scatter_dimension=0, tiled=True),
        )
        query_local = lax.all_to_all(
            query_half.astype(jnp.bfloat16), "wide", split_axis=0, concat_axis=1, tiled=True
        )
        keyval_local = lax.psum_scatter(keyval_half, "wide", scatter_dimension=0, tiled=True)
        positions = (lengths + step).astype(jnp.float32)
        rot_query = rotate(
            query_local.astype(jnp.float32).reshape(local_batch, H, DH), positions[:, None]
        ).astype(jnp.bfloat16)
        fresh_keys.append(rotate(keyval_local[:, :DH], positions).astype(jnp.bfloat16))
        fresh_values.append(keyval_local[:, DH:].astype(jnp.bfloat16))
        context = attend(
            rot_query,
            cache_keys,
            cache_values,
            jnp.stack(fresh_keys, axis=1),
            jnp.stack(fresh_values, axis=1),
            lengths,
        )
        context = context.reshape(local_batch, H * DH)
        joined = jnp.dot(
            lax.all_gather(context, ("wide", "narrow"), axis=0, tiled=True),
            w_out,
            preferred_element_type=jnp.float32,
        )
        attended = (
            joined.reshape(wide_count, narrow_count, local_batch, w_out.shape[1])
            .transpose(1, 0, 2, 3)
            .reshape(batch, w_out.shape[1])
        )
        results.append(attended.astype(jnp.bfloat16))
    return jnp.stack(results)


def solution(mesh):
    placed = (
        P(None, "groups", ("narrow", "wide")),
        P(("narrow", "wide")),
        P("narrow", "wide"),
        P(("narrow", "wide"), None),
        P(None, ("narrow", "wide")),
        P(("groups", "narrow", "wide"), None, None),
        P(("groups", "narrow", "wide"), None, None),
        P(("groups", "narrow", "wide")),
    )
    return jax.shard_map(
        local,
        mesh=mesh,
        in_specs=placed,
        out_specs=P(None, "groups", ("narrow", "wide")),
        check_vma=False,
    )
```

profile of v0, /device:TPU:0, one launch (start us, length us, event | category | flops | bytes accessed | tf_op | source)
XLA Modules:
  0.0 421.6 jit_solution(10983677006878170636)
XLA Ops:
  6.5 1.1 convert_reduce_fusion.3
  7.6 1.0 fusion.57
  8.6 0.7 convert_element_type.314
  9.3 34.9 %all-reduce.4 = (f32[16]{0:T(128)S(1)}, f32[16]{0:T(128)S(1)}, f32[16]{0:T(128)S(1)}, f32[16]{0:T(128)S(1)}, f32[16]{0:T(128)S(1)}, /*index=5*/f32[16]{0:T(128)S(1)}, f32[16]{0:T(128)S(1)}, f32[16]{0:T(128)S(1)}) all-reduce(f32[16]{0:T(128)S(1)} %get-tuple-element.12, ...), channel_id=1, replica_groups=mesh['groups'=2,'wide'=8,'narrow'=2] {'wide','narrow'}, use_global_device_ids=true, to_apply=%region_34.35 | all-reduce | flops 128 | bytes 1024 | tf_op jit(solution)/shard_map/psum | solution.py:71
  44.2 0.9 fusion.56
  45.2 0.9 fusion.161
  46.1 0.9 fusion.163
  47.1 0.9 fusion.165
  48.0 0.9 fusion.167
  49.0 30.8 %all_gather.30 = bf16[16,9216]{1,0:T(8,128)(2,1)S(1)} all-gather(bf16[16,1152]{1,0:T(8,128)(2,1)S(1)} %get-tuple-element.32), channel_id=1, replica_groups=mesh['groups'=2,'wide'=8,'narrow'=2] {'wide'}, dimensions={1}, use_global_device_ids=true | all-gather | bytes 331776 | tf_op jit(solution)/shard_map/all_gather | solution.py:81
  79.8 3.5 reduce-scatter.23.cloned.1.call-done
  83.3 11.6 %fusion.166 = f32[16,1536]{1,0:T(8,128)} fusion(bf16[16,9216]{1,0:T(8,128)(2,1)S(1)} %all_gather.30, bf16[9216,1536]{1,0:T(8,128)(2,1)} %param.10), kind=kOutput, calls=%fused_computation.285 | convolution fusion | flops 452984832 | bytes 28704768 | tf_op jit(solution)/shard_map/dot_general | solution.py:80
  95.1 31.2 %all_gather.28 = bf16[16,9216]{1,0:T(8,128)(2,1)S(1)} all-gather(bf16[16,1152]{1,0:T(8,128)(2,1)S(1)} %get-tuple-element.31), channel_id=1, replica_groups=mesh['groups'=2,'wide'=8,'narrow'=2] {'wide'}, dimensions={1}, use_global_device_ids=true | all-gather | bytes 331776 | tf_op jit(solution)/shard_map/all_gather | solution.py:81
  126.3 11.7 %fusion.164 = f32[16,1536]{1,0:T(8,128)} fusion(bf16[16,9216]{1,0:T(8,128)(2,1)S(1)} %all_gather.28, bf16[9216,1536]{1,0:T(8,128)(2,1)} %param.10), kind=kOutput, calls=%fused_computation.283 | convolution fusion | flops 452984832 | bytes 28704768 | tf_op jit(solution)/shard_map/dot_general | solution.py:80
  138.0 30.9 %all_gather.26 = bf16[16,9216]{1,0:T(8,128)(2,1)S(1)} all-gather(bf16[16,1152]{1,0:T(8,128)(2,1)S(1)} %get-tuple-element.30), channel_id=1, replica_groups=mesh['groups'=2,'wide'=8,'narrow'=2] {'wide'}, dimensions={1}, use_global_device_ids=true | all-gather | bytes 331776 | tf_op jit(solution)/shard_map/all_gather | solution.py:81
  168.9 11.8 %fusion.162 = f32[16,1536]{1,0:T(8,128)} fusion(bf16[16,9216]{1,0:T(8,128)(2,1)S(1)} %all_gather.26, bf16[9216,1536]{1,0:T(8,128)(2,1)} %param.10), kind=kOutput, calls=%fused_computation.281 | convolution fusion | flops 452984832 | bytes 28704768 | tf_op jit(solution)/shard_map/dot_general | solution.py:80
  180.7 30.9 %all_gather.24 = bf16[16,9216]{1,0:T(8,128)(2,1)S(1)} all-gather(bf16[16,1152]{1,0:T(8,128)(2,1)S(1)} %get-tuple-element.29), channel_id=1, replica_groups=mesh['groups'=2,'wide'=8,'narrow'=2] {'wide'}, dimensions={1}, use_global_device_ids=true | all-gather | bytes 331776 | tf_op jit(solution)/shard_map/all_gather | solution.py:81
  211.7 11.6 %fusion.160 = f32[16,1536]{1,0:T(8,128)} fusion(bf16[16,9216]{1,0:T(8,128)(2,1)S(1)} %all_gather.24, bf16[9216,1536]{1,0:T(8,128)(2,1)} %param.10), kind=kOutput, calls=%fused_computation.279 | convolution fusion | flops 452984832 | bytes 28704768 | tf_op jit(solution)/shard_map/dot_general | solution.py:80
  224.2 0.6 dynamic-slice
  224.8 1.3 convert_bitcast_fusion.9
  226.2 1.4 fusion.116
  227.5 1.3 convert_bitcast_fusion.11
  228.9 1.4 fusion.117
  230.2 1.3 convert_bitcast_fusion.13
  231.5 1.4 fusion.118
  232.9 1.3 multiply_subtract_fusion
  234.2 1.4 fusion.134
  235.6 0.8 convert_bitcast_fusion.4
  236.4 0.5 broadcast.283
  237.0 0.6 reduce.40
  237.5 0.6 reshape.873
  238.2 5.7 %all-to-all-start.3 = ((bf16[8,2,768]{2,1,0:T(2,128)(2,1)}), bf16[8,2,768]{2,1,0:T(2,128)(2,1)S(1)}, u32[]{:S(2)}, u32[]{:S(2)}) async-start(bf16[8,2,768]{2,1,0:T(2,128)(2,1)} %reshape.873), calls=%async_computation.10 | async-start | bytes 49152 | tf_op jit(solution)/shard_map/all_to_all | solution.py:90
  243.9 0.8 convert_bitcast_fusion.5
  244.7 0.8 convert_bitcast_fusion.6
  245.5 0.8 convert_bitcast_fusion.7
  246.3 0.6 reduce.43
  246.9 0.6 reshape.879
  247.5 0.6 reduce.42
  248.1 0.6 reshape.877
  248.7 0.6 reduce.41
  249.3 0.6 reshape.875
  249.9 0.6 all-to-all-done.3
  250.5 5.4 %all-to-all-start.2 = ((bf16[8,2,768]{2,1,0:T(2,128)(2,1)}), bf16[8,2,768]{2,1,0:T(2,128)(2,1)S(1)}, u32[]{:S(2)}, u32[]{:S(2)}) async-start(bf16[8,2,768]{2,1,0:T(2,128)(2,1)} %reshape.879), calls=%async_computation.7 | async-start | bytes 49152 | tf_op jit(solution)/shard_map/all_to_all | solution.py:90
  256.1 6.5 %all-to-all-done.2 = bf16[8,2,768]{2,1,0:T(2,128)(2,1)S(1)} async-done(((bf16[8,2,768]{2,1,0:T(2,128)(2,1)}), bf16[8,2,768]{2,1,0:T(2,128)(2,1)S(1)}, u32[]{:S(2)}, u32[]{:S(2)}) %all-to-all-start.2) | async-done | bytes 24608 | tf_op jit(solution)/shard_map/all_to_all | solution.py:90
  262.5 3.3 all-to-all-start.1
  266.0 6.4 %all-to-all-done.1 = bf16[8,2,768]{2,1,0:T(2,128)(2,1)S(1)} async-done(((bf16[8,2,768]{2,1,0:T(2,128)(2,1)}), bf16[8,2,768]{2,1,0:T(2,128)(2,1)S(1)}, u32[]{:S(2)}, u32[]{:S(2)}) %all-to-all-start.1) | async-done | bytes 24608 | tf_op jit(solution)/shard_map/all_to_all | solution.py:90
  272.4 3.3 all-to-all-start
  276.0 6.3 %all-to-all-done = bf16[8,2,768]{2,1,0:T(2,128)(2,1)S(1)} async-done(((bf16[8,2,768]{2,1,0:T(2,128)(2,1)}), bf16[8,2,768]{2,1,0:T(2,128)(2,1)S(1)}, u32[]{:S(2)}, u32[]{:S(2)}) %all-to-all-start) | async-done | bytes 24608 | tf_op jit(solution)/shard_map/all_to_all | solution.py:90
  282.6 0.5 fusion.154
  283.1 0.5 fusion.156
  283.9 0.5 fusion.158
  284.7 0.5 fusion.152
  285.4 0.4 fusion.26
  286.2 0.4 fusion.4
  287.1 0.4 fusion.7
  288.0 20.1 %all-gather.2 = bf16[16,1,12288]{2,1,0:T(2,128)(2,1)S(1)} all-gather(bf16[1,1,12288]{2,1,0:T(2,128)(2,1)S(1)} %reshape.855), channel_id=1, replica_groups=mesh['groups'=2,'wide'=8,'narrow'=2] {'wide','narrow'}, dimensions={0}, use_global_device_ids=true | all-gather | bytes 417792 | tf_op jit(solution)/shard_map/all_gather | solution.py:110
  308.1 11.2 %convolution_convert_fusion.1 = bf16[16,1152]{1,0:T(8,128)(2,1)S(1)} fusion(bf16[12288,1152]{1,0:T(8,128)(2,1)} %param.12, bf16[16,1,12288]{2,1,0:T(2,128)(2,1)S(1)} %all-gather.2), kind=kOutput, calls=%fused_computation.9 | convolution fusion | flops 453003264 | bytes 28741632 | tf_op jit(solution)/shard_map/dot_general | solution.py:109
  319.4 20.7 %all-gather.3 = bf16[16,1,12288]{2,1,0:T(2,128)(2,1)S(1)} all-gather(bf16[1,1,12288]{2,1,0:T(2,128)(2,1)S(1)} %reshape.857), channel_id=1, replica_groups=mesh['groups'=2,'wide'=8,'narrow'=2] {'wide','narrow'}, dimensions={0}, use_global_device_ids=true | all-gather | bytes 417792 | tf_op jit(solution)/shard_map/all_gather | solution.py:110
  340.0 11.2 %convolution_convert_fusion = bf16[16,1152]{1,0:T(8,128)(2,1)S(1)} fusion(bf16[12288,1152]{1,0:T(8,128)(2,1)} %param.12, bf16[16,1,12288]{2,1,0:T(2,128)(2,1)S(1)} %all-gather.3), kind=kOutput, calls=%fused_computation.8 | convolution fusion | flops 453003264 | bytes 28741632 | tf_op jit(solution)/shard_map/dot_general | solution.py:109
  351.2 19.9 %all-gather.1 = bf16[16,1,12288]{2,1,0:T(2,128)(2,1)S(1)} all-gather(bf16[1,1,12288]{2,1,0:T(2,128)(2,1)S(1)} %reshape.853), channel_id=1, replica_groups=mesh['groups'=2,'wide'=8,'narrow'=2] {'wide','narrow'}, dimensions={0}, use_global_device_ids=true | all-gather | bytes 417792 | tf_op jit(solution)/shard_map/all_gather | solution.py:110
  371.1 11.2 %convolution_convert_fusion.2 = bf16[16,1152]{1,0:T(8,128)(2,1)S(1)} fusion(bf16[12288,1152]{1,0:T(8,128)(2,1)} %param.12, bf16[16,1,12288]{2,1,0:T(2,128)(2,1)S(1)} %all-gather.1), kind=kOutput, calls=%fused_computation.10 | convolution fusion | flops 453003264 | bytes 28741632 | tf_op jit(solution)/shard_map/dot_general | solution.py:109
  382.4 20.8 %all-gather = bf16[16,1,12288]{2,1,0:T(2,128)(2,1)S(1)} all-gather(bf16[1,1,12288]{2,1,0:T(2,128)(2,1)S(1)} %reshape.851), channel_id=1, replica_groups=mesh['groups'=2,'wide'=8,'narrow'=2] {'wide','narrow'}, dimensions={0}, use_global_device_ids=true | all-gather | bytes 417792 | tf_op jit(solution)/shard_map/all_gather | solution.py:110
  403.2 11.1 %convolution_convert_fusion.3 = bf16[16,1152]{1,0:T(8,128)(2,1)S(1)} fusion(bf16[12288,1152]{1,0:T(8,128)(2,1)} %param.12, bf16[16,1,12288]{2,1,0:T(2,128)(2,1)S(1)} %all-gather), kind=kOutput, calls=%fused_computation.11 | convolution fusion | flops 453003264 | bytes 28741632 | tf_op jit(solution)/shard_map/dot_general | solution.py:109
  414.4 0.7 pad_maximum_fusion
  (92 shorter events, 3.6 us)
Async XLA Ops:
  6.5 38.6 %copy-start = (bf16[1152,512]{1,0:T(8,128)(2,1)S(1)}, bf16[1152,512]{1,0:T(8,128)(2,1)}, u32[]{:S(2)}) copy-start(bf16[1152,512]{1,0:T(8,128)(2,1)} %param.11) | copy-start | bytes 3538948
  6.5 73.3 %reduce-scatter.11.cloned.1.call-start = ((), (), s32[]{:S(2)}) async-start(), calls=%async_computation.13 | async-start | bytes 49152 | tf_op jit(solution)/shard_map/reduce_scatter | solution.py:88
  46.1 33.7 %reduce-scatter.15.cloned.1.call-start = ((), (), s32[]{:S(2)}) async-start(), calls=%async_computation.15 | async-start | bytes 49152 | tf_op jit(solution)/shard_map/reduce_scatter | solution.py:88
  47.0 32.8 %reduce-scatter.19.cloned.1.call-start = ((), (), s32[]{:S(2)}) async-start(), calls=%async_computation.17 | async-start | bytes 49152 | tf_op jit(solution)/shard_map/reduce_scatter | solution.py:88
  48.0 35.3 %reduce-scatter.23.cloned.1.call-start = ((), (), s32[]{:S(2)}) async-start(), calls=%async_computation.19 | async-start | bytes 49152 | tf_op jit(solution)/shard_map/reduce_scatter | solution.py:88
  48.9 175.9 %all-reduce.8.cloned.1.call-start = ((), (), s32[]{:S(2)}) async-start(), calls=%async_computation.20 | async-start | bytes 131072
  83.3 152.3 %reduce-scatter.21.cloned.1.call-start = ((), (), s32[]{:S(2)}) async-start(), calls=%async_computation.18 | async-start | bytes 147456 | tf_op jit(solution)/shard_map/reduce_scatter | solution.py:87
  95.0 148.9 %reduce-scatter.17.cloned.1.call-start = ((), (), s32[]{:S(2)}) async-start(), calls=%async_computation.16 | async-start | bytes 147456 | tf_op jit(solution)/shard_map/reduce_scatter | solution.py:87
  138.0 106.8 %reduce-scatter.13.cloned.1.call-start = ((), (), s32[]{:S(2)}) async-start(), calls=%async_computation.14 | async-start | bytes 147456 | tf_op jit(solution)/shard_map/reduce_scatter | solution.py:87
  168.9 55.3 %copy-start.4 = (u32[32]{0:T(128)S(1)}, u32[32]{0:T(128)}, u32[]{:S(2)}) copy-start(u32[32]{0:T(128)} %constant.39) | copy-start | bytes 388
  168.9 113.7 %copy-start.2 = (bf16[1,2048,256]{2,1,0:T(8,128)(2,1)S(1)}, bf16[1,2048,256]{2,1,0:T(8,128)(2,1)}, u32[]{:S(2)}) copy-start(bf16[1,2048,256]{2,1,0:T(8,128)(2,1)} %param.13) | copy-start | bytes 3145732
  180.7 105.2 %copy-start.3 = (bf16[1,2048,256]{2,1,0:T(8,128)(2,1)S(1)}, bf16[1,2048,256]{2,1,0:T(8,128)(2,1)}, u32[]{:S(2)}) copy-start(bf16[1,2048,256]{2,1,0:T(8,128)(2,1)} %param.14) | copy-start | bytes 3145732
  180.7 64.8 %reduce-scatter.9.cloned.1.call-start = ((), (), s32[]{:S(2)}) async-start(), calls=%async_computation.12 | async-start | bytes 147456 | tf_op jit(solution)/shard_map/reduce_scatter | solution.py:87
  238.2 12.4 %all-to-all-start.3 = ((bf16[8,2,768]{2,1,0:T(2,128)(2,1)}), bf16[8,2,768]{2,1,0:T(2,128)(2,1)S(1)}, u32[]{:S(2)}, u32[]{:S(2)}) async-start(bf16[8,2,768]{2,1,0:T(2,128)(2,1)} %reshape.873), calls=%async_computation.10 | async-start | bytes 49152 | tf_op jit(solution)/shard_map/all_to_all | solution.py:90
  250.5 12.0 %all-to-all-start.2 = ((bf16[8,2,768]{2,1,0:T(2,128)(2,1)}), bf16[8,2,768]{2,1,0:T(2,128)(2,1)S(1)}, u32[]{:S(2)}, u32[]{:S(2)}) async-start(bf16[8,2,768]{2,1,0:T(2,128)(2,1)} %reshape.879), calls=%async_computation.7 | async-start | bytes 49152 | tf_op jit(solution)/shard_map/all_to_all | solution.py:90
  262.5 9.9 %all-to-all-start.1 = ((bf16[8,2,768]{2,1,0:T(2,128)(2,1)}), bf16[8,2,768]{2,1,0:T(2,128)(2,1)S(1)}, u32[]{:S(2)}, u32[]{:S(2)}) async-start(bf16[8,2,768]{2,1,0:T(2,128)(2,1)} %reshape.877), calls=%async_computation.4 | async-start | bytes 49152 | tf_op jit(solution)/shard_map/all_to_all | solution.py:90
  272.4 9.9 %all-to-all-start = ((bf16[8,2,768]{2,1,0:T(2,128)(2,1)}), bf16[8,2,768]{2,1,0:T(2,128)(2,1)S(1)}, u32[]{:S(2)}, u32[]{:S(2)}) async-start(bf16[8,2,768]{2,1,0:T(2,128)(2,1)} %reshape.875), calls=%async_computation.1 | async-start | bytes 49152 | tf_op jit(solution)/shard_map/all_to_all | solution.py:90
  371.1 44.0 %copy-start.1 = (bf16[1152,512]{1,0:T(8,128)(2,1)S(1)}, bf16[1152,512]{1,0:T(8,128)(2,1)}, u32[]{:S(2)}) copy-start(bf16[1152,512]{1,0:T(8,128)(2,1)} %param.11) | copy-start | bytes 3538948
Sparse Core Ops, SparseCore 0:
  46.2 4.7 reduce-scatter.10
  53.2 8.5 reduce-scatter.14
  64.0 8.5 reduce-scatter.18
  74.7 8.5 reduce-scatter.22
  86.9 70.5 all-reduce.7
  159.6 7.4 reduce-scatter.20
  169.3 8.6 reduce-scatter.16
  180.8 8.1 reduce-scatter.12
  223.4 8.1 reduce-scatter.8
where the time goes:
time: 423 us; the launch traced here: 422 us
  blocking collectives  240 us (57%)
  matrix products  99.5 us (24%)
  waiting for transfers between devices  23.5 us (6%)
  starting transfers between devices  18.1 us (4%)
  other arithmetic  18 us (4%)
  between operations  14.3 us (3%)
  local copies, waits for them, and re-layouts  7.94 us (2%)
    all_gather x4, blocking collectives, local(): lax.all_gather(normed, 'wide', axis=1, tiled=True)  124 us
    all_gather x4, blocking collectives, local(): lax.all_gather(context, ('wide', 'narrow'), axis=0, tiled=True)  81.5 us
    dot_general x4, matrix products, local(): jnp.dot(lax.all_gather(normed, 'wide', axis=1, tiled=True), w_query, pref...  46.7 us
    dot_general x4, matrix products, local(): jnp.dot(lax.all_gather(context, ('wide', 'narrow'), axis=0, tiled=True),...  44.6 us
    psum x1, blocking collectives, local(): lax.psum((jnp.sum(rows_float, axis=1), jnp.sum(rows_float * rows_float, a...  34.9 us
    all_to_all x4, waiting for transfers between devices, local(): lax.all_to_all(query_half.astype(jnp.bfloat16), 'wide', split_axis=0, con...  19.8 us
    all_to_all x4, starting transfers between devices, local(): lax.all_to_all(query_half.astype(jnp.bfloat16), 'wide', split_axis=0, con...  17.8 us
  transfers between devices with their start and end apart: 13, of which 5 were waited for; matrix products, arithmetic and copies ran while one was open for 17% of the time, Pallas kernels for 0%

commit v1 on v0

v1 whole, which is shorter than its diff:
```python
import jax
import jax.numpy as jnp
from jax import lax
from jax.sharding import PartitionSpec as P

H = 48
DH = 256


epsilon = 1e-06


def rotate(vectors, positions):
    half_size = vectors.shape[-1] // 2
    ladder = jnp.arange(half_size, dtype=jnp.float32)
    frequency = jnp.exp(ladder * (-2.0 / vectors.shape[-1]) * jnp.log(10000.0))
    angles = positions[..., None] * frequency
    cosine = jnp.cos(angles)
    sine = jnp.sin(angles)
    first_half = vectors[..., :half_size]
    second_half = vectors[..., half_size:]
    return jnp.concatenate(
        [first_half * cosine - second_half * sine, second_half * cosine + first_half * sine],
        axis=-1,
    )


def attend(rot_query, cache_keys, cache_values, new_keys, new_values, lengths):
    count, steps, heads, size = rot_query.shape
    score_scale = 1.0 / jnp.sqrt(jnp.float32(DH))
    flat = rot_query.reshape(count, steps * heads, size)
    cache_scores = (
        jnp.einsum("bhd,bsd->bhs", flat, cache_keys, preferred_element_type=jnp.float32)
        * score_scale
    )
    valid = jnp.arange(cache_keys.shape[1])[None, None, :] < lengths[:, None, None]
    masked = jnp.where(valid, cache_scores, -1e30)
    fresh = (
        jnp.einsum("bhd,bjd->bhj", flat, new_keys, preferred_element_type=jnp.float32)
        * score_scale
    )
    row_step = jnp.arange(steps * heads) // heads
    seen = (jnp.arange(steps)[None, :] <= row_step[:, None])[None]
    fresh = jnp.where(seen, fresh, -1e30)
    highest = jnp.maximum(jnp.max(masked, axis=-1), jnp.max(fresh, axis=-1))[..., None]
    cache_weights = jnp.where(valid, jnp.exp(masked - highest), 0.0)
    fresh_weights = jnp.where(seen, jnp.exp(fresh - highest), 0.0)
    total = jnp.sum(cache_weights, axis=-1, keepdims=True) + jnp.sum(
        fresh_weights, axis=-1, keepdims=True
    )
    cache_probs = (cache_weights / total).astype(jnp.bfloat16)
    fresh_probs = (fresh_weights / total).astype(jnp.bfloat16)
    context = jnp.einsum(
        "bhs,bsd->bhd", cache_probs, cache_values, preferred_element_type=jnp.float32
    )
    context = context + jnp.einsum(
        "bhj,bjd->bhd", fresh_probs, new_values, preferred_element_type=jnp.float32
    )
    return context.astype(jnp.bfloat16).reshape(count, steps, heads, size)


def local(tokens, norm_gain, w_query, w_keyval, w_out, cache_keys, cache_values, lengths):
    wide_count = lax.axis_size("wide")
    narrow_count = lax.axis_size("narrow")
    steps, batch, width = tokens.shape
    count = lengths.shape[0]
    rows_all = steps * batch
    width_total = width * wide_count * narrow_count
    rows_float = tokens.reshape(rows_all, width).astype(jnp.float32)
    row_sum, row_squares = lax.psum(
        (jnp.sum(rows_float, axis=1), jnp.sum(rows_float * rows_float, axis=1)),
        ("wide", "narrow"),
    )
    average = (row_sum / width_total)[:, None]
    spread = (row_squares / width_total)[:, None] - average * average
    normed = (
        (rows_float - average) * lax.rsqrt(spread + epsilon) * norm_gain.astype(jnp.float32)
    ).astype(jnp.bfloat16)
    query_part = jnp.dot(
        lax.all_gather(normed, "wide", axis=1, tiled=True),
        w_query,
        preferred_element_type=jnp.float32,
    ).reshape(steps, narrow_count, batch // narrow_count, w_query.shape[1])
    keyval_part = jnp.dot(normed, w_keyval, preferred_element_type=jnp.float32)
    keyval_part = keyval_part.reshape(steps, batch, w_keyval.shape[1])
    query_half = lax.psum_scatter(query_part, "narrow", scatter_dimension=1, tiled=False)
    query_local = lax.all_to_all(
        query_half.astype(jnp.bfloat16), "wide", split_axis=1, concat_axis=2, tiled=True
    )
    keyval_local = lax.psum_scatter(
        keyval_part, ("narrow", "wide"), scatter_dimension=1, tiled=True
    )
    positions = (lengths[:, None] + jnp.arange(steps)).astype(jnp.float32)
    query_local = query_local.astype(jnp.float32).reshape(steps, count, H, DH).transpose(1, 0, 2, 3)
    keyval_local = keyval_local.transpose(1, 0, 2)
    rot_query = rotate(query_local, positions[..., None]).astype(jnp.bfloat16)
    new_keys = rotate(keyval_local[..., :DH], positions).astype(jnp.bfloat16)
    new_values = keyval_local[..., DH:].astype(jnp.bfloat16)
    context = attend(rot_query, cache_keys, cache_values, new_keys, new_values, lengths)
    context = context.reshape(count * steps, H * DH)
    joined = jnp.dot(
        lax.all_gather(context, ("narrow", "wide"), axis=0, tiled=True),
        w_out,
        preferred_element_type=jnp.float32,
    ).astype(jnp.bfloat16)
    return joined.reshape(batch, steps, w_out.shape[1]).transpose(1, 0, 2)


def solution(mesh):
    placed = (
        P(None, "groups", ("narrow", "wide")),
        P(("narrow", "wide")),
        P("narrow", "wide"),
        P(("narrow", "wide"), None),
        P(None, ("narrow", "wide")),
        P(("groups", "narrow", "wide"), None, None),
        P(("groups", "narrow", "wide"), None, None),
        P(("groups", "narrow", "wide")),
    )
    return jax.shard_map(
        local,
        mesh=mesh,
        in_specs=placed,
        out_specs=P(None, "groups", ("narrow", "wide")),
        check_vma=False,
    )
```

time: 423 us -> 231 us (0.55)
  blocking collectives: 240 us -> 39.7 us
  waiting for transfers between devices: 23.5 us -> 130 us
  matrix products: 99.5 us -> 26.3 us
  other arithmetic: 18 us -> 3.41 us
  starting transfers between devices: 18.1 us -> 6.19 us
    all_gather x8 -> x0, blocking collectives: 205 us -> none  [the longest x4 124 us: local(): lax.all_gather(normed, 'wide', axis=1, tiled=True)]
    unnamed x10 -> x4, waiting for transfers between devices: 0.15 us -> 85.5 us
    all_gather x0 -> x2, waiting for transfers between devices: none -> 37.7 us  [the longest x1 37.6 us: local(): lax.all_gather(context, ('narrow', 'wide'), axis=0, tiled=True)]
    dot_general x12 -> x3, matrix products: 47.3 us -> 12.4 us  [the longest x1 11.6 us: local(): jnp.dot(lax.all_gather(context, ('narrow', 'wide'), axis=0, tiled=True),...]
    dot_general x4 -> x1, matrix products: 46.7 us -> 11.9 us  [local(): jnp.dot(lax.all_gather(normed, 'wide', axis=1, tiled=True), w_query, pref...]
    all_to_all x4 -> x1, waiting for transfers between devices: 19.8 us -> 6.97 us  [local(): lax.all_to_all(query_half.astype(jnp.bfloat16), 'wide', split_axis=1, con...]
    all_to_all x4 -> x1, starting transfers between devices: 17.8 us -> 6.08 us  [local(): lax.all_to_all(query_half.astype(jnp.bfloat16), 'wide', split_axis=1, con...]
    all_to_all x8 -> x0, other arithmetic: 5.52 us -> none  [local(): lax.all_to_all(query_half.astype(jnp.bfloat16), 'wide', split_axis=0, con...]
  transfers between devices with their start and end apart: 13 -> 4, of which waited for: 5 -> 3; matrix products, arithmetic and copies ran while one was open for 17% -> 2% of each run, Pallas kernels for 0% -> 0%
where the time goes in v1:
time: 231 us
  waiting for transfers between devices  130 us (56%)
  blocking collectives  39.7 us (17%)
  matrix products  26.3 us (11%)
  between operations  15.7 us (7%)
  local copies, waits for them, and re-layouts  9.49 us (4%)
  starting transfers between devices  6.19 us (3%)
  other arithmetic  3.41 us (1%)
    unnamed x4, waiting for transfers between devices  85.5 us
    all_gather x1, waiting for transfers between devices, local(): lax.all_gather(context, ('narrow', 'wide'), axis=0, tiled=True)  37.6 us
    psum x1, blocking collectives, local(): lax.psum((jnp.sum(rows_float, axis=1), jnp.sum(rows_float * rows_float, a...  34.9 us
    dot_general x1, matrix products, local(): jnp.dot(lax.all_gather(normed, 'wide', axis=1, tiled=True), w_query, pref...  11.9 us
    dot_general x1, matrix products, local(): jnp.dot(lax.all_gather(context, ('narrow', 'wide'), axis=0, tiled=True),...  11.6 us
    all_to_all x1, waiting for transfers between devices, local(): lax.all_to_all(query_half.astype(jnp.bfloat16), 'wide', split_axis=1, con...  6.97 us
    all_to_all x1, starting transfers between devices, local(): lax.all_to_all(query_half.astype(jnp.bfloat16), 'wide', split_axis=1, con...  6.08 us
    unnamed x18, local copies, waits for them, and re-layouts  4.99 us
  transfers between devices with their start and end apart: 4, of which 3 were waited for; matrix products, arithmetic and copies ran while one was open for 2% of the time, Pallas kernels for 0%

profile of v1, /device:TPU:0, one launch (start us, length us, event | category | flops | bytes accessed | tf_op | source)
XLA Modules:
  0.0 230.9 jit_solution(4904483950213005609)
XLA Ops:
  7.4 0.0 copy-start
  7.4 0.0 copy-start.6
  7.4 0.0 copy-start.5
  7.4 0.0 copy-start.2
  7.4 0.0 all-reduce.6.cloned.1.call-start
  7.4 1.2 convert_reduce_fusion
  8.6 0.1 reduce_sum.41
  8.7 0.1 reduce_sum.43
  8.7 34.9 %all-reduce.2 = (f32[64]{0:T(128)S(1)}, f32[64]{0:T(128)S(1)}) all-reduce(f32[64]{0:T(128)S(1)} %reduce_sum.43, f32[64]{0:T(128)S(1)} %reduce_sum.41), channel_id=1, replica_groups=mesh['groups'=2,'wide'=8,'narrow'=2] {'wide','narrow'}, use_global_device_ids=true, to_apply=%region_3.0 | all-reduce | flops 128 | bytes 1024 | tf_op jit(solution)/shard_map/psum | solution.py:70
  43.6 0.1 sub.56
  43.7 0.1 mul.173
  43.8 0.7 convert_element_type.83
  44.5 0.0 copy-done
  44.5 1.3 fusion.2
  45.8 0.7 copy.23
  46.5 0.0 all-reduce.6.cloned.1.call-update
  46.5 0.0 all-gather.4.cloned.1.call-start
  46.6 0.0 copy-done.2
  46.6 0.8 fusion.11
  47.4 0.0 all-gather.4.cloned.1.call-update
  48.0 0.0 copy-done.6
  48.0 0.7 dynamic-slice.2
  48.7 0.0 copy-done.5
  48.7 0.6 dynamic-slice
  49.3 0.1 multiply_cosine_fusion.1
  49.5 85.4 %all-reduce.6.cloned.1.call-done = f32[4,16,512]{2,0,1:T(4,128)} async-done(((f32[4,16,512]{2,0,1:T(4,128)}), f32[4,16,512]{2,0,1:T(4,128)}) %all-reduce.6.cloned.1.call-update) | async-done | bytes 131088
  134.9 1.3 dynamic-slice_bitcast_fusion
  136.2 0.0 all-gather.4.cloned.1.call-done
  136.2 11.9 %fusion.43 = f32[64,1536]{1,0:T(8,128)S(1)} fusion(bf16[64,9216]{1,0:T(8,128)(2,1)} %all-gather.4.cloned.1.call-done, bf16[9216,1536]{1,0:T(8,128)(2,1)} %param.10), kind=kOutput, calls=%fused_computation.76 | convolution fusion | flops 1811939328 | bytes 29884416 | tf_op jit(solution)/shard_map/dot_general | solution.py:79
  148.2 0.0 copy-start.3
  148.2 4.8 %all-reduce.7 = bf16[4,2,8,1536]{3,2,1,0:T(8,128)(2,1)S(1)} all-reduce(f32[4,2,8,1536]{3,2,1,0:T(8,128)S(1)} %bitcast.47), channel_id=2, replica_groups=mesh['groups'=2,'wide'=8,'narrow'=2] {'narrow'}, use_global_device_ids=true, to_apply=%region_4.0.clone | all-reduce | flops 98304 | bytes 589824
  153.0 0.6 fusion.15
  153.7 0.7 copy.21
  154.3 6.1 %all-to-all-start = ((bf16[4,8,1536]{2,0,1:T(4,128)(2,1)}), bf16[4,8,1536]{2,0,1:T(4,128)(2,1)S(1)}, u32[]{:S(2)}, u32[]{:S(2)}) async-start(bf16[4,8,1536]{2,0,1:T(4,128)(2,1)} %copy.21), calls=%async_computation | async-start | bytes 196608 | tf_op jit(solution)/shard_map/all_to_all | solution.py:87
  160.4 0.0 all-gather.6.cloned.1.call-start
  160.5 0.1 fusion.36
  160.6 7.0 %all-to-all-done = bf16[4,8,1536]{2,0,1:T(4,128)(2,1)S(1)} async-done(((bf16[4,8,1536]{2,0,1:T(4,128)(2,1)}), bf16[4,8,1536]{2,0,1:T(4,128)(2,1)S(1)}, u32[]{:S(2)}, u32[]{:S(2)}) %all-to-all-start) | async-done | bytes 98336 | tf_op jit(solution)/shard_map/all_to_all | solution.py:87
  167.7 0.0 copy-done.3
  167.7 0.6 fusion.41
  168.3 0.0 copy-start.4
  168.3 0.1 fusion.42
  168.5 0.4 fusion.1
  168.9 0.2 fusion.21
  169.2 0.3 copy-done.4
  169.5 0.5 fusion.4
  170.0 0.7 reshape.375
  170.7 0.0 all-gather.6.cloned.1.call-update
  170.7 37.6 %all-gather.6.cloned.1.call-done = bf16[16,4,12288]{2,1,0:T(4,128)(2,1)} async-done(((bf16[1,4,12288]{2,1,0:T(4,128)(2,1)}), bf16[16,4,12288]{2,1,0:T(4,128)(2,1)}) %all-gather.6.cloned.1.call-update) | async-done | bytes 1572880 | tf_op jit(solution)/shard_map/all_gather | solution.py:102
  208.4 2.7 %reshape.376 = bf16[64,12288]{1,0:T(8,128)(2,1)S(1)} reshape(bf16[16,4,12288]{2,1,0:T(4,128)(2,1)} %all-gather.6.cloned.1.call-done) | data formatting | bytes 3145728
  211.1 0.0 copy-start.1
  211.1 11.6 %convolution_convert_fusion = bf16[64,1152]{1,0:T(8,128)(2,1)S(1)} fusion(bf16[64,12288]{1,0:T(8,128)(2,1)S(1)} %reshape.376, bf16[12288,1152]{1,0:T(8,128)(2,1)} %param.12), kind=kOutput, calls=%fused_computation.2 | convolution fusion | flops 1812013056 | bytes 30031872 | tf_op jit(solution)/shard_map/dot_general | solution.py:101
  222.8 0.7 copy.29
  223.5 0.0 copy-done.1
  (12 shorter events, 0.2 us)
Async XLA Ops:
  7.4 37.1 %copy-start = (bf16[1152,512]{1,0:T(8,128)(2,1)S(1)}, bf16[1152,512]{1,0:T(8,128)(2,1)}, u32[]{:S(2)}) copy-start(bf16[1152,512]{1,0:T(8,128)(2,1)} %param.11) | copy-start | bytes 3538948
  7.4 40.7 %copy-start.6 = (u32[32]{0:T(128)S(1)}, u32[32]{0:T(128)}, u32[]{:S(2)}) copy-start(u32[32]{0:T(128)} %constant.39) | copy-start | bytes 388
  7.4 41.3 %copy-start.5 = (u32[32]{0:T(128)S(1)}, u32[32]{0:T(128)}, u32[]{:S(2)}) copy-start(u32[32]{0:T(128)} %constant.35) | copy-start | bytes 388
  7.4 39.2 %copy-start.2 = (bf16[4,16,1152]{2,1,0:T(8,128)(2,1)S(1)}, bf16[4,16,1152]{2,1,0:T(8,128)(2,1)}, u32[]{:S(2)}) copy-start(bf16[4,16,1152]{2,1,0:T(8,128)(2,1)} %param.8) | copy-start | bytes 442372
  7.4 127.5 %all-reduce.6.cloned.1.call-start = ((), (), s32[]{:S(2)}) async-start(), calls=%async_computation.3 | async-start | bytes 262144
  46.5 89.7 %all-gather.4.cloned.1.call-start = ((), (), s32[]{:S(2)}) async-start(), calls=%async_computation.1 | async-start | bytes 1327104 | tf_op jit(solution)/shard_map/all_gather | solution.py:80
  148.2 19.5 %copy-start.3 = (bf16[1,2048,256]{2,1,0:T(8,128)(2,1)S(1)}, bf16[1,2048,256]{2,1,0:T(8,128)(2,1)}, u32[]{:S(2)}) copy-start(bf16[1,2048,256]{2,1,0:T(8,128)(2,1)} %param.13) | copy-start | bytes 3145732
  154.3 13.2 %all-to-all-start = ((bf16[4,8,1536]{2,0,1:T(4,128)(2,1)}), bf16[4,8,1536]{2,0,1:T(4,128)(2,1)S(1)}, u32[]{:S(2)}, u32[]{:S(2)}) async-start(bf16[4,8,1536]{2,0,1:T(4,128)(2,1)} %copy.21), calls=%async_computation | async-start | bytes 196608 | tf_op jit(solution)/shard_map/all_to_all | solution.py:87
  160.4 48.0 %all-gather.6.cloned.1.call-start = ((), (), s32[]{:S(2)}) async-start(), calls=%async_computation.2 | async-start | bytes 1671168 | tf_op jit(solution)/shard_map/all_gather | solution.py:102
  168.3 1.2 copy-start.4
  211.1 12.4 %copy-start.1 = (bf16[1152,512]{1,0:T(8,128)(2,1)S(1)}, bf16[1152,512]{1,0:T(8,128)(2,1)}, u32[]{:S(2)}) copy-start(bf16[1152,512]{1,0:T(8,128)(2,1)} %param.11) | copy-start | bytes 3538948
Sparse Core Ops, SparseCore 0:
  46.6 88.1 all-reduce.5
  170.9 37.4 all-gather.5
Sparse Core Ops, SparseCore 1:
  49.2 38.7 all-gather.3

commit v2 on v1

--- a/solution.py
+++ b/solution.py
@@ -1,6 +1,10 @@
+import functools
+
 import jax
 import jax.numpy as jnp
 from jax import lax
+from jax.experimental import pallas as pl
+from jax.experimental.pallas import tpu as pltpu
 from jax.sharding import PartitionSpec as P
 
 H = 48
@@ -59,7 +63,7 @@
     return context.astype(jnp.bfloat16).reshape(count, steps, heads, size)
 
 
-def local(tokens, norm_gain, w_query, w_keyval, w_out, cache_keys, cache_values, lengths):
+def local_plain(tokens, norm_gain, w_query, w_keyval, w_out, cache_keys, cache_values, lengths):
     wide_count = lax.axis_size("wide")
     narrow_count = lax.axis_size("narrow")
     steps, batch, width = tokens.shape
@@ -106,6 +110,325 @@
     return joined.reshape(batch, steps, w_out.shape[1]).transpose(1, 0, 2)
 
 
+MIB = 1 << 20
+IN_VMEM = pl.BlockSpec(memory_space=pltpu.VMEM)
+IN_SMEM = pl.BlockSpec(memory_space=pltpu.SMEM)
+IN_HBM = pl.BlockSpec(memory_space=pltpu.HBM)
+
+
+def call(kernel, name, out_shape, args, in_specs=None, scratch=(), limit=12 * MIB, flops=0):
+    leaves = jax.tree.leaves(out_shape)
+    moved = sum(a.size * a.dtype.itemsize for a in args) + sum(
+        o.size * jnp.dtype(o.dtype).itemsize if hasattr(o, "size") else 0 for o in leaves
+    )
+    return pl.pallas_call(
+        kernel,
+        out_shape=out_shape,
+        in_specs=in_specs or [IN_VMEM] * len(args),
+        out_specs=jax.tree.map(lambda _: IN_VMEM, out_shape),
+        scratch_shapes=list(scratch),
+        compiler_params=pltpu.CompilerParams(vmem_limit_bytes=limit),
+        cost_estimate=pl.CostEstimate(flops=flops, bytes_accessed=moved, transcendentals=0),
+        name=name,
+    )(*args)
+
+
+def load_kernel(pieces, *refs):
+    count = len(pieces)
+    sources, targets, sems = refs[:count], refs[count : 2 * count], refs[2 * count]
+    copies = []
+    for source, target, cuts in zip(sources, targets, pieces):
+        rows = source.shape[0] // cuts
+        for cut in range(cuts):
+            part = pl.ds(cut * rows, rows)
+            copies.append(
+                pltpu.make_async_copy(source.at[part], target.at[part], sems.at[len(copies)])
+            )
+    for copy in copies:
+        copy.start()
+    for copy in copies:
+        copy.wait()
+
+
+def load(name, pieces, *arrays):
+    return call(
+        functools.partial(load_kernel, pieces),
+        name,
+        [pltpu.VMEM(a.shape, a.dtype) for a in arrays],
+        arrays,
+        in_specs=[IN_HBM] * len(arrays),
+        scratch=[pltpu.SemaphoreType.DMA((sum(pieces),))],
+        limit=MIB,
+    )
+
+
+def stats_kernel(rows, *refs):
+    blocks, out = refs[:-1], refs[-1]
+    lanes = out.shape[1]
+    total = jnp.zeros((rows, lanes), jnp.float32)
+    squares = jnp.zeros((rows, lanes), jnp.float32)
+    for block in blocks:
+        for at in range(0, block.shape[1], lanes):
+            values = block[:, at : at + lanes].astype(jnp.float32)[:rows]
+            total = total + values
+            squares = squares + values * values
+    out[:rows] = total
+    out[rows:] = squares
+
+
+def project_kernel(steps, width_total, *refs):
+    place, mine, theirs = refs[:3]
+    *blocks, w_query, w_keyval, keep, send, result = refs[3:]
+    wide_at, narrow_at = place[0], place[1]
+    rows = result.shape[0]
+    width, columns = w_keyval.shape[0], w_query.shape[1]
+    sums = jnp.sum(mine[...] + theirs[...], axis=1, keepdims=True)
+    average = sums[:rows] / width_total
+    spread = sums[rows:] / width_total - average * average
+    scale = lax.rsqrt(spread + epsilon)
+    for k, block in enumerate(blocks):
+        values = block[...].astype(jnp.float32)
+        normed = ((values[:rows] - average) * scale * values[rows : rows + 1]).astype(jnp.bfloat16)
+        owner = jnp.bitwise_xor(wide_at, k)
+        weights = w_query[pl.ds(pl.multiple_of(owner * width, width), width), :]
+        product = jnp.dot(normed, weights, preferred_element_type=jnp.float32)
+        if k == 0:
+            result[:, :columns] = product
+            result[:, columns:] = jnp.dot(
+                normed, w_keyval[...], preferred_element_type=jnp.float32
+            )
+        else:
+            result[:, :columns] += product
+    half = rows // steps // 2
+    for step in range(steps):
+        for out, core in ((keep, narrow_at), (send, 1 - narrow_at)):
+            start = pl.multiple_of(step * 2 * half + core * half, half)
+            out[step * half : (step + 1) * half, :] = result[pl.ds(start, half), :]
+
+
+def combine_kernel(columns, mine, theirs, out, held):
+    wide, steps, _ = out.shape
+    lanes = held.shape[2]
+    extent = mine.shape[1]
+    for at in range(0, extent, lanes):
+        total = mine[:, at : at + lanes] + theirs[:, at : at + lanes]
+        if at < columns:
+            held[at // lanes] = total
+        else:
+            high = total.astype(jnp.bfloat16).astype(jnp.float32)
+            held[at // lanes] = high
+            held[(at + extent - columns) // lanes] = total - high
+    for at in range(held.shape[0]):
+        for to in range(wide):
+            out[to, :, at * lanes : (at + 1) * lanes] = held[
+                at, pl.ds(to, steps, stride=wide), :
+            ].astype(jnp.bfloat16)
+
+
+def attend_kernel(columns, length, cosine, sine, arrived, cache_keys, cache_values, out, queries, fresh_rows):
+    wide, steps, _ = arrived.shape
+    size = cache_keys.shape[1]
+    half = size // 2
+    heads = columns // size
+    cos, sin = cosine[...], sine[...]
+
+    def turn(vectors):
+        first, second = vectors[:, :half], vectors[:, half:]
+        return first * cos - second * sin, second * cos + first * sin
+
+    for source in range(wide):
+        for head in range(heads):
+            at = (source * heads + head) * steps
+            low, high = turn(
+                arrived[source, :, head * size : (head + 1) * size].astype(jnp.float32)
+            )
+            queries[at : at + steps, :half] = low
+            queries[at : at + steps, half:] = high
+    keyval = jnp.zeros((steps, 2 * size), jnp.float32)
+    for source in range(wide):
+        high = arrived[source, :, columns : columns + 2 * size].astype(jnp.float32)
+        low = arrived[source, :, columns + 2 * size :].astype(jnp.float32)
+        keyval = keyval + (high + low)
+    fresh_rows[...] = jnp.zeros_like(fresh_rows)
+    low, high = turn(keyval[:, :size])
+    fresh_rows[0, :steps, :half] = low
+    fresh_rows[0, :steps, half:] = high
+    fresh_rows[1, :steps, :] = keyval[:, size:]
+    query = queries[...].astype(jnp.bfloat16)
+    new_keys = fresh_rows[0].astype(jnp.bfloat16)
+    new_values = fresh_rows[1].astype(jnp.bfloat16)
+    score_scale = 1.0 / size**0.5
+    by_row = (((1,), (1,)), ((), ()))
+    scores = score_scale * lax.dot_general(
+        query, cache_keys[...], by_row, preferred_element_type=jnp.float32
+    )
+    fresh = score_scale * lax.dot_general(
+        query, new_keys, by_row, preferred_element_type=jnp.float32
+    )
+    valid = lax.broadcasted_iota(jnp.int32, scores.shape, 1) < length[0]
+    row_step = lax.rem(lax.broadcasted_iota(jnp.int32, fresh.shape, 0), steps)
+    seen = lax.broadcasted_iota(jnp.int32, fresh.shape, 1) <= row_step
+    scores = jnp.where(valid, scores, -1e30)
+    fresh = jnp.where(seen, fresh, -1e30)
+    highest = jnp.maximum(
+        jnp.max(scores, axis=1, keepdims=True), jnp.max(fresh, axis=1, keepdims=True)
+    )
+    weights = jnp.where(valid, jnp.exp(scores - highest), 0.0)
+    fresh_weights = jnp.where(seen, jnp.exp(fresh - highest), 0.0)
+    share = 1.0 / (
+        jnp.sum(weights, axis=1, keepdims=True) + jnp.sum(fresh_weights, axis=1, keepdims=True)
+    )
+    context = jnp.dot(
+        (weights * share).astype(jnp.bfloat16),
+        cache_values[...],
+        preferred_element_type=jnp.float32,
+    ) + jnp.dot(
+        (fresh_weights * share).astype(jnp.bfloat16),
+        new_values,
+        preferred_element_type=jnp.float32,
+    )
+    queries[...] = context
+    for head in range(wide * heads):
+        out[:, head * size : (head + 1) * size] = queries[
+            head * steps : (head + 1) * steps, :
+        ].astype(jnp.bfloat16)
+
+
+def assemble_kernel(*refs):
+    *blocks, out, held = refs
+    steps = blocks[0].shape[0]
+    for k, block in enumerate(blocks):
+        held[k * steps : (k + 1) * steps, :] = block[...].astype(jnp.float32)
+    out[...] = held[...].astype(jnp.bfloat16)
+
+
+def output_kernel(steps, depth, place, mine, theirs, w_out, out, result, ordered):
+    wide_at, narrow_at = place[0], place[1]
+    count = mine.shape[0] // steps
+    batch = 2 * count
+    for at in range(0, w_out.shape[0], depth):
+        rows = jnp.concatenate([mine[:, at : at + depth], theirs[:, at : at + depth]], axis=0)
+        product = jnp.dot(rows, w_out[at : at + depth, :], preferred_element_type=jnp.float32)
+        if at == 0:
+            result[...] = product
+        else:
+            result[...] += product
+    for core in range(2):
+        for k in range(count):
+            sequence = jnp.bitwise_xor(narrow_at, core) * count + jnp.bitwise_xor(wide_at, k)
+            for step in range(steps):
+                row = core * count * steps + k * steps + step
+                ordered[pl.ds(step * batch + sequence, 1), :] = result[row : row + 1, :]
+    for step in range(steps):
+        out[step] = ordered[step * batch : (step + 1) * batch, :].astype(jnp.bfloat16)
+
+
+def swap(value, axis, bits):
+    size = lax.axis_size(axis)
+    return lax.ppermute(value, axis, [(at, at ^ bits) for at in range(size)])
+
+
+def gather_wide(block, count):
+    near = {0: block}
+    for bits in range(2, count, 2):
+        near[bits] = swap(block, "wide", bits)
+    for bits in range(0, count, 2):
+        near[bits + 1] = swap(near[bits], "wide", 1)
+    return [near[k] for k in range(count)]
+
+
+def local_fast(tokens, norm_gain, w_query, w_keyval, w_out, cache_keys, cache_values, lengths):
+    wide_count = lax.axis_size("wide")
+    narrow_count = lax.axis_size("narrow")
+    steps, batch, width = tokens.shape
+    rows = steps * batch
+    columns, tail = w_query.shape[1], w_keyval.shape[1]
+    size = cache_keys.shape[2]
+    f32, bf16 = jnp.float32, jnp.bfloat16
+    place = jnp.stack([lax.axis_index("wide"), lax.axis_index("narrow")]).astype(jnp.int32)
+
+    payload = jnp.concatenate(
+        [tokens.reshape(rows, width), norm_gain[None], jnp.zeros((7, width), bf16)]
+    )
+    blocks = gather_wide(payload, wide_count)
+    query_weights, keyval_weights, keys, values = load(
+        "load_query_weights",
+        (8, 1, 1, 1),
+        w_query,
+        w_keyval,
+        cache_keys.reshape(cache_keys.shape[1:]),
+        cache_values.reshape(cache_values.shape[1:]),
+    )
+    sums = call(
+        functools.partial(stats_kernel, rows),
+        "row_sums",
+        jax.ShapeDtypeStruct((2 * rows, 128), f32),
+        blocks,
+    )
+    keep, send = call(
+        functools.partial(project_kernel, steps, width * wide_count * narrow_count),
+        "norm_and_project",
+        [jax.ShapeDtypeStruct((rows // 2, columns + tail), f32)] * 2,
+        [place, sums, swap(sums, "narrow", 1), *blocks, query_weights, keyval_weights],
+        in_specs=[IN_SMEM] + [IN_VMEM] * (wide_count + 4),
+        scratch=[pltpu.VMEM((rows, columns + tail), f32)],
+        flops=2 * rows * width * wide_count * columns,
+    )
+    outgoing = call(
+        functools.partial(combine_kernel, columns),
+        "sum_of_cores",
+        jax.ShapeDtypeStruct((wide_count, steps, columns + 2 * tail), bf16),
+        [keep, swap(send, "narrow", 1)],
+        scratch=[pltpu.VMEM(((columns + 2 * tail) // 128, rows // 2, 128), f32)],
+    )
+    arrived = lax.all_to_all(outgoing, "wide", 0, 0, tiled=True)
+    ladder = jnp.arange(size // 2, dtype=f32)
+    frequency = jnp.exp(ladder * (-2.0 / size) * jnp.log(10000.0))
+    angles = (lengths + jnp.arange(steps)).astype(f32)[:, None] * frequency
+    context = call(
+        functools.partial(attend_kernel, columns),
+        "attention",
+        jax.ShapeDtypeStruct((steps, H * size), bf16),
+        [lengths, jnp.cos(angles), jnp.sin(angles), arrived, keys, values],
+        in_specs=[IN_SMEM] + [IN_VMEM] * 5,
+        scratch=[pltpu.VMEM((steps * H, size), f32), pltpu.VMEM((2, 128, size), f32)],
+        limit=16 * MIB,
+        flops=4 * steps * H * size * keys.shape[0],
+    )
+    w_out, context = lax.optimization_barrier((w_out, context))
+    contexts = gather_wide(context, wide_count)
+    (out_weights,) = load("load_out_weights", (8,), w_out)
+    mine = call(
+        assemble_kernel,
+        "join_contexts",
+        jax.ShapeDtypeStruct((wide_count * steps, H * size), bf16),
+        contexts,
+        scratch=[pltpu.VMEM((wide_count * steps, H * size), f32)],
+    )
+    return call(
+        functools.partial(output_kernel, steps, w_out.shape[0] // 8),
+        "project_out",
+        jax.ShapeDtypeStruct((steps, batch, w_out.shape[1]), bf16),
+        [place, mine, swap(mine, "narrow", 1), out_weights],
+        in_specs=[IN_SMEM] + [IN_VMEM] * 3,
+        scratch=[pltpu.VMEM((rows, w_out.shape[1]), f32)] * 2,
+        flops=2 * rows * w_out.size,
+    )
+
+
+def local(tokens, norm_gain, w_query, w_keyval, w_out, cache_keys, cache_values, lengths):
+    fits = (
+        lengths.shape[0] == 1
+        and lax.axis_size("narrow") == 2
+        and lax.axis_size("wide") == 8
+        and tokens.shape[1] == 16
+        and tokens.shape[2] % 128 == 0
+    )
+    return (local_fast if fits else local_plain)(
+        tokens, norm_gain, w_query, w_keyval, w_out, cache_keys, cache_values, lengths
+    )
+
+
 def solution(mesh):
     placed = (
         P(None, "groups", ("narrow", "wide")),

time: 231 us -> 109 us (0.47)
  waiting for transfers between devices: 130 us -> 25.6 us
  blocking collectives: 39.7 us -> 0 us
  Pallas kernels: 0 us -> 33.8 us
  matrix products: 26.3 us -> 0 us
  starting transfers between devices: 6.19 us -> 24.5 us
  between operations: 15.7 us -> 0.77 us
  local copies, waits for them, and re-layouts: 9.49 us -> 22.9 us
    unnamed x4 -> x0, waiting for transfers between devices: 85.5 us -> none
    all_gather x2 -> x0, waiting for transfers between devices: 37.7 us -> none  [the longest x1 37.6 us: local(): lax.all_gather(context, ('narrow', 'wide'), axis=0, tiled=True)]
    psum x1 -> x0, blocking collectives: 34.9 us -> none  [local(): lax.psum((jnp.sum(rows_float, axis=1), jnp.sum(rows_float * rows_float, a...]
    pallas_call x0 -> x8, Pallas kernels: none -> 33.8 us  [call(): pl.pallas_call(kernel, out_shape=out_shape, in_specs=in_specs or [IN_VMEM...]
    dot_general x7 -> x0, matrix products: 26.3 us -> none  [the longest x1 11.9 us: local(): jnp.dot(lax.all_gather(normed, 'wide', axis=1, tiled=True), w_query, pref...]
    ppermute x0 -> x17, starting transfers between devices: none -> 20 us  [swap(): return lax.ppermute(value, axis, [(at, at ^ bits) for at in range(size)])]
    ppermute x0 -> x17, waiting for transfers between devices: none -> 17.9 us  [swap(): return lax.ppermute(value, axis, [(at, at ^ bits) for at in range(size)])]
    unnamed x18 -> x10, local copies, waits for them, and re-layouts: 4.99 us -> 22.1 us
  transfers between devices with their start and end apart: 4 -> 18, of which waited for: 3 -> 8; matrix products, arithmetic and copies ran while one was open for 2% -> 0% of each run, Pallas kernels for 0% -> 17%
where the time goes in v2:
time: 109 us
  Pallas kernels  33.8 us (31%)
  waiting for transfers between devices  25.6 us (23%)
  starting transfers between devices  24.5 us (22%)
  local copies, waits for them, and re-layouts  22.9 us (21%)
  other arithmetic  1.21 us (1%)
    pallas_call x8, Pallas kernels, call(): pl.pallas_call(kernel, out_shape=out_shape, in_specs=in_specs or [IN_VMEM...  33.8 us
    unnamed x10, local copies, waits for them, and re-layouts  22.1 us
    ppermute x17, starting transfers between devices, swap(): return lax.ppermute(value, axis, [(at, at ^ bits) for at in range(size)])  20 us
    ppermute x17, waiting for transfers between devices, swap(): return lax.ppermute(value, axis, [(at, at ^ bits) for at in range(size)])  17.9 us
    all_to_all x1, waiting for transfers between devices, local_fast(): arrived = lax.all_to_all(outgoing, 'wide', 0, 0, tiled=True)  7.68 us
    all_to_all x1, starting transfers between devices, local_fast(): arrived = lax.all_to_all(outgoing, 'wide', 0, 0, tiled=True)  4.52 us
  transfers between devices with their start and end apart: 18, of which 8 were waited for; matrix products, arithmetic and copies ran while one was open for 0% of the time, Pallas kernels for 17%

profile of v2, /device:TPU:0, one launch (start us, length us, event | category | flops | bytes accessed | tf_op | source)
XLA Modules:
  0.0 108.7 jit_solution(14143848643070448918)
XLA Ops:
  0.0 0.7 broadcast_in_dim.8
  0.7 0.1 pad.2.clone
  0.8 1.0 maximum_maximum_fusion.refs_0_.refs_3_
  1.8 3.1 %collective-permute-start.1 = (bf16[72,1152]{1,0:T(8,128)(2,1)S(1)}, bf16[72,1152]{1,0:T(8,128)(2,1)S(1)}, u32[]{:S(2)}, u32[]{:S(2)}) collective-permute-start(bf16[72,1152]{1,0:T(8,128)(2,1)S(1)} %maximum_maximum_fusion.refs_0_.refs_3_), channel_id=1, source_target_pairs={{0,4},{2,6},{4,0},{6,2},{8,12},{10,14},{12,8},{14,10},{1,5},{3,7},... | collective-permute-start | bytes 497672 | tf_op jit(solution)/shard_map/ppermute | solution.py:328
  4.9 2.6 %collective-permute-start.3 = (bf16[72,1152]{1,0:T(8,128)(2,1)S(1)}, bf16[72,1152]{1,0:T(8,128)(2,1)S(1)}, u32[]{:S(2)}, u32[]{:S(2)}) collective-permute-start(bf16[72,1152]{1,0:T(8,128)(2,1)S(1)} %maximum_maximum_fusion.refs_0_.refs_3_), channel_id=1, source_target_pairs={{0,8},{2,10},{4,12},{6,14},{8,0},{10,2},{12,4},{14,6},{1,9},{3,11}... | collective-permute-start | bytes 497672 | tf_op jit(solution)/shard_map/ppermute | solution.py:328
  7.5 0.0 collective-permute-start.5
  7.5 1.7 %collective-permute-start = (bf16[72,1152]{1,0:T(8,128)(2,1)S(1)}, bf16[72,1152]{1,0:T(8,128)(2,1)S(1)}, u32[]{:S(2)}, u32[]{:S(2)}) collective-permute-start(bf16[72,1152]{1,0:T(8,128)(2,1)S(1)} %maximum_maximum_fusion.refs_0_.refs_3_), channel_id=1, source_target_pairs={{0,2},{2,0},{4,6},{6,4},{8,10},{10,8},{12,14},{14,12},{1,3},{3,1},... | collective-permute-start | bytes 497672 | tf_op jit(solution)/shard_map/ppermute | solution.py:328
  9.2 2.5 %collective-permute-done.1.refs_2_.refs_5_ = bf16[72,1152]{1,0:T(8,128)(2,1)S(1)} collective-permute-done((bf16[72,1152]{1,0:T(8,128)(2,1)S(1)}, bf16[72,1152]{1,0:T(8,128)(2,1)S(1)}, u32[]{:S(2)}, u32[]{:S(2)}) %collective-permute-start.1) | collective-permute-done | bytes 165920 | tf_op jit(solution)/shard_map/ppermute | solution.py:328
  11.7 1.7 %collective-permute-start.2 = (bf16[72,1152]{1,0:T(8,128)(2,1)S(1)}, bf16[72,1152]{1,0:T(8,128)(2,1)S(1)}, u32[]{:S(2)}, u32[]{:S(2)}) collective-permute-start(bf16[72,1152]{1,0:T(8,128)(2,1)S(1)} %collective-permute-done.1.refs_2_.refs_5_), channel_id=1, source_target_pairs={{0,2},{2,0},{4,6},{6,4},{8,10},{10,8},{12,14},{14,12},{1,3},{3,1},... | collective-permute-start | bytes 497672 | tf_op jit(solution)/shard_map/ppermute | solution.py:328
  13.4 6.7 %collective-permute-done.3.refs_4_.refs_7_ = bf16[72,1152]{1,0:T(8,128)(2,1)S(1)} collective-permute-done((bf16[72,1152]{1,0:T(8,128)(2,1)S(1)}, bf16[72,1152]{1,0:T(8,128)(2,1)S(1)}, u32[]{:S(2)}, u32[]{:S(2)}) %collective-permute-start.3) | collective-permute-done | bytes 165920 | tf_op jit(solution)/shard_map/ppermute | solution.py:328
  20.1 1.5 %collective-permute-start.4 = (bf16[72,1152]{1,0:T(8,128)(2,1)S(1)}, bf16[72,1152]{1,0:T(8,128)(2,1)S(1)}, u32[]{:S(2)}, u32[]{:S(2)}) collective-permute-start(bf16[72,1152]{1,0:T(8,128)(2,1)S(1)} %collective-permute-done.3.refs_4_.refs_7_), channel_id=1, source_target_pairs={{0,2},{2,0},{4,6},{6,4},{8,10},{10,8},{12,14},{14,12},{1,3},{3,1},... | collective-permute-start | bytes 497672 | tf_op jit(solution)/shard_map/ppermute | solution.py:328
  21.5 0.0 collective-permute-done.5.refs_6_.refs_9_
  21.5 0.5 collective-permute-start.6
  22.1 0.0 copy-start.2
  22.1 1.3 %copy-done.2 = bf16[1152,512]{1,0:T(8,128)(2,1)S(1)} copy-done((bf16[1152,512]{1,0:T(8,128)(2,1)S(1)}, bf16[1152,512]{1,0:T(8,128)(2,1)}, u32[]{:S(2)}) %copy-start.2) | copy-done | bytes 1179672
  23.4 0.0 copy-start.3
  23.4 1.2 %copy-done.3 = bf16[1,2048,256]{2,1,0:T(8,128)(2,1)S(1)} copy-done((bf16[1,2048,256]{2,1,0:T(8,128)(2,1)S(1)}, bf16[1,2048,256]{2,1,0:T(8,128)(2,1)}, u32[]{:S(2)}) %copy-start.3) | copy-done | bytes 1048600
  24.6 0.0 copy-start.4
  24.6 1.2 %copy-done.4 = bf16[1,2048,256]{2,1,0:T(8,128)(2,1)S(1)} copy-done((bf16[1,2048,256]{2,1,0:T(8,128)(2,1)S(1)}, bf16[1,2048,256]{2,1,0:T(8,128)(2,1)}, u32[]{:S(2)}) %copy-start.4) | copy-done | bytes 1048600
  25.8 9.2 %load_query_weights.1 = (bf16[9216,1536]{1,0:T(8,128)(2,1)S(1)}, bf16[1152,512]{1,0:T(8,128)(2,1)S(1)}, bf16[2048,256]{1,0:T(8,128)(2,1)S(1)}, bf16[2048,256]{1,0:T(8,128)(2,1)S(1)}) custom-call(bf16[9216,1536]{1,0:T(8,128)(2,1)} %refs_0_.1, bf16[1152,512]{1,0:T(8,128)(2,1)S(1)} %copy-done.2, bf16[2048,256]{1,0:T(8,128)(2,1)S(1)} %bitcast.7, ...), custom_call_target="tpu_custom_call" | custom-call | bytes 31588352 | tf_op jit(solution)/shard_map/load_query_weights/pallas_call | solution.py:124
  35.0 0.0 copy-start
  35.0 9.3 %copy-done = bf16[9216,1536]{1,0:T(8,128)(2,1)} copy-done((bf16[9216,1536]{1,0:T(8,128)(2,1)}, bf16[9216,1536]{1,0:T(8,128)(2,1)S(1)}, u32[]{:S(2)}) %copy-start) | copy-done | bytes 28311576
  44.4 0.0 collective-permute-done.refs_1_.refs_4_
  44.4 0.0 collective-permute-done.2.refs_3_.refs_6_
  44.4 0.0 collective-permute-done.4.refs_5_.refs_8_
  44.4 0.0 collective-permute-done.6.refs_7_.refs_10_
  44.4 0.4 row_sums.1.refs_1_
  44.8 0.1 collective-permute-start.7
  44.8 0.1 pad_add_fusion.refs_0_.place
  44.9 1.2 %collective-permute-done.7.refs_2_ = f32[128,128]{1,0:T(8,128)S(1)} collective-permute-done((f32[128,128]{1,0:T(8,128)S(1)}, f32[128,128]{1,0:T(8,128)S(1)}, u32[]{:S(2)}, u32[]{:S(2)}) %collective-permute-start.7) | collective-permute-done | bytes 65568 | tf_op jit(solution)/shard_map/ppermute | solution.py:328
  46.1 0.0 copy-start.1
  46.1 9.1 %copy-done.1 = bf16[9216,1536]{1,0:T(8,128)(2,1)S(1)} copy-done((bf16[9216,1536]{1,0:T(8,128)(2,1)S(1)}, bf16[9216,1536]{1,0:T(8,128)(2,1)}, u32[]{:S(2)}) %copy-start.1) | copy-done | bytes 28311576
  55.1 5.9 %norm_and_project.1 = (f32[32,2048]{1,0:T(8,128)S(1)}, f32[32,2048]{1,0:T(8,128)S(1)}) custom-call(s32[2]{0:T(128)S(1)} %pad_add_fusion.refs_0_.place, f32[128,128]{1,0:T(8,128)S(1)} %row_sums.1.refs_1_, f32[128,128]{1,0:T(8,128)S(1)} %collective-permute-done.7.refs_2_, bf16[72,1152]{1,0:T(8,128)(2,1)S(1)} %maximum_maximum_fusion.refs_0_.refs_3_, ...), custom_call_target="tpu_custom_call" | custom-call | flops 1811939328 | bytes 31473672 | tf_op jit(solution)/shard_map/norm_and_project/pallas_call | solution.py:124
  61.1 0.2 collective-permute-start.8
  62.0 0.7 collective-permute-done.8.theirs
  62.7 0.8 sum_of_cores.1
  63.5 4.5 %all-to-all-start = ((bf16[8,4,2560]{2,1,0:T(4,128)(2,1)}), bf16[8,4,2560]{2,1,0:T(4,128)(2,1)S(1)}, u32[]{:S(2)}, u32[]{:S(2)}) async-start(bf16[8,4,2560]{2,1,0:T(4,128)(2,1)} %sum_of_cores.1), calls=%async_computation | async-start | bytes 327680 | tf_op jit(solution)/shard_map/all_to_all | solution.py:384
  68.0 0.1 multiply_sine_fusion
  68.1 7.7 %all-to-all-done.arrived = bf16[8,4,2560]{2,1,0:T(4,128)(2,1)S(1)} async-done(((bf16[8,4,2560]{2,1,0:T(4,128)(2,1)}), bf16[8,4,2560]{2,1,0:T(4,128)(2,1)S(1)}, u32[]{:S(2)}, u32[]{:S(2)}) %all-to-all-start) | async-done | bytes 163872 | tf_op jit(solution)/shard_map/all_to_all | solution.py:384
  75.8 1.7 %attention.1.refs_0_ = bf16[4,12288]{1,0:T(4,128)(2,1)S(1)} custom-call(s32[1]{0:T(128)} %copy.9.length, f32[4,128]{1,0:T(4,128)S(1)} %get-tuple-element.22.cosine, f32[4,128]{1,0:T(4,128)S(1)} %get-tuple-element.21.sine, bf16[8,4,2560]{2,1,0:T(4,128)(2,1)S(1)} %all-to-all-done.arrived, bf16[2048,256]{1,0:T(8,128)(2,1)S(1)} %get-tuple-element.17.cache_keys, ...), custom_call_target="tpu_custom_call" | custom-call | flops 402653184 | bytes 2363396 | tf_op jit(solution)/shard_map/attention/pallas_call | solution.py:124
  77.5 0.1 collective-permute-start.10
  77.6 1.1 %collective-permute-start.12 = (bf16[4,12288]{1,0:T(4,128)(2,1)S(1)}, bf16[4,12288]{1,0:T(4,128)(2,1)S(1)}, u32[]{:S(2)}, u32[]{:S(2)}) collective-permute-start(bf16[4,12288]{1,0:T(4,128)(2,1)S(1)} %attention.1.refs_0_), channel_id=1, source_target_pairs={{0,8},{2,10},{4,12},{6,14},{8,0},{10,2},{12,4},{14,6},{1,9},{3,11}... | collective-permute-start | bytes 294920 | tf_op jit(solution)/shard_map/ppermute | solution.py:328
  78.7 3.3 %collective-permute-start.14 = (bf16[4,12288]{1,0:T(4,128)(2,1)S(1)}, bf16[4,12288]{1,0:T(4,128)(2,1)S(1)}, u32[]{:S(2)}, u32[]{:S(2)}) collective-permute-start(bf16[4,12288]{1,0:T(4,128)(2,1)S(1)} %attention.1.refs_0_), channel_id=1, source_target_pairs={{0,12},{2,14},{4,8},{6,10},{8,4},{10,6},{12,0},{14,2},{1,13},{3,15... | collective-permute-start | bytes 294920 | tf_op jit(solution)/shard_map/ppermute | solution.py:328
  82.0 0.3 collective-permute-start.9
  82.3 0.0 collective-permute-done.10.refs_2_
  82.3 1.7 %collective-permute-start.11 = (bf16[4,12288]{1,0:T(4,128)(2,1)S(1)}, bf16[4,12288]{1,0:T(4,128)(2,1)S(1)}, u32[]{:S(2)}, u32[]{:S(2)}) collective-permute-start(bf16[4,12288]{1,0:T(4,128)(2,1)S(1)} %collective-permute-done.10.refs_2_), channel_id=1, source_target_pairs={{0,2},{2,0},{4,6},{6,4},{8,10},{10,8},{12,14},{14,12},{1,3},{3,1},... | collective-permute-start | bytes 294920 | tf_op jit(solution)/shard_map/ppermute | solution.py:328
  84.0 3.0 %collective-permute-done.12.refs_4_ = bf16[4,12288]{1,0:T(4,128)(2,1)S(1)} collective-permute-done((bf16[4,12288]{1,0:T(4,128)(2,1)S(1)}, bf16[4,12288]{1,0:T(4,128)(2,1)S(1)}, u32[]{:S(2)}, u32[]{:S(2)}) %collective-permute-start.12) | collective-permute-done | bytes 98336 | tf_op jit(solution)/shard_map/ppermute | solution.py:328
  87.1 1.2 %collective-permute-start.13 = (bf16[4,12288]{1,0:T(4,128)(2,1)S(1)}, bf16[4,12288]{1,0:T(4,128)(2,1)S(1)}, u32[]{:S(2)}, u32[]{:S(2)}) collective-permute-start(bf16[4,12288]{1,0:T(4,128)(2,1)S(1)} %collective-permute-done.12.refs_4_), channel_id=1, source_target_pairs={{0,2},{2,0},{4,6},{6,4},{8,10},{10,8},{12,14},{14,12},{1,3},{3,1},... | collective-permute-start | bytes 294920 | tf_op jit(solution)/shard_map/ppermute | solution.py:328
  88.2 0.0 collective-permute-done.14.refs_6_
  88.3 0.8 collective-permute-start.15
  89.1 0.0 collective-permute-done.9.refs_1_
  89.1 0.0 collective-permute-done.11.refs_3_
  89.1 2.6 %collective-permute-done.13.refs_5_ = bf16[4,12288]{1,0:T(4,128)(2,1)S(1)} collective-permute-done((bf16[4,12288]{1,0:T(4,128)(2,1)S(1)}, bf16[4,12288]{1,0:T(4,128)(2,1)S(1)}, u32[]{:S(2)}, u32[]{:S(2)}) %collective-permute-start.13) | collective-permute-done | bytes 98336 | tf_op jit(solution)/shard_map/ppermute | solution.py:328
  91.7 1.2 %collective-permute-done.15.refs_7_ = bf16[4,12288]{1,0:T(4,128)(2,1)S(1)} collective-permute-done((bf16[4,12288]{1,0:T(4,128)(2,1)S(1)}, bf16[4,12288]{1,0:T(4,128)(2,1)S(1)}, u32[]{:S(2)}, u32[]{:S(2)}) %collective-permute-start.15) | collective-permute-done | bytes 98336 | tf_op jit(solution)/shard_map/ppermute | solution.py:328
  92.9 0.3 join_contexts.1.mine
  93.1 0.1 collective-permute-start.16
  93.2 9.2 %load_out_weights.1.w_out = bf16[12288,1152]{1,0:T(8,128)(2,1)S(1)} custom-call(bf16[12288,1152]{1,0:T(8,128)(2,1)} %refs_0_.2), custom_call_target="tpu_custom_call" | custom-call | bytes 28311552 | tf_op jit(solution)/shard_map/load_out_weights/pallas_call | solution.py:124
  102.4 0.0 collective-permute-done.16.theirs
  102.4 6.3 %project_out.1 = bf16[4,16,1152]{2,1,0:T(8,128)(2,1)} custom-call(s32[2]{0:T(128)S(1)} %pad_add_fusion.refs_0_.place, bf16[32,12288]{1,0:T(8,128)(2,1)S(1)} %join_contexts.1.mine, bf16[32,12288]{1,0:T(8,128)(2,1)S(1)} %collective-permute-done.16.theirs, bf16[12288,1152]{1,0:T(8,128)(2,1)S(1)} %load_out_weights.1.w_out), custom_call_target="tpu_custom_call" | custom-call | flops 1811939328 | bytes 30031880 | tf_op jit(solution)/shard_map/project_out/pallas_call | solution.py:124
  (3 shorter events, 0.0 us)
Async XLA Ops:
  1.8 9.9 %collective-permute-start.1 = (bf16[72,1152]{1,0:T(8,128)(2,1)S(1)}, bf16[72,1152]{1,0:T(8,128)(2,1)S(1)}, u32[]{:S(2)}, u32[]{:S(2)}) collective-permute-start(bf16[72,1152]{1,0:T(8,128)(2,1)S(1)} %maximum_maximum_fusion.refs_0_.refs_3_), channel_id=1, source_target_pairs={{0,4},{2,6},{4,0},{6,2},{8,12},{10,14},{12,8},{14,10},{1,5},{3,7},... | collective-permute-start | bytes 497672 | tf_op jit(solution)/shard_map/ppermute | solution.py:328
  4.9 15.2 %collective-permute-start.3 = (bf16[72,1152]{1,0:T(8,128)(2,1)S(1)}, bf16[72,1152]{1,0:T(8,128)(2,1)S(1)}, u32[]{:S(2)}, u32[]{:S(2)}) collective-permute-start(bf16[72,1152]{1,0:T(8,128)(2,1)S(1)} %maximum_maximum_fusion.refs_0_.refs_3_), channel_id=1, source_target_pairs={{0,8},{2,10},{4,12},{6,14},{8,0},{10,2},{12,4},{14,6},{1,9},{3,11}... | collective-permute-start | bytes 497672 | tf_op jit(solution)/shard_map/ppermute | solution.py:328
  7.5 14.1 %collective-permute-start.5 = (bf16[72,1152]{1,0:T(8,128)(2,1)S(1)}, bf16[72,1152]{1,0:T(8,128)(2,1)S(1)}, u32[]{:S(2)}, u32[]{:S(2)}) collective-permute-start(bf16[72,1152]{1,0:T(8,128)(2,1)S(1)} %maximum_maximum_fusion.refs_0_.refs_3_), channel_id=1, source_target_pairs={{0,12},{2,14},{4,8},{6,10},{8,4},{10,6},{12,0},{14,2},{1,13},{3,15... | collective-permute-start | bytes 497672 | tf_op jit(solution)/shard_map/ppermute | solution.py:328
  7.5 36.9 %collective-permute-start = (bf16[72,1152]{1,0:T(8,128)(2,1)S(1)}, bf16[72,1152]{1,0:T(8,128)(2,1)S(1)}, u32[]{:S(2)}, u32[]{:S(2)}) collective-permute-start(bf16[72,1152]{1,0:T(8,128)(2,1)S(1)} %maximum_maximum_fusion.refs_0_.refs_3_), channel_id=1, source_target_pairs={{0,2},{2,0},{4,6},{6,4},{8,10},{10,8},{12,14},{14,12},{1,3},{3,1},... | collective-permute-start | bytes 497672 | tf_op jit(solution)/shard_map/ppermute | solution.py:328
  11.7 32.7 %collective-permute-start.2 = (bf16[72,1152]{1,0:T(8,128)(2,1)S(1)}, bf16[72,1152]{1,0:T(8,128)(2,1)S(1)}, u32[]{:S(2)}, u32[]{:S(2)}) collective-permute-start(bf16[72,1152]{1,0:T(8,128)(2,1)S(1)} %collective-permute-done.1.refs_2_.refs_5_), channel_id=1, source_target_pairs={{0,2},{2,0},{4,6},{6,4},{8,10},{10,8},{12,14},{14,12},{1,3},{3,1},... | collective-permute-start | bytes 497672 | tf_op jit(solution)/shard_map/ppermute | solution.py:328
  20.1 24.3 %collective-permute-start.4 = (bf16[72,1152]{1,0:T(8,128)(2,1)S(1)}, bf16[72,1152]{1,0:T(8,128)(2,1)S(1)}, u32[]{:S(2)}, u32[]{:S(2)}) collective-permute-start(bf16[72,1152]{1,0:T(8,128)(2,1)S(1)} %collective-permute-done.3.refs_4_.refs_7_), channel_id=1, source_target_pairs={{0,2},{2,0},{4,6},{6,4},{8,10},{10,8},{12,14},{14,12},{1,3},{3,1},... | collective-permute-start | bytes 497672 | tf_op jit(solution)/shard_map/ppermute | solution.py:328
  21.5 22.8 %collective-permute-start.6 = (bf16[72,1152]{1,0:T(8,128)(2,1)S(1)}, bf16[72,1152]{1,0:T(8,128)(2,1)S(1)}, u32[]{:S(2)}, u32[]{:S(2)}) collective-permute-start(bf16[72,1152]{1,0:T(8,128)(2,1)S(1)} %collective-permute-done.5.refs_6_.refs_9_), channel_id=1, source_target_pairs={{0,2},{2,0},{4,6},{6,4},{8,10},{10,8},{12,14},{14,12},{1,3},{3,1},... | collective-permute-start | bytes 497672 | tf_op jit(solution)/shard_map/ppermute | solution.py:328
  22.1 1.3 %copy-start.2 = (bf16[1152,512]{1,0:T(8,128)(2,1)S(1)}, bf16[1152,512]{1,0:T(8,128)(2,1)}, u32[]{:S(2)}) copy-start(bf16[1152,512]{1,0:T(8,128)(2,1)} %refs_1_.1) | copy-start | bytes 3538948
  23.4 1.2 %copy-start.3 = (bf16[1,2048,256]{2,1,0:T(8,128)(2,1)S(1)}, bf16[1,2048,256]{2,1,0:T(8,128)(2,1)}, u32[]{:S(2)}) copy-start(bf16[1,2048,256]{2,1,0:T(8,128)(2,1)} %param.13) | copy-start | bytes 3145732
  24.6 1.2 %copy-start.4 = (bf16[1,2048,256]{2,1,0:T(8,128)(2,1)S(1)}, bf16[1,2048,256]{2,1,0:T(8,128)(2,1)}, u32[]{:S(2)}) copy-start(bf16[1,2048,256]{2,1,0:T(8,128)(2,1)} %param.14) | copy-start | bytes 3145732
  35.0 9.3 %copy-start = (bf16[9216,1536]{1,0:T(8,128)(2,1)}, bf16[9216,1536]{1,0:T(8,128)(2,1)S(1)}, u32[]{:S(2)}) copy-start(bf16[9216,1536]{1,0:T(8,128)(2,1)S(1)} %get-tuple-element.13.refs_11_) | copy-start | bytes 84934656
  44.8 1.3 %collective-permute-start.7 = (f32[128,128]{1,0:T(8,128)S(1)}, f32[128,128]{1,0:T(8,128)S(1)}, u32[]{:S(2)}, u32[]{:S(2)}) collective-permute-start(f32[128,128]{1,0:T(8,128)S(1)} %row_sums.1.refs_1_), channel_id=1, source_target_pairs={{0,1},{1,0},{2,3},{3,2},{4,5},{5,4},{6,7},{7,6},{8,9},{9,8},{10,11... | collective-permute-start | bytes 196616 | tf_op jit(solution)/shard_map/ppermute | solution.py:328
  46.1 9.1 %copy-start.1 = (bf16[9216,1536]{1,0:T(8,128)(2,1)S(1)}, bf16[9216,1536]{1,0:T(8,128)(2,1)}, u32[]{:S(2)}) copy-start(bf16[9216,1536]{1,0:T(8,128)(2,1)} %copy-done) | copy-start | bytes 84934656
  61.1 1.6 %collective-permute-start.8 = (f32[32,2048]{1,0:T(8,128)S(1)}, f32[32,2048]{1,0:T(8,128)S(1)}, u32[]{:S(2)}, u32[]{:S(2)}) collective-permute-start(f32[32,2048]{1,0:T(8,128)S(1)} %get-tuple-element.16), channel_id=1, source_target_pairs={{0,1},{1,0},{2,3},{3,2},{4,5},{5,4},{6,7},{7,6},{8,9},{9,8},{10,11... | collective-permute-start | bytes 786440 | tf_op jit(solution)/shard_map/ppermute | solution.py:328
  63.5 12.3 %all-to-all-start = ((bf16[8,4,2560]{2,1,0:T(4,128)(2,1)}), bf16[8,4,2560]{2,1,0:T(4,128)(2,1)S(1)}, u32[]{:S(2)}, u32[]{:S(2)}) async-start(bf16[8,4,2560]{2,1,0:T(4,128)(2,1)} %sum_of_cores.1), calls=%async_computation | async-start | bytes 327680 | tf_op jit(solution)/shard_map/all_to_all | solution.py:384
  77.5 4.8 %collective-permute-start.10 = (bf16[4,12288]{1,0:T(4,128)(2,1)S(1)}, bf16[4,12288]{1,0:T(4,128)(2,1)S(1)}, u32[]{:S(2)}, u32[]{:S(2)}) collective-permute-start(bf16[4,12288]{1,0:T(4,128)(2,1)S(1)} %attention.1.refs_0_), channel_id=1, source_target_pairs={{0,4},{2,6},{4,0},{6,2},{8,12},{10,14},{12,8},{14,10},{1,5},{3,7},... | collective-permute-start | bytes 294920 | tf_op jit(solution)/shard_map/ppermute | solution.py:328
  77.6 9.5 %collective-permute-start.12 = (bf16[4,12288]{1,0:T(4,128)(2,1)S(1)}, bf16[4,12288]{1,0:T(4,128)(2,1)S(1)}, u32[]{:S(2)}, u32[]{:S(2)}) collective-permute-start(bf16[4,12288]{1,0:T(4,128)(2,1)S(1)} %attention.1.refs_0_), channel_id=1, source_target_pairs={{0,8},{2,10},{4,12},{6,14},{8,0},{10,2},{12,4},{14,6},{1,9},{3,11}... | collective-permute-start | bytes 294920 | tf_op jit(solution)/shard_map/ppermute | solution.py:328
  78.7 9.5 %collective-permute-start.14 = (bf16[4,12288]{1,0:T(4,128)(2,1)S(1)}, bf16[4,12288]{1,0:T(4,128)(2,1)S(1)}, u32[]{:S(2)}, u32[]{:S(2)}) collective-permute-start(bf16[4,12288]{1,0:T(4,128)(2,1)S(1)} %attention.1.refs_0_), channel_id=1, source_target_pairs={{0,12},{2,14},{4,8},{6,10},{8,4},{10,6},{12,0},{14,2},{1,13},{3,15... | collective-permute-start | bytes 294920 | tf_op jit(solution)/shard_map/ppermute | solution.py:328
  82.0 7.1 %collective-permute-start.9 = (bf16[4,12288]{1,0:T(4,128)(2,1)S(1)}, bf16[4,12288]{1,0:T(4,128)(2,1)S(1)}, u32[]{:S(2)}, u32[]{:S(2)}) collective-permute-start(bf16[4,12288]{1,0:T(4,128)(2,1)S(1)} %attention.1.refs_0_), channel_id=1, source_target_pairs={{0,2},{2,0},{4,6},{6,4},{8,10},{10,8},{12,14},{14,12},{1,3},{3,1},... | collective-permute-start | bytes 294920 | tf_op jit(solution)/shard_map/ppermute | solution.py:328
  82.3 6.8 %collective-permute-start.11 = (bf16[4,12288]{1,0:T(4,128)(2,1)S(1)}, bf16[4,12288]{1,0:T(4,128)(2,1)S(1)}, u32[]{:S(2)}, u32[]{:S(2)}) collective-permute-start(bf16[4,12288]{1,0:T(4,128)(2,1)S(1)} %collective-permute-done.10.refs_2_), channel_id=1, source_target_pairs={{0,2},{2,0},{4,6},{6,4},{8,10},{10,8},{12,14},{14,12},{1,3},{3,1},... | collective-permute-start | bytes 294920 | tf_op jit(solution)/shard_map/ppermute | solution.py:328
  87.1 4.6 %collective-permute-start.13 = (bf16[4,12288]{1,0:T(4,128)(2,1)S(1)}, bf16[4,12288]{1,0:T(4,128)(2,1)S(1)}, u32[]{:S(2)}, u32[]{:S(2)}) collective-permute-start(bf16[4,12288]{1,0:T(4,128)(2,1)S(1)} %collective-permute-done.12.refs_4_), channel_id=1, source_target_pairs={{0,2},{2,0},{4,6},{6,4},{8,10},{10,8},{12,14},{14,12},{1,3},{3,1},... | collective-permute-start | bytes 294920 | tf_op jit(solution)/shard_map/ppermute | solution.py:328
  88.3 4.6 %collective-permute-start.15 = (bf16[4,12288]{1,0:T(4,128)(2,1)S(1)}, bf16[4,12288]{1,0:T(4,128)(2,1)S(1)}, u32[]{:S(2)}, u32[]{:S(2)}) collective-permute-start(bf16[4,12288]{1,0:T(4,128)(2,1)S(1)} %collective-permute-done.14.refs_6_), channel_id=1, source_target_pairs={{0,2},{2,0},{4,6},{6,4},{8,10},{10,8},{12,14},{14,12},{1,3},{3,1},... | collective-permute-start | bytes 294920 | tf_op jit(solution)/shard_map/ppermute | solution.py:328
  93.1 9.3 %collective-permute-start.16 = (bf16[32,12288]{1,0:T(8,128)(2,1)S(1)}, bf16[32,12288]{1,0:T(8,128)(2,1)S(1)}, u32[]{:S(2)}, u32[]{:S(2)}) collective-permute-start(bf16[32,12288]{1,0:T(8,128)(2,1)S(1)} %join_contexts.1.mine), channel_id=1, source_target_pairs={{0,1},{1,0},{2,3},{3,2},{4,5},{5,4},{6,7},{7,6},{8,9},{9,8},{10,11... | collective-permute-start | bytes 2359304 | tf_op jit(solution)/shard_map/ppermute | solution.py:328

commit v3 on v2

--- a/solution.py
+++ b/solution.py
@@ -116,11 +116,9 @@
 IN_HBM = pl.BlockSpec(memory_space=pltpu.HBM)
 
 
-def call(kernel, name, out_shape, args, in_specs=None, scratch=(), limit=12 * MIB, flops=0):
-    leaves = jax.tree.leaves(out_shape)
-    moved = sum(a.size * a.dtype.itemsize for a in args) + sum(
-        o.size * jnp.dtype(o.dtype).itemsize if hasattr(o, "size") else 0 for o in leaves
-    )
+def call(kernel, name, out_shape, args, in_specs=None, scratch=(), limit=12 * MIB, flops=0, moved=None, aliases=None):
+    if moved is None:
+        moved = sum(a.size * a.dtype.itemsize for a in args)
     return pl.pallas_call(
         kernel,
         out_shape=out_shape,
@@ -128,37 +126,48 @@
         out_specs=jax.tree.map(lambda _: IN_VMEM, out_shape),
         scratch_shapes=list(scratch),
         compiler_params=pltpu.CompilerParams(vmem_limit_bytes=limit),
+        input_output_aliases=aliases or {},
         cost_estimate=pl.CostEstimate(flops=flops, bytes_accessed=moved, transcendentals=0),
         name=name,
     )(*args)
 
 
-def load_kernel(pieces, *refs):
-    count = len(pieces)
-    sources, targets, sems = refs[:count], refs[count : 2 * count], refs[2 * count]
+def in_hbm(array):
+    return pltpu.with_memory_space_constraint(array, pltpu.HBM)
+
+
+def load_kernel(start, size, pieces, *refs):
+    source, target, sems = refs[0], refs[-2], refs[-1]
+    step = size // pieces
     copies = []
-    for source, target, cuts in zip(sources, targets, pieces):
-        rows = source.shape[0] // cuts
-        for cut in range(cuts):
-            part = pl.ds(cut * rows, rows)
-            copies.append(
-                pltpu.make_async_copy(source.at[part], target.at[part], sems.at[len(copies)])
-            )
+    for at in range(pieces):
+        part = pl.ds(start + at * step, step)
+        copies.append(pltpu.make_async_copy(source.at[part], target.at[part], sems.at[at]))
     for copy in copies:
         copy.start()
     for copy in copies:
         copy.wait()
 
 
-def load(name, pieces, *arrays):
+def load(name, source, at, parts, held=None, after=(), pieces=4):
+    size = source.shape[0] // parts
+    args = [in_hbm(source), *after]
+    specs = [IN_HBM] + [pl.BlockSpec(memory_space=pl.ANY)] * len(after)
+    aliases = {}
+    if held is not None:
+        aliases = {len(args): 0}
+        args.append(held)
+        specs.append(IN_VMEM)
     return call(
-        functools.partial(load_kernel, pieces),
+        functools.partial(load_kernel, at * size, size, pieces),
         name,
-        [pltpu.VMEM(a.shape, a.dtype) for a in arrays],
-        arrays,
-        in_specs=[IN_HBM] * len(arrays),
-        scratch=[pltpu.SemaphoreType.DMA((sum(pieces),))],
+        pltpu.VMEM(source.shape, source.dtype),
+        args,
+        in_specs=specs,
+        scratch=[pltpu.SemaphoreType.DMA((pieces,))],
         limit=MIB,
+        moved=2 * size * source.shape[1],
+        aliases=aliases,
     )
 
 
@@ -177,8 +186,11 @@
 
 
 def project_kernel(steps, width_total, *refs):
-    place, mine, theirs = refs[:3]
-    *blocks, w_query, w_keyval, keep, send, result = refs[3:]
+    place, mine, theirs, w_keyval_far = refs[:4]
+    *inner, keep, send, result, w_keyval, sem = refs[4:]
+    w_query, *blocks = inner
+    fetch = pltpu.make_async_copy(w_keyval_far, w_keyval, sem)
+    fetch.start()
     wide_at, narrow_at = place[0], place[1]
     rows = result.shape[0]
     width, columns = w_keyval.shape[0], w_query.shape[1]
@@ -190,15 +202,15 @@
         values = block[...].astype(jnp.float32)
         normed = ((values[:rows] - average) * scale * values[rows : rows + 1]).astype(jnp.bfloat16)
         owner = jnp.bitwise_xor(wide_at, k)
-        weights = w_query[pl.ds(pl.multiple_of(owner * width, width), width), :]
-        product = jnp.dot(normed, weights, preferred_element_type=jnp.float32)
+        features = pl.ds(pl.multiple_of(owner * width, width), width)
+        product = jnp.dot(normed, w_query[features, :], preferred_element_type=jnp.float32)
         if k == 0:
+            own = normed
             result[:, :columns] = product
-            result[:, columns:] = jnp.dot(
-                normed, w_keyval[...], preferred_element_type=jnp.float32
-            )
         else:
             result[:, :columns] += product
+    fetch.wait()
+    result[:, columns:] = jnp.dot(own, w_keyval[...], preferred_element_type=jnp.float32)
     half = rows // steps // 2
     for step in range(steps):
         for out, core in ((keep, narrow_at), (send, 1 - narrow_at)):
@@ -225,7 +237,14 @@
             ].astype(jnp.bfloat16)
 
 
-def attend_kernel(columns, length, cosine, sine, arrived, cache_keys, cache_values, out, queries, fresh_rows):
+def attend_kernel(
+    columns, length, cosine, sine, arrived, keys_far, values_far,
+    out, queries, fresh_rows, cache_keys, cache_values, sems,
+):
+    fetch_keys = pltpu.make_async_copy(keys_far, cache_keys, sems.at[0])
+    fetch_values = pltpu.make_async_copy(values_far, cache_values, sems.at[1])
+    fetch_keys.start()
+    fetch_values.start()
     wide, steps, _ = arrived.shape
     size = cache_keys.shape[1]
     half = size // 2
@@ -259,6 +278,7 @@
     new_values = fresh_rows[1].astype(jnp.bfloat16)
     score_scale = 1.0 / size**0.5
     by_row = (((1,), (1,)), ((), ()))
+    fetch_keys.wait()
     scores = score_scale * lax.dot_general(
         query, cache_keys[...], by_row, preferred_element_type=jnp.float32
     )
@@ -278,6 +298,7 @@
     share = 1.0 / (
         jnp.sum(weights, axis=1, keepdims=True) + jnp.sum(fresh_weights, axis=1, keepdims=True)
     )
+    fetch_values.wait()
     context = jnp.dot(
         (weights * share).astype(jnp.bfloat16),
         cache_values[...],
@@ -302,13 +323,15 @@
     out[...] = held[...].astype(jnp.bfloat16)
 
 
-def output_kernel(steps, depth, place, mine, theirs, w_out, out, result, ordered):
+def output_kernel(steps, place, mine, theirs, w_out, out, result, ordered):
     wide_at, narrow_at = place[0], place[1]
     count = mine.shape[0] // steps
     batch = 2 * count
+    depth = w_out.shape[0] // 8
     for at in range(0, w_out.shape[0], depth):
-        rows = jnp.concatenate([mine[:, at : at + depth], theirs[:, at : at + depth]], axis=0)
-        product = jnp.dot(rows, w_out[at : at + depth, :], preferred_element_type=jnp.float32)
+        part = slice(at, at + depth)
+        rows = jnp.concatenate([mine[:, part], theirs[:, part]], axis=0)
+        product = jnp.dot(rows, w_out[part, :], preferred_element_type=jnp.float32)
         if at == 0:
             result[...] = product
         else:
@@ -351,14 +374,7 @@
         [tokens.reshape(rows, width), norm_gain[None], jnp.zeros((7, width), bf16)]
     )
     blocks = gather_wide(payload, wide_count)
-    query_weights, keyval_weights, keys, values = load(
-        "load_query_weights",
-        (8, 1, 1, 1),
-        w_query,
-        w_keyval,
-        cache_keys.reshape(cache_keys.shape[1:]),
-        cache_values.reshape(cache_values.shape[1:]),
-    )
+    query_weights = load("load_query_weights", w_query, 0, 1, pieces=8)
     sums = call(
         functools.partial(stats_kernel, rows),
         "row_sums",
@@ -369,9 +385,13 @@
         functools.partial(project_kernel, steps, width * wide_count * narrow_count),
         "norm_and_project",
         [jax.ShapeDtypeStruct((rows // 2, columns + tail), f32)] * 2,
-        [place, sums, swap(sums, "narrow", 1), *blocks, query_weights, keyval_weights],
-        in_specs=[IN_SMEM] + [IN_VMEM] * (wide_count + 4),
-        scratch=[pltpu.VMEM((rows, columns + tail), f32)],
+        [place, sums, swap(sums, "narrow", 1), in_hbm(w_keyval), query_weights, *blocks],
+        in_specs=[IN_SMEM, IN_VMEM, IN_VMEM, IN_HBM] + [IN_VMEM] * (wide_count + 1),
+        scratch=[
+            pltpu.VMEM((rows, columns + tail), f32),
+            pltpu.VMEM(w_keyval.shape, bf16),
+            pltpu.SemaphoreType.DMA,
+        ],
         flops=2 * rows * width * wide_count * columns,
     )
     outgoing = call(
@@ -382,6 +402,8 @@
         scratch=[pltpu.VMEM(((columns + 2 * tail) // 128, rows // 2, 128), f32)],
     )
     arrived = lax.all_to_all(outgoing, "wide", 0, 0, tiled=True)
+    keys = cache_keys.reshape(cache_keys.shape[1:])
+    values = cache_values.reshape(cache_values.shape[1:])
     ladder = jnp.arange(size // 2, dtype=f32)
     frequency = jnp.exp(ladder * (-2.0 / size) * jnp.log(10000.0))
     angles = (lengths + jnp.arange(steps)).astype(f32)[:, None] * frequency
@@ -389,15 +411,20 @@
         functools.partial(attend_kernel, columns),
         "attention",
         jax.ShapeDtypeStruct((steps, H * size), bf16),
-        [lengths, jnp.cos(angles), jnp.sin(angles), arrived, keys, values],
-        in_specs=[IN_SMEM] + [IN_VMEM] * 5,
-        scratch=[pltpu.VMEM((steps * H, size), f32), pltpu.VMEM((2, 128, size), f32)],
+        [lengths, jnp.cos(angles), jnp.sin(angles), arrived, in_hbm(keys), in_hbm(values)],
+        in_specs=[IN_SMEM] + [IN_VMEM] * 3 + [IN_HBM] * 2,
+        scratch=[
+            pltpu.VMEM((steps * H, size), f32),
+            pltpu.VMEM((2, 128, size), f32),
+            pltpu.VMEM(keys.shape, bf16),
+            pltpu.VMEM(values.shape, bf16),
+            pltpu.SemaphoreType.DMA((2,)),
+        ],
         limit=16 * MIB,
         flops=4 * steps * H * size * keys.shape[0],
     )
-    w_out, context = lax.optimization_barrier((w_out, context))
     contexts = gather_wide(context, wide_count)
-    (out_weights,) = load("load_out_weights", (8,), w_out)
+    out_weights = load("load_out_weights", w_out, 0, 1, pieces=8, after=[context])
     mine = call(
         assemble_kernel,
         "join_contexts",
@@ -406,7 +433,7 @@
         scratch=[pltpu.VMEM((wide_count * steps, H * size), f32)],
     )
     return call(
-        functools.partial(output_kernel, steps, w_out.shape[0] // 8),
+        functools.partial(output_kernel, steps),
         "project_out",
         jax.ShapeDtypeStruct((steps, batch, w_out.shape[1]), bf16),
         [place, mine, swap(mine, "narrow", 1), out_weights],

time: 109 us -> 89.5 us (0.82)
  local copies, waits for them, and re-layouts: 22.9 us -> 0.77 us
  Pallas kernels: 33.8 us -> 36.3 us
    unnamed x10 -> x0, local copies, waits for them, and re-layouts: 22.1 us -> none
    pallas_call x8, Pallas kernels: 33.8 us -> 36.3 us  [call(): pl.pallas_call(kernel, out_shape=out_shape, in_specs=in_specs or [IN_VMEM...]
  transfers between devices with their start and end apart: 18 -> 18, of which waited for: 8 -> 8; matrix products, arithmetic and copies ran while one was open for 0% -> 0% of each run, Pallas kernels for 17% -> 21%
where the time goes in v3:
time: 89.5 us; the launch traced here: 89.2 us
  Pallas kernels  36.3 us (41%)
  waiting for transfers between devices  25.6 us (29%)
  starting transfers between devices  24.5 us (27%)
  other arithmetic  1.21 us (1%)
    pallas_call x8, Pallas kernels, call(): pl.pallas_call(kernel, out_shape=out_shape, in_specs=in_specs or [IN_VMEM...  36.3 us
    ppermute x17, starting transfers between devices, swap(): return lax.ppermute(value, axis, [(at, at ^ bits) for at in range(size)])  20 us
    ppermute x17, waiting for transfers between devices, swap(): return lax.ppermute(value, axis, [(at, at ^ bits) for at in range(size)])  17.9 us
    all_to_all x1, waiting for transfers between devices, local_fast(): arrived = lax.all_to_all(outgoing, 'wide', 0, 0, tiled=True)  7.68 us
    all_to_all x1, starting transfers between devices, local_fast(): arrived = lax.all_to_all(outgoing, 'wide', 0, 0, tiled=True)  4.52 us
  transfers between devices with their start and end apart: 18, of which 8 were waited for; matrix products, arithmetic and copies ran while one was open for 0% of the time, Pallas kernels for 21%

profile of v3, /device:TPU:0, one launch (start us, length us, event | category | flops | bytes accessed | tf_op | source)
XLA Modules:
  0.0 89.2 jit_solution(11950109923132236723)
XLA Ops:
  0.0 0.7 broadcast_in_dim.8
  0.7 0.1 pad.2.clone
  0.8 1.0 %maximum_maximum_fusion.refs_0_.refs_5_ = bf16[72,1152]{1,0:T(8,128)(2,1)S(1)} fusion(bf16[1,1152]{1,0:T(2,128)(2,1)S(1)} %broadcast_in_dim.8, bf16[64,1152]{1,0:T(8,128)(2,1)} %bitcast.9, bf16[72]{0:T(256)(128)(2,1)S(1)} %pad.2.clone), kind=kLoop, calls=%fused_computation | loop fusion | flops 497664 | bytes 315792 | tf_op jit(solution)/shard_map/concatenate | solution.py:373
  1.8 3.1 %collective-permute-start.1 = (bf16[72,1152]{1,0:T(8,128)(2,1)S(1)}, bf16[72,1152]{1,0:T(8,128)(2,1)S(1)}, u32[]{:S(2)}, u32[]{:S(2)}) collective-permute-start(bf16[72,1152]{1,0:T(8,128)(2,1)S(1)} %maximum_maximum_fusion.refs_0_.refs_5_), channel_id=1, source_target_pairs={{0,4},{2,6},{4,0},{6,2},{8,12},{10,14},{12,8},{14,10},{1,5},{3,7},... | collective-permute-start | bytes 497672 | tf_op jit(solution)/shard_map/ppermute | solution.py:351
  4.9 2.6 %collective-permute-start.3 = (bf16[72,1152]{1,0:T(8,128)(2,1)S(1)}, bf16[72,1152]{1,0:T(8,128)(2,1)S(1)}, u32[]{:S(2)}, u32[]{:S(2)}) collective-permute-start(bf16[72,1152]{1,0:T(8,128)(2,1)S(1)} %maximum_maximum_fusion.refs_0_.refs_5_), channel_id=1, source_target_pairs={{0,8},{2,10},{4,12},{6,14},{8,0},{10,2},{12,4},{14,6},{1,9},{3,11}... | collective-permute-start | bytes 497672 | tf_op jit(solution)/shard_map/ppermute | solution.py:351
  7.5 0.0 collective-permute-start.5
  7.5 1.7 %collective-permute-start = (bf16[72,1152]{1,0:T(8,128)(2,1)S(1)}, bf16[72,1152]{1,0:T(8,128)(2,1)S(1)}, u32[]{:S(2)}, u32[]{:S(2)}) collective-permute-start(bf16[72,1152]{1,0:T(8,128)(2,1)S(1)} %maximum_maximum_fusion.refs_0_.refs_5_), channel_id=1, source_target_pairs={{0,2},{2,0},{4,6},{6,4},{8,10},{10,8},{12,14},{14,12},{1,3},{3,1},... | collective-permute-start | bytes 497672 | tf_op jit(solution)/shard_map/ppermute | solution.py:351
  9.2 2.5 %collective-permute-done.1.refs_2_.refs_7_ = bf16[72,1152]{1,0:T(8,128)(2,1)S(1)} collective-permute-done((bf16[72,1152]{1,0:T(8,128)(2,1)S(1)}, bf16[72,1152]{1,0:T(8,128)(2,1)S(1)}, u32[]{:S(2)}, u32[]{:S(2)}) %collective-permute-start.1) | collective-permute-done | bytes 165920 | tf_op jit(solution)/shard_map/ppermute | solution.py:351
  11.7 1.7 %collective-permute-start.2 = (bf16[72,1152]{1,0:T(8,128)(2,1)S(1)}, bf16[72,1152]{1,0:T(8,128)(2,1)S(1)}, u32[]{:S(2)}, u32[]{:S(2)}) collective-permute-start(bf16[72,1152]{1,0:T(8,128)(2,1)S(1)} %collective-permute-done.1.refs_2_.refs_7_), channel_id=1, source_target_pairs={{0,2},{2,0},{4,6},{6,4},{8,10},{10,8},{12,14},{14,12},{1,3},{3,1},... | collective-permute-start | bytes 497672 | tf_op jit(solution)/shard_map/ppermute | solution.py:351
  13.4 6.7 %collective-permute-done.3.refs_4_.refs_9_ = bf16[72,1152]{1,0:T(8,128)(2,1)S(1)} collective-permute-done((bf16[72,1152]{1,0:T(8,128)(2,1)S(1)}, bf16[72,1152]{1,0:T(8,128)(2,1)S(1)}, u32[]{:S(2)}, u32[]{:S(2)}) %collective-permute-start.3) | collective-permute-done | bytes 165920 | tf_op jit(solution)/shard_map/ppermute | solution.py:351
  20.1 1.5 %collective-permute-start.4 = (bf16[72,1152]{1,0:T(8,128)(2,1)S(1)}, bf16[72,1152]{1,0:T(8,128)(2,1)S(1)}, u32[]{:S(2)}, u32[]{:S(2)}) collective-permute-start(bf16[72,1152]{1,0:T(8,128)(2,1)S(1)} %collective-permute-done.3.refs_4_.refs_9_), channel_id=1, source_target_pairs={{0,2},{2,0},{4,6},{6,4},{8,10},{10,8},{12,14},{14,12},{1,3},{3,1},... | collective-permute-start | bytes 497672 | tf_op jit(solution)/shard_map/ppermute | solution.py:351
  21.5 0.0 collective-permute-done.5.refs_6_.refs_11_
  21.5 0.5 collective-permute-start.6
  22.1 9.2 %load_query_weights.1.refs_4_ = bf16[9216,1536]{1,0:T(8,128)(2,1)S(1)} custom-call(bf16[9216,1536]{1,0:T(8,128)(2,1)} %refs_0_.2), custom_call_target="tpu_custom_call" | custom-call | bytes 28311552 | tf_op jit(solution)/shard_map/load_query_weights/pallas_call | solution.py:122
  31.3 0.0 collective-permute-done.refs_1_.refs_6_
  31.3 0.0 collective-permute-done.2.refs_3_.refs_8_
  31.3 0.0 collective-permute-done.4.refs_5_.refs_10_
  31.3 0.0 collective-permute-done.6.refs_7_.refs_12_
  31.3 0.4 row_sums.1.refs_1_
  31.7 0.1 collective-permute-start.7
  31.8 0.1 pad_add_fusion.refs_0_.place
  31.8 1.2 %collective-permute-done.7.refs_2_ = f32[128,128]{1,0:T(8,128)S(1)} collective-permute-done((f32[128,128]{1,0:T(8,128)S(1)}, f32[128,128]{1,0:T(8,128)S(1)}, u32[]{:S(2)}, u32[]{:S(2)}) %collective-permute-start.7) | collective-permute-done | bytes 65568 | tf_op jit(solution)/shard_map/ppermute | solution.py:351
  33.0 7.2 %norm_and_project.1 = (f32[32,2048]{1,0:T(8,128)S(1)}, f32[32,2048]{1,0:T(8,128)S(1)}) custom-call(s32[2]{0:T(128)S(1)} %pad_add_fusion.refs_0_.place, f32[128,128]{1,0:T(8,128)S(1)} %row_sums.1.refs_1_, f32[128,128]{1,0:T(8,128)S(1)} %collective-permute-done.7.refs_2_, bf16[1152,512]{1,0:T(8,128)(2,1)} %refs_3_.1, ...), custom_call_target="tpu_custom_call" | custom-call | flops 1811939328 | bytes 30949384 | tf_op jit(solution)/shard_map/norm_and_project/pallas_call | solution.py:122
  40.2 0.2 collective-permute-start.8
  41.1 0.7 collective-permute-done.8.theirs
  41.8 0.8 sum_of_cores.1
  42.6 4.5 %all-to-all-start = ((bf16[8,4,2560]{2,1,0:T(4,128)(2,1)}), bf16[8,4,2560]{2,1,0:T(4,128)(2,1)S(1)}, u32[]{:S(2)}, u32[]{:S(2)}) async-start(bf16[8,4,2560]{2,1,0:T(4,128)(2,1)} %sum_of_cores.1), calls=%async_computation | async-start | bytes 327680 | tf_op jit(solution)/shard_map/all_to_all | solution.py:404
  47.1 0.1 multiply_sine_fusion
  47.2 7.7 %all-to-all-done.arrived = bf16[8,4,2560]{2,1,0:T(4,128)(2,1)S(1)} async-done(((bf16[8,4,2560]{2,1,0:T(4,128)(2,1)}), bf16[8,4,2560]{2,1,0:T(4,128)(2,1)S(1)}, u32[]{:S(2)}, u32[]{:S(2)}) %all-to-all-start) | async-done | bytes 163872 | tf_op jit(solution)/shard_map/all_to_all | solution.py:404
  54.9 3.0 %attention.1.refs_0_.refs_1_ = bf16[4,12288]{1,0:T(4,128)(2,1)S(1)} custom-call(s32[1]{0:T(128)} %copy.9.length, f32[4,128]{1,0:T(4,128)S(1)} %get-tuple-element.10.cosine, f32[4,128]{1,0:T(4,128)S(1)} %get-tuple-element.9.sine, bf16[8,4,2560]{2,1,0:T(4,128)(2,1)S(1)} %all-to-all-done.arrived, bf16[2048,256]{1,0:T(8,128)(2,1)} %bitcast.7, ...), custom_call_target="tpu_custom_call" | custom-call | flops 402653184 | bytes 2265092 | tf_op jit(solution)/shard_map/attention/pallas_call | solution.py:122
  57.9 0.1 collective-permute-start.10
  58.0 1.1 %collective-permute-start.12 = (bf16[4,12288]{1,0:T(4,128)(2,1)S(1)}, bf16[4,12288]{1,0:T(4,128)(2,1)S(1)}, u32[]{:S(2)}, u32[]{:S(2)}) collective-permute-start(bf16[4,12288]{1,0:T(4,128)(2,1)S(1)} %attention.1.refs_0_.refs_1_), channel_id=1, source_target_pairs={{0,8},{2,10},{4,12},{6,14},{8,0},{10,2},{12,4},{14,6},{1,9},{3,11}... | collective-permute-start | bytes 294920 | tf_op jit(solution)/shard_map/ppermute | solution.py:351
  59.1 3.3 %collective-permute-start.14 = (bf16[4,12288]{1,0:T(4,128)(2,1)S(1)}, bf16[4,12288]{1,0:T(4,128)(2,1)S(1)}, u32[]{:S(2)}, u32[]{:S(2)}) collective-permute-start(bf16[4,12288]{1,0:T(4,128)(2,1)S(1)} %attention.1.refs_0_.refs_1_), channel_id=1, source_target_pairs={{0,12},{2,14},{4,8},{6,10},{8,4},{10,6},{12,0},{14,2},{1,13},{3,15... | collective-permute-start | bytes 294920 | tf_op jit(solution)/shard_map/ppermute | solution.py:351
  62.4 0.3 collective-permute-start.9
  62.7 0.0 collective-permute-done.10.refs_2_
  62.7 1.7 %collective-permute-start.11 = (bf16[4,12288]{1,0:T(4,128)(2,1)S(1)}, bf16[4,12288]{1,0:T(4,128)(2,1)S(1)}, u32[]{:S(2)}, u32[]{:S(2)}) collective-permute-start(bf16[4,12288]{1,0:T(4,128)(2,1)S(1)} %collective-permute-done.10.refs_2_), channel_id=1, source_target_pairs={{0,2},{2,0},{4,6},{6,4},{8,10},{10,8},{12,14},{14,12},{1,3},{3,1},... | collective-permute-start | bytes 294920 | tf_op jit(solution)/shard_map/ppermute | solution.py:351
  64.4 3.0 %collective-permute-done.12.refs_4_ = bf16[4,12288]{1,0:T(4,128)(2,1)S(1)} collective-permute-done((bf16[4,12288]{1,0:T(4,128)(2,1)S(1)}, bf16[4,12288]{1,0:T(4,128)(2,1)S(1)}, u32[]{:S(2)}, u32[]{:S(2)}) %collective-permute-start.12) | collective-permute-done | bytes 98336 | tf_op jit(solution)/shard_map/ppermute | solution.py:351
  67.5 1.2 %collective-permute-start.13 = (bf16[4,12288]{1,0:T(4,128)(2,1)S(1)}, bf16[4,12288]{1,0:T(4,128)(2,1)S(1)}, u32[]{:S(2)}, u32[]{:S(2)}) collective-permute-start(bf16[4,12288]{1,0:T(4,128)(2,1)S(1)} %collective-permute-done.12.refs_4_), channel_id=1, source_target_pairs={{0,2},{2,0},{4,6},{6,4},{8,10},{10,8},{12,14},{14,12},{1,3},{3,1},... | collective-permute-start | bytes 294920 | tf_op jit(solution)/shard_map/ppermute | solution.py:351
  68.7 0.0 collective-permute-done.14.refs_6_
  68.7 0.8 collective-permute-start.15
  69.5 0.0 collective-permute-done.9.refs_1_
  69.5 0.0 collective-permute-done.11.refs_3_
  69.5 2.6 %collective-permute-done.13.refs_5_ = bf16[4,12288]{1,0:T(4,128)(2,1)S(1)} collective-permute-done((bf16[4,12288]{1,0:T(4,128)(2,1)S(1)}, bf16[4,12288]{1,0:T(4,128)(2,1)S(1)}, u32[]{:S(2)}, u32[]{:S(2)}) %collective-permute-start.13) | collective-permute-done | bytes 98336 | tf_op jit(solution)/shard_map/ppermute | solution.py:351
  72.1 1.2 %collective-permute-done.15.refs_7_ = bf16[4,12288]{1,0:T(4,128)(2,1)S(1)} collective-permute-done((bf16[4,12288]{1,0:T(4,128)(2,1)S(1)}, bf16[4,12288]{1,0:T(4,128)(2,1)S(1)}, u32[]{:S(2)}, u32[]{:S(2)}) %collective-permute-start.15) | collective-permute-done | bytes 98336 | tf_op jit(solution)/shard_map/ppermute | solution.py:351
  73.3 0.3 join_contexts.1.mine
  73.6 0.1 collective-permute-start.16
  73.6 9.2 %load_out_weights.1.w_out = bf16[12288,1152]{1,0:T(8,128)(2,1)S(1)} custom-call(bf16[12288,1152]{1,0:T(8,128)(2,1)} %refs_0_.3, bf16[4,12288]{1,0:T(4,128)(2,1)S(1)} %attention.1.refs_0_.refs_1_), custom_call_target="tpu_custom_call" | custom-call | bytes 28311552 | tf_op jit(solution)/shard_map/load_out_weights/pallas_call | solution.py:122
  82.8 0.0 collective-permute-done.16.theirs
  82.9 6.3 %project_out.1 = bf16[4,16,1152]{2,1,0:T(8,128)(2,1)} custom-call(s32[2]{0:T(128)S(1)} %pad_add_fusion.refs_0_.place, bf16[32,12288]{1,0:T(8,128)(2,1)S(1)} %join_contexts.1.mine, bf16[32,12288]{1,0:T(8,128)(2,1)S(1)} %collective-permute-done.16.theirs, bf16[12288,1152]{1,0:T(8,128)(2,1)S(1)} %load_out_weights.1.w_out), custom_call_target="tpu_custom_call" | custom-call | flops 1811939328 | bytes 29884424 | tf_op jit(solution)/shard_map/project_out/pallas_call | solution.py:122
  (3 shorter events, 0.0 us)
Async XLA Ops:
  1.8 9.9 %collective-permute-start.1 = (bf16[72,1152]{1,0:T(8,128)(2,1)S(1)}, bf16[72,1152]{1,0:T(8,128)(2,1)S(1)}, u32[]{:S(2)}, u32[]{:S(2)}) collective-permute-start(bf16[72,1152]{1,0:T(8,128)(2,1)S(1)} %maximum_maximum_fusion.refs_0_.refs_5_), channel_id=1, source_target_pairs={{0,4},{2,6},{4,0},{6,2},{8,12},{10,14},{12,8},{14,10},{1,5},{3,7},... | collective-permute-start | bytes 497672 | tf_op jit(solution)/shard_map/ppermute | solution.py:351
  4.9 15.2 %collective-permute-start.3 = (bf16[72,1152]{1,0:T(8,128)(2,1)S(1)}, bf16[72,1152]{1,0:T(8,128)(2,1)S(1)}, u32[]{:S(2)}, u32[]{:S(2)}) collective-permute-start(bf16[72,1152]{1,0:T(8,128)(2,1)S(1)} %maximum_maximum_fusion.refs_0_.refs_5_), channel_id=1, source_target_pairs={{0,8},{2,10},{4,12},{6,14},{8,0},{10,2},{12,4},{14,6},{1,9},{3,11}... | collective-permute-start | bytes 497672 | tf_op jit(solution)/shard_map/ppermute | solution.py:351
  7.5 14.1 %collective-permute-start.5 = (bf16[72,1152]{1,0:T(8,128)(2,1)S(1)}, bf16[72,1152]{1,0:T(8,128)(2,1)S(1)}, u32[]{:S(2)}, u32[]{:S(2)}) collective-permute-start(bf16[72,1152]{1,0:T(8,128)(2,1)S(1)} %maximum_maximum_fusion.refs_0_.refs_5_), channel_id=1, source_target_pairs={{0,12},{2,14},{4,8},{6,10},{8,4},{10,6},{12,0},{14,2},{1,13},{3,15... | collective-permute-start | bytes 497672 | tf_op jit(solution)/shard_map/ppermute | solution.py:351
  7.5 23.8 %collective-permute-start = (bf16[72,1152]{1,0:T(8,128)(2,1)S(1)}, bf16[72,1152]{1,0:T(8,128)(2,1)S(1)}, u32[]{:S(2)}, u32[]{:S(2)}) collective-permute-start(bf16[72,1152]{1,0:T(8,128)(2,1)S(1)} %maximum_maximum_fusion.refs_0_.refs_5_), channel_id=1, source_target_pairs={{0,2},{2,0},{4,6},{6,4},{8,10},{10,8},{12,14},{14,12},{1,3},{3,1},... | collective-permute-start | bytes 497672 | tf_op jit(solution)/shard_map/ppermute | solution.py:351
  11.7 19.6 %collective-permute-start.2 = (bf16[72,1152]{1,0:T(8,128)(2,1)S(1)}, bf16[72,1152]{1,0:T(8,128)(2,1)S(1)}, u32[]{:S(2)}, u32[]{:S(2)}) collective-permute-start(bf16[72,1152]{1,0:T(8,128)(2,1)S(1)} %collective-permute-done.1.refs_2_.refs_7_), channel_id=1, source_target_pairs={{0,2},{2,0},{4,6},{6,4},{8,10},{10,8},{12,14},{14,12},{1,3},{3,1},... | collective-permute-start | bytes 497672 | tf_op jit(solution)/shard_map/ppermute | solution.py:351
  20.1 11.3 %collective-permute-start.4 = (bf16[72,1152]{1,0:T(8,128)(2,1)S(1)}, bf16[72,1152]{1,0:T(8,128)(2,1)S(1)}, u32[]{:S(2)}, u32[]{:S(2)}) collective-permute-start(bf16[72,1152]{1,0:T(8,128)(2,1)S(1)} %collective-permute-done.3.refs_4_.refs_9_), channel_id=1, source_target_pairs={{0,2},{2,0},{4,6},{6,4},{8,10},{10,8},{12,14},{14,12},{1,3},{3,1},... | collective-permute-start | bytes 497672 | tf_op jit(solution)/shard_map/ppermute | solution.py:351
  21.5 9.8 %collective-permute-start.6 = (bf16[72,1152]{1,0:T(8,128)(2,1)S(1)}, bf16[72,1152]{1,0:T(8,128)(2,1)S(1)}, u32[]{:S(2)}, u32[]{:S(2)}) collective-permute-start(bf16[72,1152]{1,0:T(8,128)(2,1)S(1)} %collective-permute-done.5.refs_6_.refs_11_), channel_id=1, source_target_pairs={{0,2},{2,0},{4,6},{6,4},{8,10},{10,8},{12,14},{14,12},{1,3},{3,1},... | collective-permute-start | bytes 497672 | tf_op jit(solution)/shard_map/ppermute | solution.py:351
  31.7 1.3 %collective-permute-start.7 = (f32[128,128]{1,0:T(8,128)S(1)}, f32[128,128]{1,0:T(8,128)S(1)}, u32[]{:S(2)}, u32[]{:S(2)}) collective-permute-start(f32[128,128]{1,0:T(8,128)S(1)} %row_sums.1.refs_1_), channel_id=1, source_target_pairs={{0,1},{1,0},{2,3},{3,2},{4,5},{5,4},{6,7},{7,6},{8,9},{9,8},{10,11... | collective-permute-start | bytes 196616 | tf_op jit(solution)/shard_map/ppermute | solution.py:351
  40.2 1.6 %collective-permute-start.8 = (f32[32,2048]{1,0:T(8,128)S(1)}, f32[32,2048]{1,0:T(8,128)S(1)}, u32[]{:S(2)}, u32[]{:S(2)}) collective-permute-start(f32[32,2048]{1,0:T(8,128)S(1)} %get-tuple-element.8), channel_id=1, source_target_pairs={{0,1},{1,0},{2,3},{3,2},{4,5},{5,4},{6,7},{7,6},{8,9},{9,8},{10,11... | collective-permute-start | bytes 786440 | tf_op jit(solution)/shard_map/ppermute | solution.py:351
  42.6 12.3 %all-to-all-start = ((bf16[8,4,2560]{2,1,0:T(4,128)(2,1)}), bf16[8,4,2560]{2,1,0:T(4,128)(2,1)S(1)}, u32[]{:S(2)}, u32[]{:S(2)}) async-start(bf16[8,4,2560]{2,1,0:T(4,128)(2,1)} %sum_of_cores.1), calls=%async_computation | async-start | bytes 327680 | tf_op jit(solution)/shard_map/all_to_all | solution.py:404
  57.9 4.8 %collective-permute-start.10 = (bf16[4,12288]{1,0:T(4,128)(2,1)S(1)}, bf16[4,12288]{1,0:T(4,128)(2,1)S(1)}, u32[]{:S(2)}, u32[]{:S(2)}) collective-permute-start(bf16[4,12288]{1,0:T(4,128)(2,1)S(1)} %attention.1.refs_0_.refs_1_), channel_id=1, source_target_pairs={{0,4},{2,6},{4,0},{6,2},{8,12},{10,14},{12,8},{14,10},{1,5},{3,7},... | collective-permute-start | bytes 294920 | tf_op jit(solution)/shard_map/ppermute | solution.py:351
  58.0 9.5 %collective-permute-start.12 = (bf16[4,12288]{1,0:T(4,128)(2,1)S(1)}, bf16[4,12288]{1,0:T(4,128)(2,1)S(1)}, u32[]{:S(2)}, u32[]{:S(2)}) collective-permute-start(bf16[4,12288]{1,0:T(4,128)(2,1)S(1)} %attention.1.refs_0_.refs_1_), channel_id=1, source_target_pairs={{0,8},{2,10},{4,12},{6,14},{8,0},{10,2},{12,4},{14,6},{1,9},{3,11}... | collective-permute-start | bytes 294920 | tf_op jit(solution)/shard_map/ppermute | solution.py:351
  59.1 9.5 %collective-permute-start.14 = (bf16[4,12288]{1,0:T(4,128)(2,1)S(1)}, bf16[4,12288]{1,0:T(4,128)(2,1)S(1)}, u32[]{:S(2)}, u32[]{:S(2)}) collective-permute-start(bf16[4,12288]{1,0:T(4,128)(2,1)S(1)} %attention.1.refs_0_.refs_1_), channel_id=1, source_target_pairs={{0,12},{2,14},{4,8},{6,10},{8,4},{10,6},{12,0},{14,2},{1,13},{3,15... | collective-permute-start | bytes 294920 | tf_op jit(solution)/shard_map/ppermute | solution.py:351
  62.4 7.1 %collective-permute-start.9 = (bf16[4,12288]{1,0:T(4,128)(2,1)S(1)}, bf16[4,12288]{1,0:T(4,128)(2,1)S(1)}, u32[]{:S(2)}, u32[]{:S(2)}) collective-permute-start(bf16[4,12288]{1,0:T(4,128)(2,1)S(1)} %attention.1.refs_0_.refs_1_), channel_id=1, source_target_pairs={{0,2},{2,0},{4,6},{6,4},{8,10},{10,8},{12,14},{14,12},{1,3},{3,1},... | collective-permute-start | bytes 294920 | tf_op jit(solution)/shard_map/ppermute | solution.py:351
  62.7 6.8 %collective-permute-start.11 = (bf16[4,12288]{1,0:T(4,128)(2,1)S(1)}, bf16[4,12288]{1,0:T(4,128)(2,1)S(1)}, u32[]{:S(2)}, u32[]{:S(2)}) collective-permute-start(bf16[4,12288]{1,0:T(4,128)(2,1)S(1)} %collective-permute-done.10.refs_2_), channel_id=1, source_target_pairs={{0,2},{2,0},{4,6},{6,4},{8,10},{10,8},{12,14},{14,12},{1,3},{3,1},... | collective-permute-start | bytes 294920 | tf_op jit(solution)/shard_map/ppermute | solution.py:351
  67.5 4.6 %collective-permute-start.13 = (bf16[4,12288]{1,0:T(4,128)(2,1)S(1)}, bf16[4,12288]{1,0:T(4,128)(2,1)S(1)}, u32[]{:S(2)}, u32[]{:S(2)}) collective-permute-start(bf16[4,12288]{1,0:T(4,128)(2,1)S(1)} %collective-permute-done.12.refs_4_), channel_id=1, source_target_pairs={{0,2},{2,0},{4,6},{6,4},{8,10},{10,8},{12,14},{14,12},{1,3},{3,1},... | collective-permute-start | bytes 294920 | tf_op jit(solution)/shard_map/ppermute | solution.py:351
  68.7 4.6 %collective-permute-start.15 = (bf16[4,12288]{1,0:T(4,128)(2,1)S(1)}, bf16[4,12288]{1,0:T(4,128)(2,1)S(1)}, u32[]{:S(2)}, u32[]{:S(2)}) collective-permute-start(bf16[4,12288]{1,0:T(4,128)(2,1)S(1)} %collective-permute-done.14.refs_6_), channel_id=1, source_target_pairs={{0,2},{2,0},{4,6},{6,4},{8,10},{10,8},{12,14},{14,12},{1,3},{3,1},... | collective-permute-start | bytes 294920 | tf_op jit(solution)/shard_map/ppermute | solution.py:351
  73.6 9.3 %collective-permute-start.16 = (bf16[32,12288]{1,0:T(8,128)(2,1)S(1)}, bf16[32,12288]{1,0:T(8,128)(2,1)S(1)}, u32[]{:S(2)}, u32[]{:S(2)}) collective-permute-start(bf16[32,12288]{1,0:T(8,128)(2,1)S(1)} %join_contexts.1.mine), channel_id=1, source_target_pairs={{0,1},{1,0},{2,3},{3,2},{4,5},{5,4},{6,7},{7,6},{8,9},{9,8},{10,11... | collective-permute-start | bytes 2359304 | tf_op jit(solution)/shard_map/ppermute | solution.py:351

commit v4 on v3

--- a/solution.py
+++ b/solution.py
@@ -111,6 +111,8 @@
 
 
 MIB = 1 << 20
+EXTRA = 16
+OUT_PIECES = 8
 IN_VMEM = pl.BlockSpec(memory_space=pltpu.VMEM)
 IN_SMEM = pl.BlockSpec(memory_space=pltpu.SMEM)
 IN_HBM = pl.BlockSpec(memory_space=pltpu.HBM)
@@ -136,81 +138,155 @@
     return pltpu.with_memory_space_constraint(array, pltpu.HBM)
 
 
-def load_kernel(start, size, pieces, *refs):
-    source, target, sems = refs[0], refs[-2], refs[-1]
-    step = size // pieces
-    copies = []
-    for at in range(pieces):
-        part = pl.ds(start + at * step, step)
-        copies.append(pltpu.make_async_copy(source.at[part], target.at[part], sems.at[at]))
+def load_kernel(moves, *refs):
+    target, sems = refs[-2], refs[-1]
+    copies = [
+        pltpu.make_async_copy(refs[source].at[box], target.at[to], sems.at[at])
+        for at, (source, box, to) in enumerate(moves)
+    ]
     for copy in copies:
         copy.start()
     for copy in copies:
         copy.wait()
 
 
-def load(name, source, at, parts, held=None, after=(), pieces=4):
-    size = source.shape[0] // parts
-    args = [in_hbm(source), *after]
-    specs = [IN_HBM] + [pl.BlockSpec(memory_space=pl.ANY)] * len(after)
-    aliases = {}
-    if held is not None:
-        aliases = {len(args): 0}
-        args.append(held)
-        specs.append(IN_VMEM)
+def load(name, shape, moves, *sources, after=()):
     return call(
-        functools.partial(load_kernel, at * size, size, pieces),
+        functools.partial(load_kernel, moves),
         name,
-        pltpu.VMEM(source.shape, source.dtype),
-        args,
-        in_specs=specs,
-        scratch=[pltpu.SemaphoreType.DMA((pieces,))],
+        pltpu.VMEM(shape, sources[0].dtype),
+        [in_hbm(source) for source in sources] + list(after),
+        in_specs=[IN_HBM] * len(sources) + [pl.BlockSpec(memory_space=pl.ANY)] * len(after),
+        scratch=[pltpu.SemaphoreType.DMA((len(moves),))],
         limit=MIB,
-        moved=2 * size * source.shape[1],
-        aliases=aliases,
-    )
-
-
-def stats_kernel(rows, *refs):
-    blocks, out = refs[:-1], refs[-1]
+        moved=2 * shape[0] * shape[1],
+    )
+
+
+def boxes(rows, columns, pieces, at_row=0, source=0):
+    step = rows.size // pieces
+    return [
+        (
+            source,
+            (pl.ds(rows.start + at * step, step), columns),
+            (pl.ds(at_row + at * step, step), pl.ds(0, columns.size)),
+        )
+        for at in range(pieces)
+    ]
+
+
+def sums_kernel(tokens, out):
+    rows = tokens.shape[0]
     lanes = out.shape[1]
-    total = jnp.zeros((rows, lanes), jnp.float32)
-    squares = jnp.zeros((rows, lanes), jnp.float32)
-    for block in blocks:
-        for at in range(0, block.shape[1], lanes):
-            values = block[:, at : at + lanes].astype(jnp.float32)[:rows]
-            total = total + values
-            squares = squares + values * values
-    out[:rows] = total
-    out[rows:] = squares
-
-
-def project_kernel(steps, width_total, *refs):
-    place, mine, theirs, w_keyval_far = refs[:4]
-    *inner, keep, send, result, w_keyval, sem = refs[4:]
-    w_query, *blocks = inner
-    fetch = pltpu.make_async_copy(w_keyval_far, w_keyval, sem)
-    fetch.start()
+    values = tokens[...].astype(jnp.float32)
+    at_lane = lax.broadcasted_iota(jnp.int32, (rows, lanes), 1)
+    at_row = lax.broadcasted_iota(jnp.int32, (rows, lanes), 0)
+    out[...] = jnp.zeros_like(out)
+    for row, column in enumerate(
+        (
+            jnp.sum(values, axis=1, keepdims=True),
+            jnp.sum(values * values, axis=1, keepdims=True),
+        )
+    ):
+        out[row : row + 1, :] = jnp.sum(
+            jnp.where(at_lane == at_row, column, 0.0), axis=0, keepdims=True
+        )
+
+
+def payload_kernel(tokens, gain, mine, theirs, out, extra):
+    rows, width = tokens.shape
+    lanes = out.shape[1]
+    parts = width // lanes
+    extra[...] = jnp.zeros_like(extra)
+    for at in range(parts):
+        span = slice(at * lanes, (at + 1) * lanes)
+        extra[at : at + 1, :] = gain[:, span].astype(jnp.float32)
+        out[at * rows : (at + 1) * rows, :] = tokens[:, span]
+    for at in range(2):
+        left = mine[at : at + 1, :] + theirs[at : at + 1, :]
+        for piece in range(3):
+            row = parts + 3 * at + piece
+            part = left.astype(jnp.bfloat16).astype(jnp.float32)
+            extra[row : row + 1, :] = part
+            left = left - part
+    out[parts * rows :, :] = extra[...].astype(jnp.bfloat16)
+
+
+class Stream:
+    def __init__(self, copies, flight=3):
+        self.copies, self.started, self.done = copies, 0, 0
+        self.start(flight)
+
+    def start(self, count):
+        for copy in self.copies[self.started : self.started + count]:
+            copy.start()
+        self.started = min(self.started + count, len(self.copies))
+
+    def take(self, at):
+        while self.done <= at:
+            self.copies[self.done].wait()
+            self.done += 1
+            self.start(1)
+
+
+def project_kernel(steps, width_total, place, w_keyval_far, w_query, early, *refs):
+    *blocks, keep, send, result, normed, late, w_keyval, sems = refs
     wide_at, narrow_at = place[0], place[1]
     rows = result.shape[0]
-    width, columns = w_keyval.shape[0], w_query.shape[1]
-    sums = jnp.sum(mine[...] + theirs[...], axis=1, keepdims=True)
-    average = sums[:rows] / width_total
-    spread = sums[rows:] / width_total - average * average
+    width, part = w_keyval.shape[0], early.shape[1]
+    columns = w_query.shape[1]
+    lanes = blocks[0].shape[1]
+    parts = width // lanes
+    spots = [
+        pl.ds(pl.multiple_of(jnp.bitwise_xor(wide_at, k) * width, width), width)
+        for k in range(len(blocks))
+    ]
+    stream = Stream(
+        [pltpu.make_async_copy(w_keyval_far, w_keyval, sems.at[len(blocks)])]
+        + [
+            pltpu.make_async_copy(
+                w_query.at[spot, pl.ds(part, columns - part)], late.at[spot], sems.at[k]
+            )
+            for k, spot in enumerate(spots)
+        ]
+    )
+    tail = pl.ds(parts * rows, blocks[0].shape[0] - parts * rows)
+    sums = blocks[0][tail, :].astype(jnp.float32)
+    for block in blocks[1:]:
+        sums = sums + block[tail, :].astype(jnp.float32)
+    totals = [
+        sums[at : at + 1] + sums[at + 1 : at + 2] + sums[at + 2 : at + 3]
+        for at in (parts, parts + 3)
+    ]
+    average = totals[0] / width_total
+    spread = totals[1] / width_total - average * average
     scale = lax.rsqrt(spread + epsilon)
-    for k, block in enumerate(blocks):
-        values = block[...].astype(jnp.float32)
-        normed = ((values[:rows] - average) * scale * values[rows : rows + 1]).astype(jnp.bfloat16)
-        owner = jnp.bitwise_xor(wide_at, k)
-        features = pl.ds(pl.multiple_of(owner * width, width), width)
-        product = jnp.dot(normed, w_query[features, :], preferred_element_type=jnp.float32)
-        if k == 0:
-            own = normed
-            result[:, :columns] = product
-        else:
-            result[:, :columns] += product
-    fetch.wait()
-    result[:, columns:] = jnp.dot(own, w_keyval[...], preferred_element_type=jnp.float32)
+    at_lane = lax.broadcasted_iota(jnp.int32, (rows, lanes), 1)
+    at_row = lax.broadcasted_iota(jnp.int32, (rows, lanes), 0)
+
+    def stand(flat):
+        return jnp.sum(jnp.where(at_lane == at_row, flat, 0.0), axis=1, keepdims=True)
+
+    average, scale = stand(average), stand(scale)
+    for weights, span in ((early, slice(0, part)), (late, slice(part, columns))):
+        for k, block in enumerate(blocks):
+            if weights is early:
+                gains = block[tail, :].astype(jnp.float32)
+                for at in range(parts):
+                    values = block[at * rows : (at + 1) * rows, :].astype(jnp.float32)
+                    normed[k, :, at * lanes : (at + 1) * lanes] = (
+                        (values - average) * scale * gains[at : at + 1]
+                    ).astype(jnp.bfloat16)
+            else:
+                stream.take(k + 1)
+            product = jnp.dot(normed[k], weights[spots[k], :], preferred_element_type=jnp.float32)
+            if k == 0:
+                result[:, span] = product
+            else:
+                result[:, span] += product
+            if weights is early and k in (2, 4, 6):
+                stream.take(k // 2 - 1)
+    result[:, columns:] = jnp.dot(normed[0], w_keyval[...], preferred_element_type=jnp.float32)
     half = rows // steps // 2
     for step in range(steps):
         for out, core in ((keep, narrow_at), (send, 1 - narrow_at)):
@@ -238,15 +314,11 @@
 
 
 def attend_kernel(
-    columns, length, cosine, sine, arrived, keys_far, values_far,
-    out, queries, fresh_rows, cache_keys, cache_values, sems,
+    columns, length, cosine, sine, arrived, cache, out, queries, fresh_rows
 ):
-    fetch_keys = pltpu.make_async_copy(keys_far, cache_keys, sems.at[0])
-    fetch_values = pltpu.make_async_copy(values_far, cache_values, sems.at[1])
-    fetch_keys.start()
-    fetch_values.start()
+    slots = cache.shape[0] // 2
     wide, steps, _ = arrived.shape
-    size = cache_keys.shape[1]
+    size = cache.shape[1]
     half = size // 2
     heads = columns // size
     cos, sin = cosine[...], sine[...]
@@ -278,9 +350,8 @@
     new_values = fresh_rows[1].astype(jnp.bfloat16)
     score_scale = 1.0 / size**0.5
     by_row = (((1,), (1,)), ((), ()))
-    fetch_keys.wait()
     scores = score_scale * lax.dot_general(
-        query, cache_keys[...], by_row, preferred_element_type=jnp.float32
+        query, cache[:slots, :], by_row, preferred_element_type=jnp.float32
     )
     fresh = score_scale * lax.dot_general(
         query, new_keys, by_row, preferred_element_type=jnp.float32
@@ -298,10 +369,9 @@
     share = 1.0 / (
         jnp.sum(weights, axis=1, keepdims=True) + jnp.sum(fresh_weights, axis=1, keepdims=True)
     )
-    fetch_values.wait()
     context = jnp.dot(
         (weights * share).astype(jnp.bfloat16),
-        cache_values[...],
+        cache[slots:, :],
         preferred_element_type=jnp.float32,
     ) + jnp.dot(
         (fresh_weights * share).astype(jnp.bfloat16),
@@ -315,27 +385,40 @@
         ].astype(jnp.bfloat16)
 
 
-def assemble_kernel(*refs):
-    *blocks, out, held = refs
-    steps = blocks[0].shape[0]
-    for k, block in enumerate(blocks):
-        held[k * steps : (k + 1) * steps, :] = block[...].astype(jnp.float32)
-    out[...] = held[...].astype(jnp.bfloat16)
-
-
-def output_kernel(steps, place, mine, theirs, w_out, out, result, ordered):
+def output_kernel(steps, place, w_out, early, *refs):
+    *blocks, out, joined, result, ordered, late, sems = refs
     wide_at, narrow_at = place[0], place[1]
-    count = mine.shape[0] // steps
-    batch = 2 * count
-    depth = w_out.shape[0] // 8
+    batch = len(blocks)
+    count = batch // 2
+    deep = early.shape[0]
+    piece = late.shape[0] // OUT_PIECES
+    stream = Stream(
+        [
+            pltpu.make_async_copy(
+                w_out.at[pl.ds(deep + at * piece, piece)],
+                late.at[pl.ds(at * piece, piece)],
+                sems.at[at],
+            )
+            for at in range(OUT_PIECES)
+        ]
+    )
+    depth = joined.shape[1]
     for at in range(0, w_out.shape[0], depth):
-        part = slice(at, at + depth)
-        rows = jnp.concatenate([mine[:, part], theirs[:, part]], axis=0)
-        product = jnp.dot(rows, w_out[part, :], preferred_element_type=jnp.float32)
+        for k, block in enumerate(blocks):
+            joined[k * steps : (k + 1) * steps, :] = block[:, at : at + depth].astype(jnp.float32)
+        rows = joined[...].astype(jnp.bfloat16)
+        if at < deep:
+            weights = early[at : at + depth, :]
+        else:
+            stream.take((at + depth - deep) // piece - 1)
+            weights = late[at - deep : at - deep + depth, :]
+        product = jnp.dot(rows, weights, preferred_element_type=jnp.float32)
         if at == 0:
             result[...] = product
         else:
             result[...] += product
+        if at + depth in (deep // 2, deep):
+            stream.take((at + depth) * 2 // deep - 1)
     for core in range(2):
         for k in range(count):
             sequence = jnp.bitwise_xor(narrow_at, core) * count + jnp.bitwise_xor(wide_at, k)
@@ -351,13 +434,26 @@
     return lax.ppermute(value, axis, [(at, at ^ bits) for at in range(size)])
 
 
-def gather_wide(block, count):
+def gather_tokens(block):
     near = {0: block}
-    for bits in range(2, count, 2):
+    for bits in (4, 2, 1):
         near[bits] = swap(block, "wide", bits)
-    for bits in range(0, count, 2):
+    near[1], near[2], near[4] = lax.optimization_barrier((near[1], near[2], near[4]))
+    near[6] = swap(near[4], "wide", 2)
+    near[5] = swap(near[4], "wide", 1)
+    near[3] = swap(near[2], "wide", 1)
+    near[7] = swap(near[5], "wide", 2)
+    return [near[k] for k in range(8)]
+
+
+def gather_contexts(block, loader):
+    near = {0: block}
+    for bits in (2, 4, 6, 1):
+        near[bits] = swap(block, "wide", bits)
+    near[4], near[6], held = lax.optimization_barrier((near[4], near[6], loader(near[2])))
+    for bits in (2, 4, 6):
         near[bits + 1] = swap(near[bits], "wide", 1)
-    return [near[k] for k in range(count)]
+    return [near[k] for k in range(8)], held
 
 
 def local_fast(tokens, norm_gain, w_query, w_keyval, w_out, cache_keys, cache_values, lengths):
@@ -370,28 +466,38 @@
     f32, bf16 = jnp.float32, jnp.bfloat16
     place = jnp.stack([lax.axis_index("wide"), lax.axis_index("narrow")]).astype(jnp.int32)
 
-    payload = jnp.concatenate(
-        [tokens.reshape(rows, width), norm_gain[None], jnp.zeros((7, width), bf16)]
-    )
-    blocks = gather_wide(payload, wide_count)
-    query_weights = load("load_query_weights", w_query, 0, 1, pieces=8)
-    sums = call(
-        functools.partial(stats_kernel, rows),
-        "row_sums",
-        jax.ShapeDtypeStruct((2 * rows, 128), f32),
-        blocks,
+    own = tokens.reshape(rows, width)
+    sums = call(sums_kernel, "row_sums", jax.ShapeDtypeStruct((8, 128), f32), [own])
+    payload = call(
+        payload_kernel,
+        "payload",
+        jax.ShapeDtypeStruct((width // 128 * rows + EXTRA, 128), bf16),
+        [own, norm_gain[None], sums, swap(sums, "narrow", 1)],
+        scratch=[pltpu.VMEM((EXTRA, 128), f32)],
+    )
+    blocks = gather_tokens(payload)
+    part = columns // 2
+    deep = w_query.shape[0]
+    early_weights = load(
+        "load_query_weights",
+        (deep, part),
+        boxes(pl.ds(0, deep), pl.ds(0, part), 8),
+        w_query,
     )
     keep, send = call(
         functools.partial(project_kernel, steps, width * wide_count * narrow_count),
         "norm_and_project",
         [jax.ShapeDtypeStruct((rows // 2, columns + tail), f32)] * 2,
-        [place, sums, swap(sums, "narrow", 1), in_hbm(w_keyval), query_weights, *blocks],
-        in_specs=[IN_SMEM, IN_VMEM, IN_VMEM, IN_HBM] + [IN_VMEM] * (wide_count + 1),
+        [place, in_hbm(w_keyval), in_hbm(w_query), early_weights, *blocks],
+        in_specs=[IN_SMEM, IN_HBM, IN_HBM] + [IN_VMEM] * (wide_count + 1),
         scratch=[
             pltpu.VMEM((rows, columns + tail), f32),
+            pltpu.VMEM((wide_count, rows, width), bf16),
+            pltpu.VMEM((deep, columns - part), bf16),
             pltpu.VMEM(w_keyval.shape, bf16),
-            pltpu.SemaphoreType.DMA,
+            pltpu.SemaphoreType.DMA((wide_count + 1,)),
         ],
+        limit=24 * MIB,
         flops=2 * rows * width * wide_count * columns,
     )
     outgoing = call(
@@ -402,8 +508,16 @@
         scratch=[pltpu.VMEM(((columns + 2 * tail) // 128, rows // 2, 128), f32)],
     )
     arrived = lax.all_to_all(outgoing, "wide", 0, 0, tiled=True)
-    keys = cache_keys.reshape(cache_keys.shape[1:])
-    values = cache_values.reshape(cache_values.shape[1:])
+    slots = cache_keys.shape[1]
+    cache = load(
+        "load_cache",
+        (2 * slots, size),
+        boxes(pl.ds(0, slots), pl.ds(0, size), 4)
+        + boxes(pl.ds(0, slots), pl.ds(0, size), 4, at_row=slots, source=1),
+        cache_keys.reshape(slots, size),
+        cache_values.reshape(slots, size),
+        after=[outgoing],
+    )
     ladder = jnp.arange(size // 2, dtype=f32)
     frequency = jnp.exp(ladder * (-2.0 / size) * jnp.log(10000.0))
     angles = (lengths + jnp.arange(steps)).astype(f32)[:, None] * frequency
@@ -411,34 +525,41 @@
         functools.partial(attend_kernel, columns),
         "attention",
         jax.ShapeDtypeStruct((steps, H * size), bf16),
-        [lengths, jnp.cos(angles), jnp.sin(angles), arrived, in_hbm(keys), in_hbm(values)],
-        in_specs=[IN_SMEM] + [IN_VMEM] * 3 + [IN_HBM] * 2,
+        [lengths, jnp.cos(angles), jnp.sin(angles), arrived, cache],
+        in_specs=[IN_SMEM] + [IN_VMEM] * 4,
         scratch=[
             pltpu.VMEM((steps * H, size), f32),
             pltpu.VMEM((2, 128, size), f32),
-            pltpu.VMEM(keys.shape, bf16),
-            pltpu.VMEM(values.shape, bf16),
-            pltpu.SemaphoreType.DMA((2,)),
         ],
         limit=16 * MIB,
-        flops=4 * steps * H * size * keys.shape[0],
-    )
-    contexts = gather_wide(context, wide_count)
-    out_weights = load("load_out_weights", w_out, 0, 1, pieces=8, after=[context])
-    mine = call(
-        assemble_kernel,
-        "join_contexts",
-        jax.ShapeDtypeStruct((wide_count * steps, H * size), bf16),
-        contexts,
-        scratch=[pltpu.VMEM((wide_count * steps, H * size), f32)],
-    )
+        flops=4 * steps * H * size * slots,
+    )
+    deep = w_out.shape[0] // 2
+    contexts, early_weights = gather_contexts(
+        context,
+        lambda block: load(
+            "load_out_weights",
+            (deep, w_out.shape[1]),
+            boxes(pl.ds(0, deep), pl.ds(0, w_out.shape[1]), 8),
+            w_out,
+            after=[block],
+        ),
+    )
+    contexts = contexts + [swap(block, "narrow", 1) for block in contexts]
     return call(
         functools.partial(output_kernel, steps),
         "project_out",
         jax.ShapeDtypeStruct((steps, batch, w_out.shape[1]), bf16),
-        [place, mine, swap(mine, "narrow", 1), out_weights],
-        in_specs=[IN_SMEM] + [IN_VMEM] * 3,
-        scratch=[pltpu.VMEM((rows, w_out.shape[1]), f32)] * 2,
+        [place, in_hbm(w_out), early_weights, *contexts],
+        in_specs=[IN_SMEM, IN_HBM] + [IN_VMEM] * (1 + batch),
+        scratch=[
+            pltpu.VMEM((rows, w_out.shape[0] // 8), f32),
+            pltpu.VMEM((rows, w_out.shape[1]), f32),
+            pltpu.VMEM((rows, w_out.shape[1]), f32),
+            pltpu.VMEM((w_out.shape[0] - deep, w_out.shape[1]), bf16),
+            pltpu.SemaphoreType.DMA((OUT_PIECES,)),
+        ],
+        limit=28 * MIB,
         flops=2 * rows * w_out.size,
     )
 
@@ -450,6 +571,8 @@
         and lax.axis_size("wide") == 8
         and tokens.shape[1] == 16
         and tokens.shape[2] % 128 == 0
+        and tokens.shape[2] // 128 + 6 <= EXTRA
+        and tokens.shape[0] * 16 <= 128
     )
     return (local_fast if fits else local_plain)(
         tokens, norm_gain, w_query, w_keyval, w_out, cache_keys, cache_values, lengths

time: 89.5 us -> 83.1 us (0.928)
  Pallas kernels: 36.3 us -> 32.5 us
  waiting for transfers between devices: 25.6 us -> 24.1 us
  other arithmetic: 1.21 us -> 0.2 us
  starting transfers between devices: 24.5 us -> 23.5 us
    pallas_call x8 -> x9, Pallas kernels: 36.3 us -> 32.5 us  [call(): pl.pallas_call(kernel, out_shape=out_shape, in_specs=in_specs or [IN_VMEM...]
    all_to_all x1, waiting for transfers between devices: 7.68 us -> 6.07 us  [local_fast(): arrived = lax.all_to_all(outgoing, 'wide', 0, 0, tiled=True)]
    concatenate x1 -> x0, other arithmetic: 1.01 us -> none  [local_fast(): jnp.concatenate([tokens.reshape(rows, width), norm_gain[None], jnp.zeros(...]
    unnamed x0 -> x2, local copies, waits for them, and re-layouts: none -> 0.91 us
    ppermute x17 -> x24, starting transfers between devices: 20 us -> 19.7 us  [swap(): return lax.ppermute(value, axis, [(at, at ^ bits) for at in range(size)])]
    ppermute x17 -> x24, waiting for transfers between devices: 17.9 us -> 18 us  [swap(): return lax.ppermute(value, axis, [(at, at ^ bits) for at in range(size)])]
  transfers between devices with their start and end apart: 18 -> 25, of which waited for: 8 -> 13; matrix products, arithmetic and copies ran while one was open for 0% -> 1% of each run, Pallas kernels for 21% -> 14%
where the time goes in v4:
time: 83.1 us; the launch traced here: 82.8 us
  Pallas kernels  32.5 us (39%)
  waiting for transfers between devices  24.1 us (29%)
  starting transfers between devices  23.5 us (28%)
  local copies, waits for them, and re-layouts  1.6 us (2%)
  between operations  0.93 us (1%)
    pallas_call x9, Pallas kernels, call(): pl.pallas_call(kernel, out_shape=out_shape, in_specs=in_specs or [IN_VMEM...  32.5 us
    ppermute x24, starting transfers between devices, swap(): return lax.ppermute(value, axis, [(at, at ^ bits) for at in range(size)])  19.7 us
    ppermute x24, waiting for transfers between devices, swap(): return lax.ppermute(value, axis, [(at, at ^ bits) for at in range(size)])  18 us
    all_to_all x1, waiting for transfers between devices, local_fast(): arrived = lax.all_to_all(outgoing, 'wide', 0, 0, tiled=True)  6.07 us
    all_to_all x1, starting transfers between devices, local_fast(): arrived = lax.all_to_all(outgoing, 'wide', 0, 0, tiled=True)  3.81 us
  transfers between devices with their start and end apart: 25, of which 13 were waited for; matrix products, arithmetic and copies ran while one was open for 1% of the time, Pallas kernels for 14%

profile of v4, /device:TPU:0, one launch (start us, length us, event | category | flops | bytes accessed | tf_op | source)
XLA Modules:
  0.0 82.8 jit_solution(5880250167056325262)
XLA Ops:
  0.0 0.0 copy-start
  0.0 0.9 %copy-done = bf16[4,16,1152]{2,1,0:T(8,128)(2,1)S(1)} copy-done((bf16[4,16,1152]{2,1,0:T(8,128)(2,1)S(1)}, bf16[4,16,1152]{2,1,0:T(8,128)(2,1)}, u32[]{:S(2)}) %copy-start) | copy-done | bytes 147480
  0.9 0.1 row_sums.1.mine
  1.0 0.5 collective-permute-start
  1.6 0.7 broadcast_in_dim.2.gain
  2.2 0.1 collective-permute-done.theirs
  2.4 2.9 %collective-permute-start.1 = (bf16[592,128]{1,0:T(8,128)(2,1)S(1)}, bf16[592,128]{1,0:T(8,128)(2,1)S(1)}, u32[]{:S(2)}, u32[]{:S(2)}) collective-permute-start(bf16[592,128]{1,0:T(8,128)(2,1)S(1)} %payload.1.refs_0_), channel_id=1, source_target_pairs={{0,2},{2,0},{4,6},{6,4},{8,10},{10,8},{12,14},{14,12},{1,3},{3,1},... | collective-permute-start | bytes 454664 | tf_op jit(solution)/shard_map/ppermute | solution.py:434
  5.3 1.6 %collective-permute-start.2 = (bf16[592,128]{1,0:T(8,128)(2,1)S(1)}, bf16[592,128]{1,0:T(8,128)(2,1)S(1)}, u32[]{:S(2)}, u32[]{:S(2)}) collective-permute-start(bf16[592,128]{1,0:T(8,128)(2,1)S(1)} %payload.1.refs_0_), channel_id=1, source_target_pairs={{0,4},{2,6},{4,0},{6,2},{8,12},{10,14},{12,8},{14,10},{1,5},{3,7},... | collective-permute-start | bytes 454664 | tf_op jit(solution)/shard_map/ppermute | solution.py:434
  6.9 2.6 %collective-permute-start.3 = (bf16[592,128]{1,0:T(8,128)(2,1)S(1)}, bf16[592,128]{1,0:T(8,128)(2,1)S(1)}, u32[]{:S(2)}, u32[]{:S(2)}) collective-permute-start(bf16[592,128]{1,0:T(8,128)(2,1)S(1)} %payload.1.refs_0_), channel_id=1, source_target_pairs={{0,8},{2,10},{4,12},{6,14},{8,0},{10,2},{12,4},{14,6},{1,9},{3,11}... | collective-permute-start | bytes 454664 | tf_op jit(solution)/shard_map/ppermute | solution.py:434
  9.5 0.1 collective-permute-done.1.refs_1_
  9.6 4.4 %collective-permute-done.2.refs_2_ = bf16[592,128]{1,0:T(8,128)(2,1)S(1)} collective-permute-done((bf16[592,128]{1,0:T(8,128)(2,1)S(1)}, bf16[592,128]{1,0:T(8,128)(2,1)S(1)}, u32[]{:S(2)}, u32[]{:S(2)}) %collective-permute-start.2) | collective-permute-done | bytes 151584 | tf_op jit(solution)/shard_map/ppermute | solution.py:434
  14.0 2.5 %collective-permute-done.3.refs_4_ = bf16[592,128]{1,0:T(8,128)(2,1)S(1)} collective-permute-done((bf16[592,128]{1,0:T(8,128)(2,1)S(1)}, bf16[592,128]{1,0:T(8,128)(2,1)S(1)}, u32[]{:S(2)}, u32[]{:S(2)}) %collective-permute-start.3) | collective-permute-done | bytes 151584 | tf_op jit(solution)/shard_map/ppermute | solution.py:434
  16.5 0.5 collective-permute-start.5
  17.1 0.4 collective-permute-start.6
  17.5 1.5 %collective-permute-start.4 = (bf16[592,128]{1,0:T(8,128)(2,1)S(1)}, bf16[592,128]{1,0:T(8,128)(2,1)S(1)}, u32[]{:S(2)}, u32[]{:S(2)}) collective-permute-start(bf16[592,128]{1,0:T(8,128)(2,1)S(1)} %collective-permute-done.2.refs_2_), channel_id=1, source_target_pairs={{0,2},{2,0},{4,6},{6,4},{8,10},{10,8},{12,14},{14,12},{1,3},{3,1},... | collective-permute-start | bytes 454664 | tf_op jit(solution)/shard_map/ppermute | solution.py:434
  19.0 2.7 %collective-permute-done.5.refs_5_ = bf16[592,128]{1,0:T(8,128)(2,1)S(1)} collective-permute-done((bf16[592,128]{1,0:T(8,128)(2,1)S(1)}, bf16[592,128]{1,0:T(8,128)(2,1)S(1)}, u32[]{:S(2)}, u32[]{:S(2)}) %collective-permute-start.5) | collective-permute-done | bytes 151584 | tf_op jit(solution)/shard_map/ppermute | solution.py:434
  21.8 1.7 %collective-permute-start.7 = (bf16[592,128]{1,0:T(8,128)(2,1)S(1)}, bf16[592,128]{1,0:T(8,128)(2,1)S(1)}, u32[]{:S(2)}, u32[]{:S(2)}) collective-permute-start(bf16[592,128]{1,0:T(8,128)(2,1)S(1)} %collective-permute-done.5.refs_5_), channel_id=1, source_target_pairs={{0,4},{2,6},{4,0},{6,2},{8,12},{10,14},{12,8},{14,10},{1,5},{3,7},... | collective-permute-start | bytes 454664 | tf_op jit(solution)/shard_map/ppermute | solution.py:434
  23.4 5.2 %load_query_weights.1.early = bf16[9216,768]{1,0:T(8,128)(2,1)S(1)} custom-call(bf16[9216,1536]{1,0:T(8,128)(2,1)} %w_query.1), custom_call_target="tpu_custom_call" | custom-call | bytes 14155776 | tf_op jit(solution)/shard_map/load_query_weights/pallas_call | solution.py:124
  28.6 0.1 pad_add_fusion.place
  28.7 0.0 collective-permute-done.6.refs_6_
  28.7 0.0 collective-permute-done.4.refs_3_
  28.7 0.0 collective-permute-done.7.refs_7_
  28.7 9.5 %norm_and_project.1 = (f32[32,2048]{1,0:T(8,128)S(1)}, f32[32,2048]{1,0:T(8,128)S(1)}) custom-call(s32[2]{0:T(128)S(1)} %pad_add_fusion.place, bf16[1152,512]{1,0:T(8,128)(2,1)} %w_keyval_far.1, bf16[9216,1536]{1,0:T(8,128)(2,1)} %w_query.1, bf16[9216,768]{1,0:T(8,128)(2,1)S(1)} %load_query_weights.1.early, bf16[592,128]{1,0:T(8,128)(2,1)S(1)} %payload.1.refs_0_, ...), custom_call_target="tpu_custom_call" | custom-call | flops 1811939328 | bytes 44859400 | tf_op jit(solution)/shard_map/norm_and_project/pallas_call | solution.py:124
  38.2 0.1 collective-permute-start.8
  38.9 0.9 %collective-permute-done.8.theirs = f32[32,2048]{1,0:T(8,128)S(1)} collective-permute-done((f32[32,2048]{1,0:T(8,128)S(1)}, f32[32,2048]{1,0:T(8,128)S(1)}, u32[]{:S(2)}, u32[]{:S(2)}) %collective-permute-start.8) | collective-permute-done | bytes 262176 | tf_op jit(solution)/shard_map/ppermute | solution.py:434
  39.8 0.8 sum_of_cores.1.refs_2_
  40.5 3.8 %all-to-all-start = ((bf16[8,4,2560]{2,1,0:T(4,128)(2,1)}), bf16[8,4,2560]{2,1,0:T(4,128)(2,1)S(1)}, u32[]{:S(2)}, u32[]{:S(2)}) async-start(bf16[8,4,2560]{2,1,0:T(4,128)(2,1)} %sum_of_cores.1.refs_2_), calls=%async_computation | async-start | bytes 327680 | tf_op jit(solution)/shard_map/all_to_all | solution.py:510
  44.4 0.1 multiply_sine_fusion
  44.5 1.6 %load_cache.1.cache = bf16[4096,256]{1,0:T(8,128)(2,1)S(1)} custom-call(bf16[2048,256]{1,0:T(8,128)(2,1)} %bitcast.9, bf16[2048,256]{1,0:T(8,128)(2,1)} %bitcast.10, bf16[8,4,2560]{2,1,0:T(4,128)(2,1)} %sum_of_cores.1.refs_2_), custom_call_target="tpu_custom_call" | custom-call | bytes 2097152 | tf_op jit(solution)/shard_map/load_cache/pallas_call | solution.py:124
  46.1 6.1 %all-to-all-done.arrived = bf16[8,4,2560]{2,1,0:T(4,128)(2,1)S(1)} async-done(((bf16[8,4,2560]{2,1,0:T(4,128)(2,1)}), bf16[8,4,2560]{2,1,0:T(4,128)(2,1)S(1)}, u32[]{:S(2)}, u32[]{:S(2)}) %all-to-all-start) | async-done | bytes 163872 | tf_op jit(solution)/shard_map/all_to_all | solution.py:510
  52.1 1.7 %attention.1.refs_0_ = bf16[4,12288]{1,0:T(4,128)(2,1)S(1)} custom-call(s32[1]{0:T(128)} %copy.9.length, f32[4,128]{1,0:T(4,128)S(1)} %get-tuple-element.22.cosine, f32[4,128]{1,0:T(4,128)S(1)} %get-tuple-element.21.sine, bf16[8,4,2560]{2,1,0:T(4,128)(2,1)S(1)} %all-to-all-done.arrived, bf16[4096,256]{1,0:T(8,128)(2,1)S(1)} %load_cache.1.cache), custom_call_target="tpu_custom_call" | custom-call | flops 402653184 | bytes 2265092 | tf_op jit(solution)/shard_map/attention/pallas_call | solution.py:124
  53.9 0.1 collective-permute-start.11
  53.9 2.0 %collective-permute-start.10 = (bf16[4,12288]{1,0:T(4,128)(2,1)S(1)}, bf16[4,12288]{1,0:T(4,128)(2,1)S(1)}, u32[]{:S(2)}, u32[]{:S(2)}) collective-permute-start(bf16[4,12288]{1,0:T(4,128)(2,1)S(1)} %attention.1.refs_0_), channel_id=1, source_target_pairs={{0,12},{2,14},{4,8},{6,10},{8,4},{10,6},{12,0},{14,2},{1,13},{3,15... | collective-permute-start | bytes 294920 | tf_op jit(solution)/shard_map/ppermute | solution.py:434
  55.9 1.5 %collective-permute-start.9 = (bf16[4,12288]{1,0:T(4,128)(2,1)S(1)}, bf16[4,12288]{1,0:T(4,128)(2,1)S(1)}, u32[]{:S(2)}, u32[]{:S(2)}) collective-permute-start(bf16[4,12288]{1,0:T(4,128)(2,1)S(1)} %attention.1.refs_0_), channel_id=1, source_target_pairs={{0,8},{2,10},{4,12},{6,14},{8,0},{10,2},{12,4},{14,6},{1,9},{3,11}... | collective-permute-start | bytes 294920 | tf_op jit(solution)/shard_map/ppermute | solution.py:434
  57.4 0.3 collective-permute-start.12
  57.7 0.0 collective-permute-start.16
  57.8 2.1 %collective-permute-done.11.refs_1_.refs_2_ = bf16[4,12288]{1,0:T(4,128)(2,1)S(1)} collective-permute-done((bf16[4,12288]{1,0:T(4,128)(2,1)S(1)}, bf16[4,12288]{1,0:T(4,128)(2,1)S(1)}, u32[]{:S(2)}, u32[]{:S(2)}) %collective-permute-start.11) | collective-permute-done | bytes 98336 | tf_op jit(solution)/shard_map/ppermute | solution.py:434
  59.9 5.2 %load_out_weights.1.early = bf16[6144,1152]{1,0:T(8,128)(2,1)S(1)} custom-call(bf16[12288,1152]{1,0:T(8,128)(2,1)} %w_out.1, bf16[4,12288]{1,0:T(4,128)(2,1)S(1)} %collective-permute-done.11.refs_1_.refs_2_), custom_call_target="tpu_custom_call" | custom-call | bytes 14155776 | tf_op jit(solution)/shard_map/load_out_weights/pallas_call | solution.py:124
  65.0 0.0 collective-permute-done.10.refs_6_
  65.0 0.0 collective-permute-done.9.refs_4_
  65.0 0.9 %collective-permute-start.14 = (bf16[4,12288]{1,0:T(4,128)(2,1)S(1)}, bf16[4,12288]{1,0:T(4,128)(2,1)S(1)}, u32[]{:S(2)}, u32[]{:S(2)}) collective-permute-start(bf16[4,12288]{1,0:T(4,128)(2,1)S(1)} %collective-permute-done.9.refs_4_), channel_id=1, source_target_pairs={{0,2},{2,0},{4,6},{6,4},{8,10},{10,8},{12,14},{14,12},{1,3},{3,1},... | collective-permute-start | bytes 294920 | tf_op jit(solution)/shard_map/ppermute | solution.py:434
  66.0 1.2 %collective-permute-start.15 = (bf16[4,12288]{1,0:T(4,128)(2,1)S(1)}, bf16[4,12288]{1,0:T(4,128)(2,1)S(1)}, u32[]{:S(2)}, u32[]{:S(2)}) collective-permute-start(bf16[4,12288]{1,0:T(4,128)(2,1)S(1)} %collective-permute-done.10.refs_6_), channel_id=1, source_target_pairs={{0,2},{2,0},{4,6},{6,4},{8,10},{10,8},{12,14},{14,12},{1,3},{3,1},... | collective-permute-start | bytes 294920 | tf_op jit(solution)/shard_map/ppermute | solution.py:434
  67.1 0.0 collective-permute-start.20
  67.1 0.0 collective-permute-done.12.refs_1_
  67.1 0.5 collective-permute-start.22
  67.6 0.0 collective-permute-done.16.refs_8_
  67.6 0.8 %collective-permute-start.13 = (bf16[4,12288]{1,0:T(4,128)(2,1)S(1)}, bf16[4,12288]{1,0:T(4,128)(2,1)S(1)}, u32[]{:S(2)}, u32[]{:S(2)}) collective-permute-start(bf16[4,12288]{1,0:T(4,128)(2,1)S(1)} %collective-permute-done.11.refs_1_.refs_2_), channel_id=1, source_target_pairs={{0,2},{2,0},{4,6},{6,4},{8,10},{10,8},{12,14},{14,12},{1,3},{3,1},... | collective-permute-start | bytes 294920 | tf_op jit(solution)/shard_map/ppermute | solution.py:434
  68.5 1.2 %collective-permute-done.14.refs_5_ = bf16[4,12288]{1,0:T(4,128)(2,1)S(1)} collective-permute-done((bf16[4,12288]{1,0:T(4,128)(2,1)S(1)}, bf16[4,12288]{1,0:T(4,128)(2,1)S(1)}, u32[]{:S(2)}, u32[]{:S(2)}) %collective-permute-start.14) | collective-permute-done | bytes 98336 | tf_op jit(solution)/shard_map/ppermute | solution.py:434
  69.7 0.0 collective-permute-start.18
  69.7 1.4 %collective-permute-done.15.refs_7_ = bf16[4,12288]{1,0:T(4,128)(2,1)S(1)} collective-permute-done((bf16[4,12288]{1,0:T(4,128)(2,1)S(1)}, bf16[4,12288]{1,0:T(4,128)(2,1)S(1)}, u32[]{:S(2)}, u32[]{:S(2)}) %collective-permute-start.15) | collective-permute-done | bytes 98336 | tf_op jit(solution)/shard_map/ppermute | solution.py:434
  71.2 0.0 collective-permute-start.17
  71.2 0.0 collective-permute-done.20.refs_12_
  71.2 0.5 collective-permute-start.21
  71.7 0.0 collective-permute-done.22.refs_14_
  71.7 0.1 collective-permute-start.23
  71.8 1.1 %collective-permute-done.13.refs_3_ = bf16[4,12288]{1,0:T(4,128)(2,1)S(1)} collective-permute-done((bf16[4,12288]{1,0:T(4,128)(2,1)S(1)}, bf16[4,12288]{1,0:T(4,128)(2,1)S(1)}, u32[]{:S(2)}, u32[]{:S(2)}) %collective-permute-start.13) | collective-permute-done | bytes 98336 | tf_op jit(solution)/shard_map/ppermute | solution.py:434
  72.9 0.0 collective-permute-start.19
  72.9 0.0 collective-permute-done.17.refs_9_
  72.9 0.0 collective-permute-done.18.refs_10_
  72.9 0.0 collective-permute-done.21.refs_13_
  72.9 0.1 collective-permute-done.23.refs_15_
  73.0 1.2 %collective-permute-done.19.refs_11_ = bf16[4,12288]{1,0:T(4,128)(2,1)S(1)} collective-permute-done((bf16[4,12288]{1,0:T(4,128)(2,1)S(1)}, bf16[4,12288]{1,0:T(4,128)(2,1)S(1)}, u32[]{:S(2)}, u32[]{:S(2)}) %collective-permute-start.19) | collective-permute-done | bytes 98336 | tf_op jit(solution)/shard_map/ppermute | solution.py:434
  74.2 8.5 %project_out.1 = bf16[4,16,1152]{2,1,0:T(8,128)(2,1)} custom-call(s32[2]{0:T(128)S(1)} %pad_add_fusion.place, bf16[12288,1152]{1,0:T(8,128)(2,1)} %w_out.1, bf16[6144,1152]{1,0:T(8,128)(2,1)S(1)} %load_out_weights.1.early, bf16[4,12288]{1,0:T(4,128)(2,1)S(1)} %attention.1.refs_0_, bf16[4,12288]{1,0:T(4,128)(2,1)S(1)} %collective-permute-done.12.refs_1_, ...), custom_call_target="tpu_custom_call" | custom-call | flops 1811939328 | bytes 44040200 | tf_op jit(solution)/shard_map/project_out/pallas_call | solution.py:124
  (3 shorter events, 0.1 us)
Async XLA Ops:
  0.0 0.9 %copy-start = (bf16[4,16,1152]{2,1,0:T(8,128)(2,1)S(1)}, bf16[4,16,1152]{2,1,0:T(8,128)(2,1)}, u32[]{:S(2)}) copy-start(bf16[4,16,1152]{2,1,0:T(8,128)(2,1)} %param.8) | copy-start | bytes 442372
  1.0 1.3 %collective-permute-start = (f32[8,128]{1,0:T(8,128)S(1)}, f32[8,128]{1,0:T(8,128)S(1)}, u32[]{:S(2)}, u32[]{:S(2)}) collective-permute-start(f32[8,128]{1,0:T(8,128)S(1)} %row_sums.1.mine), channel_id=1, source_target_pairs={{0,1},{1,0},{2,3},{3,2},{4,5},{5,4},{6,7},{7,6},{8,9},{9,8},{10,11... | collective-permute-start | bytes 12296 | tf_op jit(solution)/shard_map/ppermute | solution.py:434
  2.4 7.2 %collective-permute-start.1 = (bf16[592,128]{1,0:T(8,128)(2,1)S(1)}, bf16[592,128]{1,0:T(8,128)(2,1)S(1)}, u32[]{:S(2)}, u32[]{:S(2)}) collective-permute-start(bf16[592,128]{1,0:T(8,128)(2,1)S(1)} %payload.1.refs_0_), channel_id=1, source_target_pairs={{0,2},{2,0},{4,6},{6,4},{8,10},{10,8},{12,14},{14,12},{1,3},{3,1},... | collective-permute-start | bytes 454664 | tf_op jit(solution)/shard_map/ppermute | solution.py:434
  5.3 8.7 %collective-permute-start.2 = (bf16[592,128]{1,0:T(8,128)(2,1)S(1)}, bf16[592,128]{1,0:T(8,128)(2,1)S(1)}, u32[]{:S(2)}, u32[]{:S(2)}) collective-permute-start(bf16[592,128]{1,0:T(8,128)(2,1)S(1)} %payload.1.refs_0_), channel_id=1, source_target_pairs={{0,4},{2,6},{4,0},{6,2},{8,12},{10,14},{12,8},{14,10},{1,5},{3,7},... | collective-permute-start | bytes 454664 | tf_op jit(solution)/shard_map/ppermute | solution.py:434
  6.9 9.6 %collective-permute-start.3 = (bf16[592,128]{1,0:T(8,128)(2,1)S(1)}, bf16[592,128]{1,0:T(8,128)(2,1)S(1)}, u32[]{:S(2)}, u32[]{:S(2)}) collective-permute-start(bf16[592,128]{1,0:T(8,128)(2,1)S(1)} %payload.1.refs_0_), channel_id=1, source_target_pairs={{0,8},{2,10},{4,12},{6,14},{8,0},{10,2},{12,4},{14,6},{1,9},{3,11}... | collective-permute-start | bytes 454664 | tf_op jit(solution)/shard_map/ppermute | solution.py:434
  16.5 5.2 %collective-permute-start.5 = (bf16[592,128]{1,0:T(8,128)(2,1)S(1)}, bf16[592,128]{1,0:T(8,128)(2,1)S(1)}, u32[]{:S(2)}, u32[]{:S(2)}) collective-permute-start(bf16[592,128]{1,0:T(8,128)(2,1)S(1)} %collective-permute-done.3.refs_4_), channel_id=1, source_target_pairs={{0,2},{2,0},{4,6},{6,4},{8,10},{10,8},{12,14},{14,12},{1,3},{3,1},... | collective-permute-start | bytes 454664 | tf_op jit(solution)/shard_map/ppermute | solution.py:434
  17.1 11.6 %collective-permute-start.6 = (bf16[592,128]{1,0:T(8,128)(2,1)S(1)}, bf16[592,128]{1,0:T(8,128)(2,1)S(1)}, u32[]{:S(2)}, u32[]{:S(2)}) collective-permute-start(bf16[592,128]{1,0:T(8,128)(2,1)S(1)} %collective-permute-done.3.refs_4_), channel_id=1, source_target_pairs={{0,4},{2,6},{4,0},{6,2},{8,12},{10,14},{12,8},{14,10},{1,5},{3,7},... | collective-permute-start | bytes 454664 | tf_op jit(solution)/shard_map/ppermute | solution.py:434
  17.5 11.1 %collective-permute-start.4 = (bf16[592,128]{1,0:T(8,128)(2,1)S(1)}, bf16[592,128]{1,0:T(8,128)(2,1)S(1)}, u32[]{:S(2)}, u32[]{:S(2)}) collective-permute-start(bf16[592,128]{1,0:T(8,128)(2,1)S(1)} %collective-permute-done.2.refs_2_), channel_id=1, source_target_pairs={{0,2},{2,0},{4,6},{6,4},{8,10},{10,8},{12,14},{14,12},{1,3},{3,1},... | collective-permute-start | bytes 454664 | tf_op jit(solution)/shard_map/ppermute | solution.py:434
  21.8 6.9 %collective-permute-start.7 = (bf16[592,128]{1,0:T(8,128)(2,1)S(1)}, bf16[592,128]{1,0:T(8,128)(2,1)S(1)}, u32[]{:S(2)}, u32[]{:S(2)}) collective-permute-start(bf16[592,128]{1,0:T(8,128)(2,1)S(1)} %collective-permute-done.5.refs_5_), channel_id=1, source_target_pairs={{0,4},{2,6},{4,0},{6,2},{8,12},{10,14},{12,8},{14,10},{1,5},{3,7},... | collective-permute-start | bytes 454664 | tf_op jit(solution)/shard_map/ppermute | solution.py:434
  38.2 1.6 %collective-permute-start.8 = (f32[32,2048]{1,0:T(8,128)S(1)}, f32[32,2048]{1,0:T(8,128)S(1)}, u32[]{:S(2)}, u32[]{:S(2)}) collective-permute-start(f32[32,2048]{1,0:T(8,128)S(1)} %get-tuple-element.17), channel_id=1, source_target_pairs={{0,1},{1,0},{2,3},{3,2},{4,5},{5,4},{6,7},{7,6},{8,9},{9,8},{10,11... | collective-permute-start | bytes 786440 | tf_op jit(solution)/shard_map/ppermute | solution.py:434
  40.5 11.6 %all-to-all-start = ((bf16[8,4,2560]{2,1,0:T(4,128)(2,1)}), bf16[8,4,2560]{2,1,0:T(4,128)(2,1)S(1)}, u32[]{:S(2)}, u32[]{:S(2)}) async-start(bf16[8,4,2560]{2,1,0:T(4,128)(2,1)} %sum_of_cores.1.refs_2_), calls=%async_computation | async-start | bytes 327680 | tf_op jit(solution)/shard_map/all_to_all | solution.py:510
  53.9 6.0 %collective-permute-start.11 = (bf16[4,12288]{1,0:T(4,128)(2,1)S(1)}, bf16[4,12288]{1,0:T(4,128)(2,1)S(1)}, u32[]{:S(2)}, u32[]{:S(2)}) collective-permute-start(bf16[4,12288]{1,0:T(4,128)(2,1)S(1)} %attention.1.refs_0_), channel_id=1, source_target_pairs={{0,4},{2,6},{4,0},{6,2},{8,12},{10,14},{12,8},{14,10},{1,5},{3,7},... | collective-permute-start | bytes 294920 | tf_op jit(solution)/shard_map/ppermute | solution.py:434
  53.9 11.1 %collective-permute-start.10 = (bf16[4,12288]{1,0:T(4,128)(2,1)S(1)}, bf16[4,12288]{1,0:T(4,128)(2,1)S(1)}, u32[]{:S(2)}, u32[]{:S(2)}) collective-permute-start(bf16[4,12288]{1,0:T(4,128)(2,1)S(1)} %attention.1.refs_0_), channel_id=1, source_target_pairs={{0,12},{2,14},{4,8},{6,10},{8,4},{10,6},{12,0},{14,2},{1,13},{3,15... | collective-permute-start | bytes 294920 | tf_op jit(solution)/shard_map/ppermute | solution.py:434
  55.9 9.1 %collective-permute-start.9 = (bf16[4,12288]{1,0:T(4,128)(2,1)S(1)}, bf16[4,12288]{1,0:T(4,128)(2,1)S(1)}, u32[]{:S(2)}, u32[]{:S(2)}) collective-permute-start(bf16[4,12288]{1,0:T(4,128)(2,1)S(1)} %attention.1.refs_0_), channel_id=1, source_target_pairs={{0,8},{2,10},{4,12},{6,14},{8,0},{10,2},{12,4},{14,6},{1,9},{3,11}... | collective-permute-start | bytes 294920 | tf_op jit(solution)/shard_map/ppermute | solution.py:434
  57.4 9.7 %collective-permute-start.12 = (bf16[4,12288]{1,0:T(4,128)(2,1)S(1)}, bf16[4,12288]{1,0:T(4,128)(2,1)S(1)}, u32[]{:S(2)}, u32[]{:S(2)}) collective-permute-start(bf16[4,12288]{1,0:T(4,128)(2,1)S(1)} %attention.1.refs_0_), channel_id=1, source_target_pairs={{0,2},{2,0},{4,6},{6,4},{8,10},{10,8},{12,14},{14,12},{1,3},{3,1},... | collective-permute-start | bytes 294920 | tf_op jit(solution)/shard_map/ppermute | solution.py:434
  57.7 9.9 %collective-permute-start.16 = (bf16[4,12288]{1,0:T(4,128)(2,1)S(1)}, bf16[4,12288]{1,0:T(4,128)(2,1)S(1)}, u32[]{:S(2)}, u32[]{:S(2)}) collective-permute-start(bf16[4,12288]{1,0:T(4,128)(2,1)S(1)} %attention.1.refs_0_), channel_id=1, source_target_pairs={{0,1},{1,0},{2,3},{3,2},{4,5},{5,4},{6,7},{7,6},{8,9},{9,8},{10,11... | collective-permute-start | bytes 294920 | tf_op jit(solution)/shard_map/ppermute | solution.py:434
  65.0 4.7 %collective-permute-start.14 = (bf16[4,12288]{1,0:T(4,128)(2,1)S(1)}, bf16[4,12288]{1,0:T(4,128)(2,1)S(1)}, u32[]{:S(2)}, u32[]{:S(2)}) collective-permute-start(bf16[4,12288]{1,0:T(4,128)(2,1)S(1)} %collective-permute-done.9.refs_4_), channel_id=1, source_target_pairs={{0,2},{2,0},{4,6},{6,4},{8,10},{10,8},{12,14},{14,12},{1,3},{3,1},... | collective-permute-start | bytes 294920 | tf_op jit(solution)/shard_map/ppermute | solution.py:434
  66.0 5.2 %collective-permute-start.15 = (bf16[4,12288]{1,0:T(4,128)(2,1)S(1)}, bf16[4,12288]{1,0:T(4,128)(2,1)S(1)}, u32[]{:S(2)}, u32[]{:S(2)}) collective-permute-start(bf16[4,12288]{1,0:T(4,128)(2,1)S(1)} %collective-permute-done.10.refs_6_), channel_id=1, source_target_pairs={{0,2},{2,0},{4,6},{6,4},{8,10},{10,8},{12,14},{14,12},{1,3},{3,1},... | collective-permute-start | bytes 294920 | tf_op jit(solution)/shard_map/ppermute | solution.py:434
  67.1 4.0 %collective-permute-start.20 = (bf16[4,12288]{1,0:T(4,128)(2,1)S(1)}, bf16[4,12288]{1,0:T(4,128)(2,1)S(1)}, u32[]{:S(2)}, u32[]{:S(2)}) collective-permute-start(bf16[4,12288]{1,0:T(4,128)(2,1)S(1)} %collective-permute-done.9.refs_4_), channel_id=1, source_target_pairs={{0,1},{1,0},{2,3},{3,2},{4,5},{5,4},{6,7},{7,6},{8,9},{9,8},{10,11... | collective-permute-start | bytes 294920 | tf_op jit(solution)/shard_map/ppermute | solution.py:434
  67.1 4.5 %collective-permute-start.22 = (bf16[4,12288]{1,0:T(4,128)(2,1)S(1)}, bf16[4,12288]{1,0:T(4,128)(2,1)S(1)}, u32[]{:S(2)}, u32[]{:S(2)}) collective-permute-start(bf16[4,12288]{1,0:T(4,128)(2,1)S(1)} %collective-permute-done.10.refs_6_), channel_id=1, source_target_pairs={{0,1},{1,0},{2,3},{3,2},{4,5},{5,4},{6,7},{7,6},{8,9},{9,8},{10,11... | collective-permute-start | bytes 294920 | tf_op jit(solution)/shard_map/ppermute | solution.py:434
  67.6 5.2 %collective-permute-start.13 = (bf16[4,12288]{1,0:T(4,128)(2,1)S(1)}, bf16[4,12288]{1,0:T(4,128)(2,1)S(1)}, u32[]{:S(2)}, u32[]{:S(2)}) collective-permute-start(bf16[4,12288]{1,0:T(4,128)(2,1)S(1)} %collective-permute-done.11.refs_1_.refs_2_), channel_id=1, source_target_pairs={{0,2},{2,0},{4,6},{6,4},{8,10},{10,8},{12,14},{14,12},{1,3},{3,1},... | collective-permute-start | bytes 294920 | tf_op jit(solution)/shard_map/ppermute | solution.py:434
  69.7 3.2 %collective-permute-start.18 = (bf16[4,12288]{1,0:T(4,128)(2,1)S(1)}, bf16[4,12288]{1,0:T(4,128)(2,1)S(1)}, u32[]{:S(2)}, u32[]{:S(2)}) collective-permute-start(bf16[4,12288]{1,0:T(4,128)(2,1)S(1)} %collective-permute-done.11.refs_1_.refs_2_), channel_id=1, source_target_pairs={{0,1},{1,0},{2,3},{3,2},{4,5},{5,4},{6,7},{7,6},{8,9},{9,8},{10,11... | collective-permute-start | bytes 294920 | tf_op jit(solution)/shard_map/ppermute | solution.py:434
  71.2 1.7 %collective-permute-start.17 = (bf16[4,12288]{1,0:T(4,128)(2,1)S(1)}, bf16[4,12288]{1,0:T(4,128)(2,1)S(1)}, u32[]{:S(2)}, u32[]{:S(2)}) collective-permute-start(bf16[4,12288]{1,0:T(4,128)(2,1)S(1)} %collective-permute-done.12.refs_1_), channel_id=1, source_target_pairs={{0,1},{1,0},{2,3},{3,2},{4,5},{5,4},{6,7},{7,6},{8,9},{9,8},{10,11... | collective-permute-start | bytes 294920 | tf_op jit(solution)/shard_map/ppermute | solution.py:434
  71.2 1.7 %collective-permute-start.21 = (bf16[4,12288]{1,0:T(4,128)(2,1)S(1)}, bf16[4,12288]{1,0:T(4,128)(2,1)S(1)}, u32[]{:S(2)}, u32[]{:S(2)}) collective-permute-start(bf16[4,12288]{1,0:T(4,128)(2,1)S(1)} %collective-permute-done.14.refs_5_), channel_id=1, source_target_pairs={{0,1},{1,0},{2,3},{3,2},{4,5},{5,4},{6,7},{7,6},{8,9},{9,8},{10,11... | collective-permute-start | bytes 294920 | tf_op jit(solution)/shard_map/ppermute | solution.py:434
  71.7 1.3 %collective-permute-start.23 = (bf16[4,12288]{1,0:T(4,128)(2,1)S(1)}, bf16[4,12288]{1,0:T(4,128)(2,1)S(1)}, u32[]{:S(2)}, u32[]{:S(2)}) collective-permute-start(bf16[4,12288]{1,0:T(4,128)(2,1)S(1)} %collective-permute-done.15.refs_7_), channel_id=1, source_target_pairs={{0,1},{1,0},{2,3},{3,2},{4,5},{5,4},{6,7},{7,6},{8,9},{9,8},{10,11... | collective-permute-start | bytes 294920 | tf_op jit(solution)/shard_map/ppermute | solution.py:434
  72.9 1.3 %collective-permute-start.19 = (bf16[4,12288]{1,0:T(4,128)(2,1)S(1)}, bf16[4,12288]{1,0:T(4,128)(2,1)S(1)}, u32[]{:S(2)}, u32[]{:S(2)}) collective-permute-start(bf16[4,12288]{1,0:T(4,128)(2,1)S(1)} %collective-permute-done.13.refs_3_), channel_id=1, source_target_pairs={{0,1},{1,0},{2,3},{3,2},{4,5},{5,4},{6,7},{7,6},{8,9},{9,8},{10,11... | collective-permute-start | bytes 294920 | tf_op jit(solution)/shard_map/ppermute | solution.py:434

commit v5 on v4

--- a/solution.py
+++ b/solution.py
@@ -213,7 +213,7 @@
 
 
 class Stream:
-    def __init__(self, copies, flight=3):
+    def __init__(self, copies, flight=5):
         self.copies, self.started, self.done = copies, 0, 0
         self.start(flight)
 
@@ -385,40 +385,42 @@
         ].astype(jnp.bfloat16)
 
 
-def output_kernel(steps, place, w_out, early, *refs):
+def output_kernel(steps, place, w_out, *refs):
     *blocks, out, joined, result, ordered, late, sems = refs
+    parts, blocks = [*blocks[:2], late], blocks[2:]
     wide_at, narrow_at = place[0], place[1]
     batch = len(blocks)
     count = batch // 2
-    deep = early.shape[0]
-    piece = late.shape[0] // OUT_PIECES
+    deep, depth = late.shape[0], joined.shape[1]
+    piece = deep // OUT_PIECES
     stream = Stream(
         [
             pltpu.make_async_copy(
-                w_out.at[pl.ds(deep + at * piece, piece)],
+                w_out.at[pl.ds(2 * deep + at * piece, piece)],
                 late.at[pl.ds(at * piece, piece)],
                 sems.at[at],
             )
             for at in range(OUT_PIECES)
         ]
     )
-    depth = joined.shape[1]
-    for at in range(0, w_out.shape[0], depth):
+    for at in range(0, 3 * deep, depth):
         for k, block in enumerate(blocks):
             joined[k * steps : (k + 1) * steps, :] = block[:, at : at + depth].astype(jnp.float32)
         rows = joined[...].astype(jnp.bfloat16)
-        if at < deep:
-            weights = early[at : at + depth, :]
-        else:
-            stream.take((at + depth - deep) // piece - 1)
-            weights = late[at - deep : at - deep + depth, :]
-        product = jnp.dot(rows, weights, preferred_element_type=jnp.float32)
+        inside = at % deep
+        if at >= 2 * deep:
+            stream.take((inside + depth) // piece - 1)
+        product = jnp.dot(
+            rows,
+            parts[at // deep][inside : inside + depth, :],
+            preferred_element_type=jnp.float32,
+        )
         if at == 0:
             result[...] = product
         else:
             result[...] += product
-        if at + depth in (deep // 2, deep):
-            stream.take((at + depth) * 2 // deep - 1)
+        if at in (3 * depth, 5 * depth, 7 * depth):
+            stream.take(at // depth // 2 - 1)
     for core in range(2):
         for k in range(count):
             sequence = jnp.bitwise_xor(narrow_at, core) * count + jnp.bitwise_xor(wide_at, k)
@@ -448,12 +450,19 @@
 
 def gather_contexts(block, loader):
     near = {0: block}
-    for bits in (2, 4, 6, 1):
+    for bits in (4, 2, 1):
         near[bits] = swap(block, "wide", bits)
-    near[4], near[6], held = lax.optimization_barrier((near[4], near[6], loader(near[2])))
-    for bits in (2, 4, 6):
-        near[bits + 1] = swap(near[bits], "wide", 1)
-    return [near[k] for k in range(8)], held
+    first = loader(0, block)
+    near[1], near[2], near[4], first = lax.optimization_barrier((near[1], near[2], near[4], first))
+    near[6] = swap(near[4], "wide", 2)
+    near[5] = swap(near[4], "wide", 1)
+    near[3] = swap(near[2], "wide", 1)
+    near[7] = swap(near[5], "wide", 2)
+    second = loader(1, near[4])
+    near[3], near[6], near[7], second = lax.optimization_barrier(
+        (near[3], near[6], near[7], second)
+    )
+    return [near[k] for k in range(8)], [first, second]
 
 
 def local_fast(tokens, norm_gain, w_query, w_keyval, w_out, cache_keys, cache_values, lengths):
@@ -476,7 +485,7 @@
         scratch=[pltpu.VMEM((EXTRA, 128), f32)],
     )
     blocks = gather_tokens(payload)
-    part = columns // 2
+    part = columns // 3 * 2
     deep = w_query.shape[0]
     early_weights = load(
         "load_query_weights",
@@ -534,13 +543,13 @@
         limit=16 * MIB,
         flops=4 * steps * H * size * slots,
     )
-    deep = w_out.shape[0] // 2
+    deep = w_out.shape[0] // 3
     contexts, early_weights = gather_contexts(
         context,
-        lambda block: load(
+        lambda at, block: load(
             "load_out_weights",
             (deep, w_out.shape[1]),
-            boxes(pl.ds(0, deep), pl.ds(0, w_out.shape[1]), 8),
+            boxes(pl.ds(at * deep, deep), pl.ds(0, w_out.shape[1]), 8),
             w_out,
             after=[block],
         ),
@@ -550,13 +559,13 @@
         functools.partial(output_kernel, steps),
         "project_out",
         jax.ShapeDtypeStruct((steps, batch, w_out.shape[1]), bf16),
-        [place, in_hbm(w_out), early_weights, *contexts],
-        in_specs=[IN_SMEM, IN_HBM] + [IN_VMEM] * (1 + batch),
+        [place, in_hbm(w_out), *early_weights, *contexts],
+        in_specs=[IN_SMEM, IN_HBM] + [IN_VMEM] * (2 + batch),
         scratch=[
-            pltpu.VMEM((rows, w_out.shape[0] // 8), f32),
+            pltpu.VMEM((rows, deep // 4), f32),
             pltpu.VMEM((rows, w_out.shape[1]), f32),
             pltpu.VMEM((rows, w_out.shape[1]), f32),
-            pltpu.VMEM((w_out.shape[0] - deep, w_out.shape[1]), bf16),
+            pltpu.VMEM((deep, w_out.shape[1]), bf16),
             pltpu.SemaphoreType.DMA((OUT_PIECES,)),
         ],
         limit=28 * MIB,

time: 83.1 us -> 79.4 us (0.955)
  waiting for transfers between devices: 24.1 us -> 19.5 us
  starting transfers between devices: 23.5 us -> 24.4 us
    ppermute x24, waiting for transfers between devices: 18 us -> 13.5 us  [swap(): return lax.ppermute(value, axis, [(at, at ^ bits) for at in range(size)])]
    ppermute x24, starting transfers between devices: 19.7 us -> 20.6 us  [swap(): return lax.ppermute(value, axis, [(at, at ^ bits) for at in range(size)])]
    pallas_call x9 -> x10, Pallas kernels: 32.5 us -> 32.6 us  [call(): pl.pallas_call(kernel, out_shape=out_shape, in_specs=in_specs or [IN_VMEM...]
  transfers between devices with their start and end apart: 25 -> 25, of which waited for: 13 -> 12; matrix products, arithmetic and copies ran while one was open for 1% -> 1% of each run, Pallas kernels for 14% -> 20%
where the time goes in v5:
time: 79.4 us; the launch traced here: 79.1 us
  Pallas kernels  32.6 us (41%)
  starting transfers between devices  24.4 us (31%)
  waiting for transfers between devices  19.5 us (25%)
  local copies, waits for them, and re-layouts  1.6 us (2%)
    pallas_call x10, Pallas kernels, call(): pl.pallas_call(kernel, out_shape=out_shape, in_specs=in_specs or [IN_VMEM...  32.6 us
    ppermute x24, starting transfers between devices, swap(): return lax.ppermute(value, axis, [(at, at ^ bits) for at in range(size)])  20.6 us
    ppermute x24, waiting for transfers between devices, swap(): return lax.ppermute(value, axis, [(at, at ^ bits) for at in range(size)])  13.5 us
    all_to_all x1, waiting for transfers between devices, local_fast(): arrived = lax.all_to_all(outgoing, 'wide', 0, 0, tiled=True)  6.07 us
    all_to_all x1, starting transfers between devices, local_fast(): arrived = lax.all_to_all(outgoing, 'wide', 0, 0, tiled=True)  3.81 us
  transfers between devices with their start and end apart: 25, of which 12 were waited for; matrix products, arithmetic and copies ran while one was open for 1% of the time, Pallas kernels for 20%

profile of v5, /device:TPU:0, one launch (start us, length us, event | category | flops | bytes accessed | tf_op | source)
XLA Modules:
  0.0 79.1 jit_solution(16324530617109991694)
XLA Ops:
  0.0 0.0 copy-start
  0.0 0.9 %copy-done = bf16[4,16,1152]{2,1,0:T(8,128)(2,1)S(1)} copy-done((bf16[4,16,1152]{2,1,0:T(8,128)(2,1)S(1)}, bf16[4,16,1152]{2,1,0:T(8,128)(2,1)}, u32[]{:S(2)}) %copy-start) | copy-done | bytes 147480
  0.9 0.1 row_sums.1.mine
  1.0 0.5 collective-permute-start
  1.6 0.7 broadcast_in_dim.2.gain
  2.2 0.1 collective-permute-done.theirs
  2.4 2.9 %collective-permute-start.1 = (bf16[592,128]{1,0:T(8,128)(2,1)S(1)}, bf16[592,128]{1,0:T(8,128)(2,1)S(1)}, u32[]{:S(2)}, u32[]{:S(2)}) collective-permute-start(bf16[592,128]{1,0:T(8,128)(2,1)S(1)} %payload.1.refs_0_), channel_id=1, source_target_pairs={{0,2},{2,0},{4,6},{6,4},{8,10},{10,8},{12,14},{14,12},{1,3},{3,1},... | collective-permute-start | bytes 454664 | tf_op jit(solution)/shard_map/ppermute | solution.py:436
  5.3 1.6 %collective-permute-start.2 = (bf16[592,128]{1,0:T(8,128)(2,1)S(1)}, bf16[592,128]{1,0:T(8,128)(2,1)S(1)}, u32[]{:S(2)}, u32[]{:S(2)}) collective-permute-start(bf16[592,128]{1,0:T(8,128)(2,1)S(1)} %payload.1.refs_0_), channel_id=1, source_target_pairs={{0,4},{2,6},{4,0},{6,2},{8,12},{10,14},{12,8},{14,10},{1,5},{3,7},... | collective-permute-start | bytes 454664 | tf_op jit(solution)/shard_map/ppermute | solution.py:436
  6.9 2.6 %collective-permute-start.3 = (bf16[592,128]{1,0:T(8,128)(2,1)S(1)}, bf16[592,128]{1,0:T(8,128)(2,1)S(1)}, u32[]{:S(2)}, u32[]{:S(2)}) collective-permute-start(bf16[592,128]{1,0:T(8,128)(2,1)S(1)} %payload.1.refs_0_), channel_id=1, source_target_pairs={{0,8},{2,10},{4,12},{6,14},{8,0},{10,2},{12,4},{14,6},{1,9},{3,11}... | collective-permute-start | bytes 454664 | tf_op jit(solution)/shard_map/ppermute | solution.py:436
  9.5 0.1 collective-permute-done.1.refs_1_
  9.6 4.4 %collective-permute-done.2.refs_2_ = bf16[592,128]{1,0:T(8,128)(2,1)S(1)} collective-permute-done((bf16[592,128]{1,0:T(8,128)(2,1)S(1)}, bf16[592,128]{1,0:T(8,128)(2,1)S(1)}, u32[]{:S(2)}, u32[]{:S(2)}) %collective-permute-start.2) | collective-permute-done | bytes 151584 | tf_op jit(solution)/shard_map/ppermute | solution.py:436
  14.0 2.5 %collective-permute-done.3.refs_4_ = bf16[592,128]{1,0:T(8,128)(2,1)S(1)} collective-permute-done((bf16[592,128]{1,0:T(8,128)(2,1)S(1)}, bf16[592,128]{1,0:T(8,128)(2,1)S(1)}, u32[]{:S(2)}, u32[]{:S(2)}) %collective-permute-start.3) | collective-permute-done | bytes 151584 | tf_op jit(solution)/shard_map/ppermute | solution.py:436
  16.5 0.5 collective-permute-start.5
  17.1 0.4 collective-permute-start.6
  17.5 1.5 %collective-permute-start.4 = (bf16[592,128]{1,0:T(8,128)(2,1)S(1)}, bf16[592,128]{1,0:T(8,128)(2,1)S(1)}, u32[]{:S(2)}, u32[]{:S(2)}) collective-permute-start(bf16[592,128]{1,0:T(8,128)(2,1)S(1)} %collective-permute-done.2.refs_2_), channel_id=1, source_target_pairs={{0,2},{2,0},{4,6},{6,4},{8,10},{10,8},{12,14},{14,12},{1,3},{3,1},... | collective-permute-start | bytes 454664 | tf_op jit(solution)/shard_map/ppermute | solution.py:436
  19.0 2.7 %collective-permute-done.5.refs_5_ = bf16[592,128]{1,0:T(8,128)(2,1)S(1)} collective-permute-done((bf16[592,128]{1,0:T(8,128)(2,1)S(1)}, bf16[592,128]{1,0:T(8,128)(2,1)S(1)}, u32[]{:S(2)}, u32[]{:S(2)}) %collective-permute-start.5) | collective-permute-done | bytes 151584 | tf_op jit(solution)/shard_map/ppermute | solution.py:436
  21.8 1.7 %collective-permute-start.7 = (bf16[592,128]{1,0:T(8,128)(2,1)S(1)}, bf16[592,128]{1,0:T(8,128)(2,1)S(1)}, u32[]{:S(2)}, u32[]{:S(2)}) collective-permute-start(bf16[592,128]{1,0:T(8,128)(2,1)S(1)} %collective-permute-done.5.refs_5_), channel_id=1, source_target_pairs={{0,4},{2,6},{4,0},{6,2},{8,12},{10,14},{12,8},{14,10},{1,5},{3,7},... | collective-permute-start | bytes 454664 | tf_op jit(solution)/shard_map/ppermute | solution.py:436
  23.4 6.6 %load_query_weights.1.early = bf16[9216,1024]{1,0:T(8,128)(2,1)S(1)} custom-call(bf16[9216,1536]{1,0:T(8,128)(2,1)} %w_query.1), custom_call_target="tpu_custom_call" | custom-call | bytes 18874368 | tf_op jit(solution)/shard_map/load_query_weights/pallas_call | solution.py:124
  30.1 0.1 pad_add_fusion.place
  30.1 0.0 collective-permute-done.6.refs_6_
  30.1 0.0 collective-permute-done.4.refs_3_
  30.1 0.0 collective-permute-done.7.refs_7_
  30.1 6.8 %norm_and_project.1 = (f32[32,2048]{1,0:T(8,128)S(1)}, f32[32,2048]{1,0:T(8,128)S(1)}) custom-call(s32[2]{0:T(128)S(1)} %pad_add_fusion.place, bf16[1152,512]{1,0:T(8,128)(2,1)} %w_keyval_far.1, bf16[9216,1536]{1,0:T(8,128)(2,1)} %w_query.1, bf16[9216,1024]{1,0:T(8,128)(2,1)S(1)} %load_query_weights.1.early, bf16[592,128]{1,0:T(8,128)(2,1)S(1)} %payload.1.refs_0_, ...), custom_call_target="tpu_custom_call" | custom-call | flops 1811939328 | bytes 49577992 | tf_op jit(solution)/shard_map/norm_and_project/pallas_call | solution.py:124
  36.9 0.1 collective-permute-start.8
  37.7 0.9 %collective-permute-done.8.theirs = f32[32,2048]{1,0:T(8,128)S(1)} collective-permute-done((f32[32,2048]{1,0:T(8,128)S(1)}, f32[32,2048]{1,0:T(8,128)S(1)}, u32[]{:S(2)}, u32[]{:S(2)}) %collective-permute-start.8) | collective-permute-done | bytes 262176 | tf_op jit(solution)/shard_map/ppermute | solution.py:436
  38.5 0.8 sum_of_cores.1.refs_2_
  39.3 3.8 %all-to-all-start = ((bf16[8,4,2560]{2,1,0:T(4,128)(2,1)}), bf16[8,4,2560]{2,1,0:T(4,128)(2,1)S(1)}, u32[]{:S(2)}, u32[]{:S(2)}) async-start(bf16[8,4,2560]{2,1,0:T(4,128)(2,1)} %sum_of_cores.1.refs_2_), calls=%async_computation | async-start | bytes 327680 | tf_op jit(solution)/shard_map/all_to_all | solution.py:519
  43.1 0.1 multiply_sine_fusion
  43.2 1.6 %load_cache.1.cache = bf16[4096,256]{1,0:T(8,128)(2,1)S(1)} custom-call(bf16[2048,256]{1,0:T(8,128)(2,1)} %bitcast.9, bf16[2048,256]{1,0:T(8,128)(2,1)} %bitcast.10, bf16[8,4,2560]{2,1,0:T(4,128)(2,1)} %sum_of_cores.1.refs_2_), custom_call_target="tpu_custom_call" | custom-call | bytes 2097152 | tf_op jit(solution)/shard_map/load_cache/pallas_call | solution.py:124
  44.8 6.1 %all-to-all-done.arrived = bf16[8,4,2560]{2,1,0:T(4,128)(2,1)S(1)} async-done(((bf16[8,4,2560]{2,1,0:T(4,128)(2,1)}), bf16[8,4,2560]{2,1,0:T(4,128)(2,1)S(1)}, u32[]{:S(2)}, u32[]{:S(2)}) %all-to-all-start) | async-done | bytes 163872 | tf_op jit(solution)/shard_map/all_to_all | solution.py:519
  50.9 1.7 %attention.1.refs_1_.refs_2_ = bf16[4,12288]{1,0:T(4,128)(2,1)S(1)} custom-call(s32[1]{0:T(128)} %copy.9.length, f32[4,128]{1,0:T(4,128)S(1)} %get-tuple-element.32.cosine, f32[4,128]{1,0:T(4,128)S(1)} %get-tuple-element.31.sine, bf16[8,4,2560]{2,1,0:T(4,128)(2,1)S(1)} %all-to-all-done.arrived, bf16[4096,256]{1,0:T(8,128)(2,1)S(1)} %load_cache.1.cache), custom_call_target="tpu_custom_call" | custom-call | flops 402653184 | bytes 2265092 | tf_op jit(solution)/shard_map/attention/pallas_call | solution.py:124
  52.6 0.1 collective-permute-start.10
  52.7 1.3 %collective-permute-start.11 = (bf16[4,12288]{1,0:T(4,128)(2,1)S(1)}, bf16[4,12288]{1,0:T(4,128)(2,1)S(1)}, u32[]{:S(2)}, u32[]{:S(2)}) collective-permute-start(bf16[4,12288]{1,0:T(4,128)(2,1)S(1)} %attention.1.refs_1_.refs_2_), channel_id=1, source_target_pairs={{0,8},{2,10},{4,12},{6,14},{8,0},{10,2},{12,4},{14,6},{1,9},{3,11}... | collective-permute-start | bytes 294920 | tf_op jit(solution)/shard_map/ppermute | solution.py:436
  54.0 1.4 %collective-permute-start.9 = (bf16[4,12288]{1,0:T(4,128)(2,1)S(1)}, bf16[4,12288]{1,0:T(4,128)(2,1)S(1)}, u32[]{:S(2)}, u32[]{:S(2)}) collective-permute-start(bf16[4,12288]{1,0:T(4,128)(2,1)S(1)} %attention.1.refs_1_.refs_2_), channel_id=1, source_target_pairs={{0,2},{2,0},{4,6},{6,4},{8,10},{10,8},{12,14},{14,12},{1,3},{3,1},... | collective-permute-start | bytes 294920 | tf_op jit(solution)/shard_map/ppermute | solution.py:436
  55.5 3.8 %load_out_weights.2.refs_0_ = bf16[4096,1152]{1,0:T(8,128)(2,1)S(1)} custom-call(bf16[12288,1152]{1,0:T(8,128)(2,1)} %w_out.1, bf16[4,12288]{1,0:T(4,128)(2,1)S(1)} %attention.1.refs_1_.refs_2_), custom_call_target="tpu_custom_call" | custom-call | bytes 9437184 | tf_op jit(solution)/shard_map/load_out_weights/pallas_call | solution.py:124
  59.3 0.0 collective-permute-done.10.refs_4_
  59.3 0.0 collective-permute-done.11.refs_1_.refs_6_
  59.3 0.0 collective-permute-done.9.refs_3_
  59.3 1.3 %collective-permute-start.14 = (bf16[4,12288]{1,0:T(4,128)(2,1)S(1)}, bf16[4,12288]{1,0:T(4,128)(2,1)S(1)}, u32[]{:S(2)}, u32[]{:S(2)}) collective-permute-start(bf16[4,12288]{1,0:T(4,128)(2,1)S(1)} %collective-permute-done.11.refs_1_.refs_6_), channel_id=1, source_target_pairs={{0,2},{2,0},{4,6},{6,4},{8,10},{10,8},{12,14},{14,12},{1,3},{3,1},... | collective-permute-start | bytes 294920 | tf_op jit(solution)/shard_map/ppermute | solution.py:436
  60.6 0.8 collective-permute-start.12
  61.4 0.9 %collective-permute-start.13 = (bf16[4,12288]{1,0:T(4,128)(2,1)S(1)}, bf16[4,12288]{1,0:T(4,128)(2,1)S(1)}, u32[]{:S(2)}, u32[]{:S(2)}) collective-permute-start(bf16[4,12288]{1,0:T(4,128)(2,1)S(1)} %collective-permute-done.11.refs_1_.refs_6_), channel_id=1, source_target_pairs={{0,4},{2,6},{4,0},{6,2},{8,12},{10,14},{12,8},{14,10},{1,5},{3,7},... | collective-permute-start | bytes 294920 | tf_op jit(solution)/shard_map/ppermute | solution.py:436
  62.3 1.7 %collective-permute-done.14.refs_7_ = bf16[4,12288]{1,0:T(4,128)(2,1)S(1)} collective-permute-done((bf16[4,12288]{1,0:T(4,128)(2,1)S(1)}, bf16[4,12288]{1,0:T(4,128)(2,1)S(1)}, u32[]{:S(2)}, u32[]{:S(2)}) %collective-permute-start.14) | collective-permute-done | bytes 98336 | tf_op jit(solution)/shard_map/ppermute | solution.py:436
  64.0 0.9 %collective-permute-start.15 = (bf16[4,12288]{1,0:T(4,128)(2,1)S(1)}, bf16[4,12288]{1,0:T(4,128)(2,1)S(1)}, u32[]{:S(2)}, u32[]{:S(2)}) collective-permute-start(bf16[4,12288]{1,0:T(4,128)(2,1)S(1)} %collective-permute-done.14.refs_7_), channel_id=1, source_target_pairs={{0,4},{2,6},{4,0},{6,2},{8,12},{10,14},{12,8},{14,10},{1,5},{3,7},... | collective-permute-start | bytes 294920 | tf_op jit(solution)/shard_map/ppermute | solution.py:436
  64.9 0.0 collective-permute-start.16
  64.9 0.5 collective-permute-start.17
  65.4 0.0 collective-permute-done.12.refs_5_
  65.4 0.0 collective-permute-start.18
  65.4 3.8 %load_out_weights.3.refs_1_ = bf16[4096,1152]{1,0:T(8,128)(2,1)S(1)} custom-call(bf16[12288,1152]{1,0:T(8,128)(2,1)} %w_out.1, bf16[4,12288]{1,0:T(4,128)(2,1)S(1)} %collective-permute-done.11.refs_1_.refs_6_), custom_call_target="tpu_custom_call" | custom-call | bytes 9437184 | tf_op jit(solution)/shard_map/load_out_weights/pallas_call | solution.py:124
  69.2 0.0 collective-permute-done.13.refs_8_
  69.2 0.6 collective-permute-start.20
  69.7 0.0 collective-permute-done.15.refs_9_
  69.7 0.1 collective-permute-start.21
  69.8 0.0 collective-permute-done.16.refs_10_
  69.8 0.4 collective-permute-start.19
  70.3 0.0 collective-permute-done.17.refs_11_
  70.3 0.1 collective-permute-start.22
  70.3 0.0 collective-permute-done.18.refs_12_
  70.4 0.4 collective-permute-start.23
  70.8 0.0 collective-permute-done.20.refs_14_
  70.8 0.3 collective-permute-done.21.refs_15_
  71.0 0.2 collective-permute-done.19.refs_13_
  71.2 0.4 collective-permute-done.22.refs_16_
  71.6 0.2 collective-permute-done.23.refs_17_
  71.7 7.3 %project_out.1 = bf16[4,16,1152]{2,1,0:T(8,128)(2,1)} custom-call(s32[2]{0:T(128)S(1)} %pad_add_fusion.place, bf16[12288,1152]{1,0:T(8,128)(2,1)} %w_out.1, bf16[4096,1152]{1,0:T(8,128)(2,1)S(1)} %load_out_weights.2.refs_0_, bf16[4096,1152]{1,0:T(8,128)(2,1)S(1)} %load_out_weights.3.refs_1_, bf16[4,12288]{1,0:T(4,128)(2,1)S(1)} %attention.1.refs_1_.refs_2_, ...), custom_call_target="tpu_custom_call" | custom-call | flops 1811939328 | bytes 48758792 | tf_op jit(solution)/shard_map/project_out/pallas_call | solution.py:124
  (3 shorter events, 0.1 us)
Async XLA Ops:
  0.0 0.9 %copy-start = (bf16[4,16,1152]{2,1,0:T(8,128)(2,1)S(1)}, bf16[4,16,1152]{2,1,0:T(8,128)(2,1)}, u32[]{:S(2)}) copy-start(bf16[4,16,1152]{2,1,0:T(8,128)(2,1)} %param.8) | copy-start | bytes 442372
  1.0 1.3 %collective-permute-start = (f32[8,128]{1,0:T(8,128)S(1)}, f32[8,128]{1,0:T(8,128)S(1)}, u32[]{:S(2)}, u32[]{:S(2)}) collective-permute-start(f32[8,128]{1,0:T(8,128)S(1)} %row_sums.1.mine), channel_id=1, source_target_pairs={{0,1},{1,0},{2,3},{3,2},{4,5},{5,4},{6,7},{7,6},{8,9},{9,8},{10,11... | collective-permute-start | bytes 12296 | tf_op jit(solution)/shard_map/ppermute | solution.py:436
  2.4 7.2 %collective-permute-start.1 = (bf16[592,128]{1,0:T(8,128)(2,1)S(1)}, bf16[592,128]{1,0:T(8,128)(2,1)S(1)}, u32[]{:S(2)}, u32[]{:S(2)}) collective-permute-start(bf16[592,128]{1,0:T(8,128)(2,1)S(1)} %payload.1.refs_0_), channel_id=1, source_target_pairs={{0,2},{2,0},{4,6},{6,4},{8,10},{10,8},{12,14},{14,12},{1,3},{3,1},... | collective-permute-start | bytes 454664 | tf_op jit(solution)/shard_map/ppermute | solution.py:436
  5.3 8.7 %collective-permute-start.2 = (bf16[592,128]{1,0:T(8,128)(2,1)S(1)}, bf16[592,128]{1,0:T(8,128)(2,1)S(1)}, u32[]{:S(2)}, u32[]{:S(2)}) collective-permute-start(bf16[592,128]{1,0:T(8,128)(2,1)S(1)} %payload.1.refs_0_), channel_id=1, source_target_pairs={{0,4},{2,6},{4,0},{6,2},{8,12},{10,14},{12,8},{14,10},{1,5},{3,7},... | collective-permute-start | bytes 454664 | tf_op jit(solution)/shard_map/ppermute | solution.py:436
  6.9 9.6 %collective-permute-start.3 = (bf16[592,128]{1,0:T(8,128)(2,1)S(1)}, bf16[592,128]{1,0:T(8,128)(2,1)S(1)}, u32[]{:S(2)}, u32[]{:S(2)}) collective-permute-start(bf16[592,128]{1,0:T(8,128)(2,1)S(1)} %payload.1.refs_0_), channel_id=1, source_target_pairs={{0,8},{2,10},{4,12},{6,14},{8,0},{10,2},{12,4},{14,6},{1,9},{3,11}... | collective-permute-start | bytes 454664 | tf_op jit(solution)/shard_map/ppermute | solution.py:436
  16.5 5.2 %collective-permute-start.5 = (bf16[592,128]{1,0:T(8,128)(2,1)S(1)}, bf16[592,128]{1,0:T(8,128)(2,1)S(1)}, u32[]{:S(2)}, u32[]{:S(2)}) collective-permute-start(bf16[592,128]{1,0:T(8,128)(2,1)S(1)} %collective-permute-done.3.refs_4_), channel_id=1, source_target_pairs={{0,2},{2,0},{4,6},{6,4},{8,10},{10,8},{12,14},{14,12},{1,3},{3,1},... | collective-permute-start | bytes 454664 | tf_op jit(solution)/shard_map/ppermute | solution.py:436
  17.1 13.1 %collective-permute-start.6 = (bf16[592,128]{1,0:T(8,128)(2,1)S(1)}, bf16[592,128]{1,0:T(8,128)(2,1)S(1)}, u32[]{:S(2)}, u32[]{:S(2)}) collective-permute-start(bf16[592,128]{1,0:T(8,128)(2,1)S(1)} %collective-permute-done.3.refs_4_), channel_id=1, source_target_pairs={{0,4},{2,6},{4,0},{6,2},{8,12},{10,14},{12,8},{14,10},{1,5},{3,7},... | collective-permute-start | bytes 454664 | tf_op jit(solution)/shard_map/ppermute | solution.py:436
  17.5 12.6 %collective-permute-start.4 = (bf16[592,128]{1,0:T(8,128)(2,1)S(1)}, bf16[592,128]{1,0:T(8,128)(2,1)S(1)}, u32[]{:S(2)}, u32[]{:S(2)}) collective-permute-start(bf16[592,128]{1,0:T(8,128)(2,1)S(1)} %collective-permute-done.2.refs_2_), channel_id=1, source_target_pairs={{0,2},{2,0},{4,6},{6,4},{8,10},{10,8},{12,14},{14,12},{1,3},{3,1},... | collective-permute-start | bytes 454664 | tf_op jit(solution)/shard_map/ppermute | solution.py:436
  21.8 8.4 %collective-permute-start.7 = (bf16[592,128]{1,0:T(8,128)(2,1)S(1)}, bf16[592,128]{1,0:T(8,128)(2,1)S(1)}, u32[]{:S(2)}, u32[]{:S(2)}) collective-permute-start(bf16[592,128]{1,0:T(8,128)(2,1)S(1)} %collective-permute-done.5.refs_5_), channel_id=1, source_target_pairs={{0,4},{2,6},{4,0},{6,2},{8,12},{10,14},{12,8},{14,10},{1,5},{3,7},... | collective-permute-start | bytes 454664 | tf_op jit(solution)/shard_map/ppermute | solution.py:436
  36.9 1.6 %collective-permute-start.8 = (f32[32,2048]{1,0:T(8,128)S(1)}, f32[32,2048]{1,0:T(8,128)S(1)}, u32[]{:S(2)}, u32[]{:S(2)}) collective-permute-start(f32[32,2048]{1,0:T(8,128)S(1)} %get-tuple-element.22), channel_id=1, source_target_pairs={{0,1},{1,0},{2,3},{3,2},{4,5},{5,4},{6,7},{7,6},{8,9},{9,8},{10,11... | collective-permute-start | bytes 786440 | tf_op jit(solution)/shard_map/ppermute | solution.py:436
  39.3 11.6 %all-to-all-start = ((bf16[8,4,2560]{2,1,0:T(4,128)(2,1)}), bf16[8,4,2560]{2,1,0:T(4,128)(2,1)S(1)}, u32[]{:S(2)}, u32[]{:S(2)}) async-start(bf16[8,4,2560]{2,1,0:T(4,128)(2,1)} %sum_of_cores.1.refs_2_), calls=%async_computation | async-start | bytes 327680 | tf_op jit(solution)/shard_map/all_to_all | solution.py:519
  52.6 6.6 %collective-permute-start.10 = (bf16[4,12288]{1,0:T(4,128)(2,1)S(1)}, bf16[4,12288]{1,0:T(4,128)(2,1)S(1)}, u32[]{:S(2)}, u32[]{:S(2)}) collective-permute-start(bf16[4,12288]{1,0:T(4,128)(2,1)S(1)} %attention.1.refs_1_.refs_2_), channel_id=1, source_target_pairs={{0,4},{2,6},{4,0},{6,2},{8,12},{10,14},{12,8},{14,10},{1,5},{3,7},... | collective-permute-start | bytes 294920 | tf_op jit(solution)/shard_map/ppermute | solution.py:436
  52.7 6.6 %collective-permute-start.11 = (bf16[4,12288]{1,0:T(4,128)(2,1)S(1)}, bf16[4,12288]{1,0:T(4,128)(2,1)S(1)}, u32[]{:S(2)}, u32[]{:S(2)}) collective-permute-start(bf16[4,12288]{1,0:T(4,128)(2,1)S(1)} %attention.1.refs_1_.refs_2_), channel_id=1, source_target_pairs={{0,8},{2,10},{4,12},{6,14},{8,0},{10,2},{12,4},{14,6},{1,9},{3,11}... | collective-permute-start | bytes 294920 | tf_op jit(solution)/shard_map/ppermute | solution.py:436
  54.0 5.2 %collective-permute-start.9 = (bf16[4,12288]{1,0:T(4,128)(2,1)S(1)}, bf16[4,12288]{1,0:T(4,128)(2,1)S(1)}, u32[]{:S(2)}, u32[]{:S(2)}) collective-permute-start(bf16[4,12288]{1,0:T(4,128)(2,1)S(1)} %attention.1.refs_1_.refs_2_), channel_id=1, source_target_pairs={{0,2},{2,0},{4,6},{6,4},{8,10},{10,8},{12,14},{14,12},{1,3},{3,1},... | collective-permute-start | bytes 294920 | tf_op jit(solution)/shard_map/ppermute | solution.py:436
  59.3 4.7 %collective-permute-start.14 = (bf16[4,12288]{1,0:T(4,128)(2,1)S(1)}, bf16[4,12288]{1,0:T(4,128)(2,1)S(1)}, u32[]{:S(2)}, u32[]{:S(2)}) collective-permute-start(bf16[4,12288]{1,0:T(4,128)(2,1)S(1)} %collective-permute-done.11.refs_1_.refs_6_), channel_id=1, source_target_pairs={{0,2},{2,0},{4,6},{6,4},{8,10},{10,8},{12,14},{14,12},{1,3},{3,1},... | collective-permute-start | bytes 294920 | tf_op jit(solution)/shard_map/ppermute | solution.py:436
  60.6 4.8 %collective-permute-start.12 = (bf16[4,12288]{1,0:T(4,128)(2,1)S(1)}, bf16[4,12288]{1,0:T(4,128)(2,1)S(1)}, u32[]{:S(2)}, u32[]{:S(2)}) collective-permute-start(bf16[4,12288]{1,0:T(4,128)(2,1)S(1)} %collective-permute-done.10.refs_4_), channel_id=1, source_target_pairs={{0,2},{2,0},{4,6},{6,4},{8,10},{10,8},{12,14},{14,12},{1,3},{3,1},... | collective-permute-start | bytes 294920 | tf_op jit(solution)/shard_map/ppermute | solution.py:436
  61.4 7.8 %collective-permute-start.13 = (bf16[4,12288]{1,0:T(4,128)(2,1)S(1)}, bf16[4,12288]{1,0:T(4,128)(2,1)S(1)}, u32[]{:S(2)}, u32[]{:S(2)}) collective-permute-start(bf16[4,12288]{1,0:T(4,128)(2,1)S(1)} %collective-permute-done.11.refs_1_.refs_6_), channel_id=1, source_target_pairs={{0,4},{2,6},{4,0},{6,2},{8,12},{10,14},{12,8},{14,10},{1,5},{3,7},... | collective-permute-start | bytes 294920 | tf_op jit(solution)/shard_map/ppermute | solution.py:436
  64.0 5.8 %collective-permute-start.15 = (bf16[4,12288]{1,0:T(4,128)(2,1)S(1)}, bf16[4,12288]{1,0:T(4,128)(2,1)S(1)}, u32[]{:S(2)}, u32[]{:S(2)}) collective-permute-start(bf16[4,12288]{1,0:T(4,128)(2,1)S(1)} %collective-permute-done.14.refs_7_), channel_id=1, source_target_pairs={{0,4},{2,6},{4,0},{6,2},{8,12},{10,14},{12,8},{14,10},{1,5},{3,7},... | collective-permute-start | bytes 294920 | tf_op jit(solution)/shard_map/ppermute | solution.py:436
  64.9 5.0 %collective-permute-start.16 = (bf16[4,12288]{1,0:T(4,128)(2,1)S(1)}, bf16[4,12288]{1,0:T(4,128)(2,1)S(1)}, u32[]{:S(2)}, u32[]{:S(2)}) collective-permute-start(bf16[4,12288]{1,0:T(4,128)(2,1)S(1)} %attention.1.refs_1_.refs_2_), channel_id=1, source_target_pairs={{0,1},{1,0},{2,3},{3,2},{4,5},{5,4},{6,7},{7,6},{8,9},{9,8},{10,11... | collective-permute-start | bytes 294920 | tf_op jit(solution)/shard_map/ppermute | solution.py:436
  64.9 5.4 %collective-permute-start.17 = (bf16[4,12288]{1,0:T(4,128)(2,1)S(1)}, bf16[4,12288]{1,0:T(4,128)(2,1)S(1)}, u32[]{:S(2)}, u32[]{:S(2)}) collective-permute-start(bf16[4,12288]{1,0:T(4,128)(2,1)S(1)} %collective-permute-done.9.refs_3_), channel_id=1, source_target_pairs={{0,1},{1,0},{2,3},{3,2},{4,5},{5,4},{6,7},{7,6},{8,9},{9,8},{10,11... | collective-permute-start | bytes 294920 | tf_op jit(solution)/shard_map/ppermute | solution.py:436
  65.4 5.0 %collective-permute-start.18 = (bf16[4,12288]{1,0:T(4,128)(2,1)S(1)}, bf16[4,12288]{1,0:T(4,128)(2,1)S(1)}, u32[]{:S(2)}, u32[]{:S(2)}) collective-permute-start(bf16[4,12288]{1,0:T(4,128)(2,1)S(1)} %collective-permute-done.10.refs_4_), channel_id=1, source_target_pairs={{0,1},{1,0},{2,3},{3,2},{4,5},{5,4},{6,7},{7,6},{8,9},{9,8},{10,11... | collective-permute-start | bytes 294920 | tf_op jit(solution)/shard_map/ppermute | solution.py:436
  69.2 1.6 %collective-permute-start.20 = (bf16[4,12288]{1,0:T(4,128)(2,1)S(1)}, bf16[4,12288]{1,0:T(4,128)(2,1)S(1)}, u32[]{:S(2)}, u32[]{:S(2)}) collective-permute-start(bf16[4,12288]{1,0:T(4,128)(2,1)S(1)} %collective-permute-done.11.refs_1_.refs_6_), channel_id=1, source_target_pairs={{0,1},{1,0},{2,3},{3,2},{4,5},{5,4},{6,7},{7,6},{8,9},{9,8},{10,11... | collective-permute-start | bytes 294920 | tf_op jit(solution)/shard_map/ppermute | solution.py:436
  69.7 1.3 %collective-permute-start.21 = (bf16[4,12288]{1,0:T(4,128)(2,1)S(1)}, bf16[4,12288]{1,0:T(4,128)(2,1)S(1)}, u32[]{:S(2)}, u32[]{:S(2)}) collective-permute-start(bf16[4,12288]{1,0:T(4,128)(2,1)S(1)} %collective-permute-done.14.refs_7_), channel_id=1, source_target_pairs={{0,1},{1,0},{2,3},{3,2},{4,5},{5,4},{6,7},{7,6},{8,9},{9,8},{10,11... | collective-permute-start | bytes 294920 | tf_op jit(solution)/shard_map/ppermute | solution.py:436
  69.8 1.4 %collective-permute-start.19 = (bf16[4,12288]{1,0:T(4,128)(2,1)S(1)}, bf16[4,12288]{1,0:T(4,128)(2,1)S(1)}, u32[]{:S(2)}, u32[]{:S(2)}) collective-permute-start(bf16[4,12288]{1,0:T(4,128)(2,1)S(1)} %collective-permute-done.12.refs_5_), channel_id=1, source_target_pairs={{0,1},{1,0},{2,3},{3,2},{4,5},{5,4},{6,7},{7,6},{8,9},{9,8},{10,11... | collective-permute-start | bytes 294920 | tf_op jit(solution)/shard_map/ppermute | solution.py:436
  70.3 1.3 %collective-permute-start.22 = (bf16[4,12288]{1,0:T(4,128)(2,1)S(1)}, bf16[4,12288]{1,0:T(4,128)(2,1)S(1)}, u32[]{:S(2)}, u32[]{:S(2)}) collective-permute-start(bf16[4,12288]{1,0:T(4,128)(2,1)S(1)} %collective-permute-done.13.refs_8_), channel_id=1, source_target_pairs={{0,1},{1,0},{2,3},{3,2},{4,5},{5,4},{6,7},{7,6},{8,9},{9,8},{10,11... | collective-permute-start | bytes 294920 | tf_op jit(solution)/shard_map/ppermute | solution.py:436
  70.4 1.4 %collective-permute-start.23 = (bf16[4,12288]{1,0:T(4,128)(2,1)S(1)}, bf16[4,12288]{1,0:T(4,128)(2,1)S(1)}, u32[]{:S(2)}, u32[]{:S(2)}) collective-permute-start(bf16[4,12288]{1,0:T(4,128)(2,1)S(1)} %collective-permute-done.15.refs_9_), channel_id=1, source_target_pairs={{0,1},{1,0},{2,3},{3,2},{4,5},{5,4},{6,7},{7,6},{8,9},{9,8},{10,11... | collective-permute-start | bytes 294920 | tf_op jit(solution)/shard_map/ppermute | solution.py:436

commit v6 on v5

--- a/solution.py
+++ b/solution.py
@@ -440,11 +440,12 @@
     near = {0: block}
     for bits in (4, 2, 1):
         near[bits] = swap(block, "wide", bits)
-    near[1], near[2], near[4] = lax.optimization_barrier((near[1], near[2], near[4]))
+    near[4], near[2], near[1] = lax.optimization_barrier((near[4], near[2], near[1]))
     near[6] = swap(near[4], "wide", 2)
     near[5] = swap(near[4], "wide", 1)
+    near[5], near[2] = lax.optimization_barrier((near[5], near[2]))
+    near[7] = swap(near[5], "wide", 2)
     near[3] = swap(near[2], "wide", 1)
-    near[7] = swap(near[5], "wide", 2)
     return [near[k] for k in range(8)]
 
 

time: 79.4 us -> 78.9 us (level)
  waiting for transfers between devices: 19.5 us -> 16.7 us
  starting transfers between devices: 24.4 us -> 26.7 us
    ppermute x24, waiting for transfers between devices: 13.5 us -> 10.7 us  [swap(): return lax.ppermute(value, axis, [(at, at ^ bits) for at in range(size)])]
    ppermute x24, starting transfers between devices: 20.6 us -> 22.4 us  [swap(): return lax.ppermute(value, axis, [(at, at ^ bits) for at in range(size)])]
  transfers between devices with their start and end apart: 25 -> 25, of which waited for: 12 -> 11; matrix products, arithmetic and copies ran while one was open for 1% -> 1% of each run, Pallas kernels for 20% -> 20%
where the time goes in v6:
time: 78.9 us; the launch traced here: 78.5 us
  Pallas kernels  32.6 us (41%)
  starting transfers between devices  26.7 us (34%)
  waiting for transfers between devices  16.7 us (21%)
  local copies, waits for them, and re-layouts  1.6 us (2%)
    pallas_call x10, Pallas kernels, call(): pl.pallas_call(kernel, out_shape=out_shape, in_specs=in_specs or [IN_VMEM...  32.6 us
    ppermute x24, starting transfers between devices, swap(): return lax.ppermute(value, axis, [(at, at ^ bits) for at in range(size)])  22.4 us
    ppermute x24, waiting for transfers between devices, swap(): return lax.ppermute(value, axis, [(at, at ^ bits) for at in range(size)])  10.7 us
    all_to_all x1, waiting for transfers between devices, local_fast(): arrived = lax.all_to_all(outgoing, 'wide', 0, 0, tiled=True)  6.07 us
    all_to_all x1, starting transfers between devices, local_fast(): arrived = lax.all_to_all(outgoing, 'wide', 0, 0, tiled=True)  4.29 us
  transfers between devices with their start and end apart: 25, of which 11 were waited for; matrix products, arithmetic and copies ran while one was open for 1% of the time, Pallas kernels for 20%

profile of v6, /device:TPU:0, one launch (start us, length us, event | category | flops | bytes accessed | tf_op | source)
XLA Modules:
  0.0 78.5 jit_solution(16878681473540445948)
XLA Ops:
  0.0 0.0 copy-start
  0.0 0.9 %copy-done = bf16[4,16,1152]{2,1,0:T(8,128)(2,1)S(1)} copy-done((bf16[4,16,1152]{2,1,0:T(8,128)(2,1)S(1)}, bf16[4,16,1152]{2,1,0:T(8,128)(2,1)}, u32[]{:S(2)}) %copy-start) | copy-done | bytes 147480
  0.9 0.1 row_sums.1.mine
  1.0 0.5 collective-permute-start
  1.6 0.7 broadcast_in_dim.2.gain
  2.2 0.1 collective-permute-done.theirs
  2.4 4.0 %collective-permute-start.1 = (bf16[592,128]{1,0:T(8,128)(2,1)S(1)}, bf16[592,128]{1,0:T(8,128)(2,1)S(1)}, u32[]{:S(2)}, u32[]{:S(2)}) collective-permute-start(bf16[592,128]{1,0:T(8,128)(2,1)S(1)} %payload.1.refs_0_), channel_id=1, source_target_pairs={{0,8},{2,10},{4,12},{6,14},{8,0},{10,2},{12,4},{14,6},{1,9},{3,11}... | collective-permute-start | bytes 454664 | tf_op jit(solution)/shard_map/ppermute | solution.py:436
  6.4 1.6 %collective-permute-start.2 = (bf16[592,128]{1,0:T(8,128)(2,1)S(1)}, bf16[592,128]{1,0:T(8,128)(2,1)S(1)}, u32[]{:S(2)}, u32[]{:S(2)}) collective-permute-start(bf16[592,128]{1,0:T(8,128)(2,1)S(1)} %payload.1.refs_0_), channel_id=1, source_target_pairs={{0,4},{2,6},{4,0},{6,2},{8,12},{10,14},{12,8},{14,10},{1,5},{3,7},... | collective-permute-start | bytes 454664 | tf_op jit(solution)/shard_map/ppermute | solution.py:436
  8.0 1.5 %collective-permute-start.3 = (bf16[592,128]{1,0:T(8,128)(2,1)S(1)}, bf16[592,128]{1,0:T(8,128)(2,1)S(1)}, u32[]{:S(2)}, u32[]{:S(2)}) collective-permute-start(bf16[592,128]{1,0:T(8,128)(2,1)S(1)} %payload.1.refs_0_), channel_id=1, source_target_pairs={{0,2},{2,0},{4,6},{6,4},{8,10},{10,8},{12,14},{14,12},{1,3},{3,1},... | collective-permute-start | bytes 454664 | tf_op jit(solution)/shard_map/ppermute | solution.py:436
  9.5 4.6 %collective-permute-done.1.refs_4_ = bf16[592,128]{1,0:T(8,128)(2,1)S(1)} collective-permute-done((bf16[592,128]{1,0:T(8,128)(2,1)S(1)}, bf16[592,128]{1,0:T(8,128)(2,1)S(1)}, u32[]{:S(2)}, u32[]{:S(2)}) %collective-permute-start.1) | collective-permute-done | bytes 151584 | tf_op jit(solution)/shard_map/ppermute | solution.py:436
  14.0 0.2 collective-permute-done.2.refs_2_
  14.2 0.0 collective-permute-done.3.refs_1_
  14.2 1.5 %collective-permute-start.4 = (bf16[592,128]{1,0:T(8,128)(2,1)S(1)}, bf16[592,128]{1,0:T(8,128)(2,1)S(1)}, u32[]{:S(2)}, u32[]{:S(2)}) collective-permute-start(bf16[592,128]{1,0:T(8,128)(2,1)S(1)} %collective-permute-done.1.refs_4_), channel_id=1, source_target_pairs={{0,2},{2,0},{4,6},{6,4},{8,10},{10,8},{12,14},{14,12},{1,3},{3,1},... | collective-permute-start | bytes 454664 | tf_op jit(solution)/shard_map/ppermute | solution.py:436
  15.8 1.4 %collective-permute-start.6 = (bf16[592,128]{1,0:T(8,128)(2,1)S(1)}, bf16[592,128]{1,0:T(8,128)(2,1)S(1)}, u32[]{:S(2)}, u32[]{:S(2)}) collective-permute-start(bf16[592,128]{1,0:T(8,128)(2,1)S(1)} %collective-permute-done.1.refs_4_), channel_id=1, source_target_pairs={{0,4},{2,6},{4,0},{6,2},{8,12},{10,14},{12,8},{14,10},{1,5},{3,7},... | collective-permute-start | bytes 454664 | tf_op jit(solution)/shard_map/ppermute | solution.py:436
  17.2 2.2 %collective-permute-done.4.refs_5_ = bf16[592,128]{1,0:T(8,128)(2,1)S(1)} collective-permute-done((bf16[592,128]{1,0:T(8,128)(2,1)S(1)}, bf16[592,128]{1,0:T(8,128)(2,1)S(1)}, u32[]{:S(2)}, u32[]{:S(2)}) %collective-permute-start.4) | collective-permute-done | bytes 151584 | tf_op jit(solution)/shard_map/ppermute | solution.py:436
  19.4 1.5 %collective-permute-start.5 = (bf16[592,128]{1,0:T(8,128)(2,1)S(1)}, bf16[592,128]{1,0:T(8,128)(2,1)S(1)}, u32[]{:S(2)}, u32[]{:S(2)}) collective-permute-start(bf16[592,128]{1,0:T(8,128)(2,1)S(1)} %collective-permute-done.2.refs_2_), channel_id=1, source_target_pairs={{0,2},{2,0},{4,6},{6,4},{8,10},{10,8},{12,14},{14,12},{1,3},{3,1},... | collective-permute-start | bytes 454664 | tf_op jit(solution)/shard_map/ppermute | solution.py:436
  21.0 1.4 %collective-permute-start.7 = (bf16[592,128]{1,0:T(8,128)(2,1)S(1)}, bf16[592,128]{1,0:T(8,128)(2,1)S(1)}, u32[]{:S(2)}, u32[]{:S(2)}) collective-permute-start(bf16[592,128]{1,0:T(8,128)(2,1)S(1)} %collective-permute-done.4.refs_5_), channel_id=1, source_target_pairs={{0,4},{2,6},{4,0},{6,2},{8,12},{10,14},{12,8},{14,10},{1,5},{3,7},... | collective-permute-start | bytes 454664 | tf_op jit(solution)/shard_map/ppermute | solution.py:436
  22.4 6.6 %load_query_weights.1.early = bf16[9216,1024]{1,0:T(8,128)(2,1)S(1)} custom-call(bf16[9216,1536]{1,0:T(8,128)(2,1)} %w_query.1), custom_call_target="tpu_custom_call" | custom-call | bytes 18874368 | tf_op jit(solution)/shard_map/load_query_weights/pallas_call | solution.py:124
  29.0 0.1 pad_add_fusion.place
  29.1 0.0 collective-permute-done.6.refs_6_
  29.1 0.0 collective-permute-done.5.refs_3_
  29.1 0.0 collective-permute-done.7.refs_7_
  29.1 6.8 %norm_and_project.1 = (f32[32,2048]{1,0:T(8,128)S(1)}, f32[32,2048]{1,0:T(8,128)S(1)}) custom-call(s32[2]{0:T(128)S(1)} %pad_add_fusion.place, bf16[1152,512]{1,0:T(8,128)(2,1)} %w_keyval_far.1, bf16[9216,1536]{1,0:T(8,128)(2,1)} %w_query.1, bf16[9216,1024]{1,0:T(8,128)(2,1)S(1)} %load_query_weights.1.early, bf16[592,128]{1,0:T(8,128)(2,1)S(1)} %payload.1.refs_0_, ...), custom_call_target="tpu_custom_call" | custom-call | flops 1811939328 | bytes 49577992 | tf_op jit(solution)/shard_map/norm_and_project/pallas_call | solution.py:124
  35.9 0.1 collective-permute-start.8
  36.7 0.9 %collective-permute-done.8.theirs = f32[32,2048]{1,0:T(8,128)S(1)} collective-permute-done((f32[32,2048]{1,0:T(8,128)S(1)}, f32[32,2048]{1,0:T(8,128)S(1)}, u32[]{:S(2)}, u32[]{:S(2)}) %collective-permute-start.8) | collective-permute-done | bytes 262176 | tf_op jit(solution)/shard_map/ppermute | solution.py:436
  37.5 0.8 sum_of_cores.1.refs_2_
  38.3 4.3 %all-to-all-start = ((bf16[8,4,2560]{2,1,0:T(4,128)(2,1)}), bf16[8,4,2560]{2,1,0:T(4,128)(2,1)S(1)}, u32[]{:S(2)}, u32[]{:S(2)}) async-start(bf16[8,4,2560]{2,1,0:T(4,128)(2,1)} %sum_of_cores.1.refs_2_), calls=%async_computation | async-start | bytes 327680 | tf_op jit(solution)/shard_map/all_to_all | solution.py:520
  42.6 0.1 multiply_sine_fusion
  42.7 1.6 %load_cache.1.cache = bf16[4096,256]{1,0:T(8,128)(2,1)S(1)} custom-call(bf16[2048,256]{1,0:T(8,128)(2,1)} %bitcast.9, bf16[2048,256]{1,0:T(8,128)(2,1)} %bitcast.10, bf16[8,4,2560]{2,1,0:T(4,128)(2,1)} %sum_of_cores.1.refs_2_), custom_call_target="tpu_custom_call" | custom-call | bytes 2097152 | tf_op jit(solution)/shard_map/load_cache/pallas_call | solution.py:124
  44.3 6.1 %all-to-all-done.arrived = bf16[8,4,2560]{2,1,0:T(4,128)(2,1)S(1)} async-done(((bf16[8,4,2560]{2,1,0:T(4,128)(2,1)}), bf16[8,4,2560]{2,1,0:T(4,128)(2,1)S(1)}, u32[]{:S(2)}, u32[]{:S(2)}) %all-to-all-start) | async-done | bytes 163872 | tf_op jit(solution)/shard_map/all_to_all | solution.py:520
  50.4 1.7 %attention.1.refs_1_.refs_2_ = bf16[4,12288]{1,0:T(4,128)(2,1)S(1)} custom-call(s32[1]{0:T(128)} %copy.9.length, f32[4,128]{1,0:T(4,128)S(1)} %get-tuple-element.36.cosine, f32[4,128]{1,0:T(4,128)S(1)} %get-tuple-element.35.sine, bf16[8,4,2560]{2,1,0:T(4,128)(2,1)S(1)} %all-to-all-done.arrived, bf16[4096,256]{1,0:T(8,128)(2,1)S(1)} %load_cache.1.cache), custom_call_target="tpu_custom_call" | custom-call | flops 402653184 | bytes 2265092 | tf_op jit(solution)/shard_map/attention/pallas_call | solution.py:124
  52.1 0.1 collective-permute-start.10
  52.2 1.3 %collective-permute-start.11 = (bf16[4,12288]{1,0:T(4,128)(2,1)S(1)}, bf16[4,12288]{1,0:T(4,128)(2,1)S(1)}, u32[]{:S(2)}, u32[]{:S(2)}) collective-permute-start(bf16[4,12288]{1,0:T(4,128)(2,1)S(1)} %attention.1.refs_1_.refs_2_), channel_id=1, source_target_pairs={{0,8},{2,10},{4,12},{6,14},{8,0},{10,2},{12,4},{14,6},{1,9},{3,11}... | collective-permute-start | bytes 294920 | tf_op jit(solution)/shard_map/ppermute | solution.py:436
  53.5 1.4 %collective-permute-start.9 = (bf16[4,12288]{1,0:T(4,128)(2,1)S(1)}, bf16[4,12288]{1,0:T(4,128)(2,1)S(1)}, u32[]{:S(2)}, u32[]{:S(2)}) collective-permute-start(bf16[4,12288]{1,0:T(4,128)(2,1)S(1)} %attention.1.refs_1_.refs_2_), channel_id=1, source_target_pairs={{0,2},{2,0},{4,6},{6,4},{8,10},{10,8},{12,14},{14,12},{1,3},{3,1},... | collective-permute-start | bytes 294920 | tf_op jit(solution)/shard_map/ppermute | solution.py:436
  54.9 3.8 %load_out_weights.2.refs_0_ = bf16[4096,1152]{1,0:T(8,128)(2,1)S(1)} custom-call(bf16[12288,1152]{1,0:T(8,128)(2,1)} %w_out.1, bf16[4,12288]{1,0:T(4,128)(2,1)S(1)} %attention.1.refs_1_.refs_2_), custom_call_target="tpu_custom_call" | custom-call | bytes 9437184 | tf_op jit(solution)/shard_map/load_out_weights/pallas_call | solution.py:124
  58.7 0.0 collective-permute-done.10.refs_4_
  58.7 0.0 collective-permute-done.11.refs_1_.refs_6_
  58.7 0.0 collective-permute-done.9.refs_3_
  58.8 1.3 %collective-permute-start.14 = (bf16[4,12288]{1,0:T(4,128)(2,1)S(1)}, bf16[4,12288]{1,0:T(4,128)(2,1)S(1)}, u32[]{:S(2)}, u32[]{:S(2)}) collective-permute-start(bf16[4,12288]{1,0:T(4,128)(2,1)S(1)} %collective-permute-done.11.refs_1_.refs_6_), channel_id=1, source_target_pairs={{0,2},{2,0},{4,6},{6,4},{8,10},{10,8},{12,14},{14,12},{1,3},{3,1},... | collective-permute-start | bytes 294920 | tf_op jit(solution)/shard_map/ppermute | solution.py:436
  60.1 0.8 collective-permute-start.12
  60.8 0.9 %collective-permute-start.13 = (bf16[4,12288]{1,0:T(4,128)(2,1)S(1)}, bf16[4,12288]{1,0:T(4,128)(2,1)S(1)}, u32[]{:S(2)}, u32[]{:S(2)}) collective-permute-start(bf16[4,12288]{1,0:T(4,128)(2,1)S(1)} %collective-permute-done.11.refs_1_.refs_6_), channel_id=1, source_target_pairs={{0,4},{2,6},{4,0},{6,2},{8,12},{10,14},{12,8},{14,10},{1,5},{3,7},... | collective-permute-start | bytes 294920 | tf_op jit(solution)/shard_map/ppermute | solution.py:436
  61.7 1.7 %collective-permute-done.14.refs_7_ = bf16[4,12288]{1,0:T(4,128)(2,1)S(1)} collective-permute-done((bf16[4,12288]{1,0:T(4,128)(2,1)S(1)}, bf16[4,12288]{1,0:T(4,128)(2,1)S(1)}, u32[]{:S(2)}, u32[]{:S(2)}) %collective-permute-start.14) | collective-permute-done | bytes 98336 | tf_op jit(solution)/shard_map/ppermute | solution.py:436
  63.4 0.9 %collective-permute-start.15 = (bf16[4,12288]{1,0:T(4,128)(2,1)S(1)}, bf16[4,12288]{1,0:T(4,128)(2,1)S(1)}, u32[]{:S(2)}, u32[]{:S(2)}) collective-permute-start(bf16[4,12288]{1,0:T(4,128)(2,1)S(1)} %collective-permute-done.14.refs_7_), channel_id=1, source_target_pairs={{0,4},{2,6},{4,0},{6,2},{8,12},{10,14},{12,8},{14,10},{1,5},{3,7},... | collective-permute-start | bytes 294920 | tf_op jit(solution)/shard_map/ppermute | solution.py:436
  64.3 0.0 collective-permute-start.16
  64.3 0.5 collective-permute-start.17
  64.8 0.0 collective-permute-done.12.refs_5_
  64.8 0.0 collective-permute-start.18
  64.8 3.8 %load_out_weights.3.refs_1_ = bf16[4096,1152]{1,0:T(8,128)(2,1)S(1)} custom-call(bf16[12288,1152]{1,0:T(8,128)(2,1)} %w_out.1, bf16[4,12288]{1,0:T(4,128)(2,1)S(1)} %collective-permute-done.11.refs_1_.refs_6_), custom_call_target="tpu_custom_call" | custom-call | bytes 9437184 | tf_op jit(solution)/shard_map/load_out_weights/pallas_call | solution.py:124
  68.6 0.0 collective-permute-done.13.refs_8_
  68.6 0.6 collective-permute-start.20
  69.2 0.0 collective-permute-done.15.refs_9_
  69.2 0.1 collective-permute-start.21
  69.3 0.0 collective-permute-done.16.refs_10_
  69.3 0.4 collective-permute-start.19
  69.7 0.0 collective-permute-done.17.refs_11_
  69.7 0.1 collective-permute-start.22
  69.8 0.0 collective-permute-done.18.refs_12_
  69.8 0.4 collective-permute-start.23
  70.2 0.0 collective-permute-done.20.refs_14_
  70.2 0.3 collective-permute-done.21.refs_15_
  70.5 0.2 collective-permute-done.19.refs_13_
  70.7 0.4 collective-permute-done.22.refs_16_
  71.0 0.2 collective-permute-done.23.refs_17_
  71.2 7.3 %project_out.1 = bf16[4,16,1152]{2,1,0:T(8,128)(2,1)} custom-call(s32[2]{0:T(128)S(1)} %pad_add_fusion.place, bf16[12288,1152]{1,0:T(8,128)(2,1)} %w_out.1, bf16[4096,1152]{1,0:T(8,128)(2,1)S(1)} %load_out_weights.2.refs_0_, bf16[4096,1152]{1,0:T(8,128)(2,1)S(1)} %load_out_weights.3.refs_1_, bf16[4,12288]{1,0:T(4,128)(2,1)S(1)} %attention.1.refs_1_.refs_2_, ...), custom_call_target="tpu_custom_call" | custom-call | flops 1811939328 | bytes 48758792 | tf_op jit(solution)/shard_map/project_out/pallas_call | solution.py:124
  (3 shorter events, 0.1 us)
Async XLA Ops:
  0.0 0.9 %copy-start = (bf16[4,16,1152]{2,1,0:T(8,128)(2,1)S(1)}, bf16[4,16,1152]{2,1,0:T(8,128)(2,1)}, u32[]{:S(2)}) copy-start(bf16[4,16,1152]{2,1,0:T(8,128)(2,1)} %param.8) | copy-start | bytes 442372
  1.0 1.3 %collective-permute-start = (f32[8,128]{1,0:T(8,128)S(1)}, f32[8,128]{1,0:T(8,128)S(1)}, u32[]{:S(2)}, u32[]{:S(2)}) collective-permute-start(f32[8,128]{1,0:T(8,128)S(1)} %row_sums.1.mine), channel_id=1, source_target_pairs={{0,1},{1,0},{2,3},{3,2},{4,5},{5,4},{6,7},{7,6},{8,9},{9,8},{10,11... | collective-permute-start | bytes 12296 | tf_op jit(solution)/shard_map/ppermute | solution.py:436
  2.4 11.6 %collective-permute-start.1 = (bf16[592,128]{1,0:T(8,128)(2,1)S(1)}, bf16[592,128]{1,0:T(8,128)(2,1)S(1)}, u32[]{:S(2)}, u32[]{:S(2)}) collective-permute-start(bf16[592,128]{1,0:T(8,128)(2,1)S(1)} %payload.1.refs_0_), channel_id=1, source_target_pairs={{0,8},{2,10},{4,12},{6,14},{8,0},{10,2},{12,4},{14,6},{1,9},{3,11}... | collective-permute-start | bytes 454664 | tf_op jit(solution)/shard_map/ppermute | solution.py:436
  6.4 7.8 %collective-permute-start.2 = (bf16[592,128]{1,0:T(8,128)(2,1)S(1)}, bf16[592,128]{1,0:T(8,128)(2,1)S(1)}, u32[]{:S(2)}, u32[]{:S(2)}) collective-permute-start(bf16[592,128]{1,0:T(8,128)(2,1)S(1)} %payload.1.refs_0_), channel_id=1, source_target_pairs={{0,4},{2,6},{4,0},{6,2},{8,12},{10,14},{12,8},{14,10},{1,5},{3,7},... | collective-permute-start | bytes 454664 | tf_op jit(solution)/shard_map/ppermute | solution.py:436
  8.0 6.2 %collective-permute-start.3 = (bf16[592,128]{1,0:T(8,128)(2,1)S(1)}, bf16[592,128]{1,0:T(8,128)(2,1)S(1)}, u32[]{:S(2)}, u32[]{:S(2)}) collective-permute-start(bf16[592,128]{1,0:T(8,128)(2,1)S(1)} %payload.1.refs_0_), channel_id=1, source_target_pairs={{0,2},{2,0},{4,6},{6,4},{8,10},{10,8},{12,14},{14,12},{1,3},{3,1},... | collective-permute-start | bytes 454664 | tf_op jit(solution)/shard_map/ppermute | solution.py:436
  14.2 5.2 %collective-permute-start.4 = (bf16[592,128]{1,0:T(8,128)(2,1)S(1)}, bf16[592,128]{1,0:T(8,128)(2,1)S(1)}, u32[]{:S(2)}, u32[]{:S(2)}) collective-permute-start(bf16[592,128]{1,0:T(8,128)(2,1)S(1)} %collective-permute-done.1.refs_4_), channel_id=1, source_target_pairs={{0,2},{2,0},{4,6},{6,4},{8,10},{10,8},{12,14},{14,12},{1,3},{3,1},... | collective-permute-start | bytes 454664 | tf_op jit(solution)/shard_map/ppermute | solution.py:436
  15.8 13.3 %collective-permute-start.6 = (bf16[592,128]{1,0:T(8,128)(2,1)S(1)}, bf16[592,128]{1,0:T(8,128)(2,1)S(1)}, u32[]{:S(2)}, u32[]{:S(2)}) collective-permute-start(bf16[592,128]{1,0:T(8,128)(2,1)S(1)} %collective-permute-done.1.refs_4_), channel_id=1, source_target_pairs={{0,4},{2,6},{4,0},{6,2},{8,12},{10,14},{12,8},{14,10},{1,5},{3,7},... | collective-permute-start | bytes 454664 | tf_op jit(solution)/shard_map/ppermute | solution.py:436
  19.4 9.7 %collective-permute-start.5 = (bf16[592,128]{1,0:T(8,128)(2,1)S(1)}, bf16[592,128]{1,0:T(8,128)(2,1)S(1)}, u32[]{:S(2)}, u32[]{:S(2)}) collective-permute-start(bf16[592,128]{1,0:T(8,128)(2,1)S(1)} %collective-permute-done.2.refs_2_), channel_id=1, source_target_pairs={{0,2},{2,0},{4,6},{6,4},{8,10},{10,8},{12,14},{14,12},{1,3},{3,1},... | collective-permute-start | bytes 454664 | tf_op jit(solution)/shard_map/ppermute | solution.py:436
  21.0 8.2 %collective-permute-start.7 = (bf16[592,128]{1,0:T(8,128)(2,1)S(1)}, bf16[592,128]{1,0:T(8,128)(2,1)S(1)}, u32[]{:S(2)}, u32[]{:S(2)}) collective-permute-start(bf16[592,128]{1,0:T(8,128)(2,1)S(1)} %collective-permute-done.4.refs_5_), channel_id=1, source_target_pairs={{0,4},{2,6},{4,0},{6,2},{8,12},{10,14},{12,8},{14,10},{1,5},{3,7},... | collective-permute-start | bytes 454664 | tf_op jit(solution)/shard_map/ppermute | solution.py:436
  35.9 1.6 %collective-permute-start.8 = (f32[32,2048]{1,0:T(8,128)S(1)}, f32[32,2048]{1,0:T(8,128)S(1)}, u32[]{:S(2)}, u32[]{:S(2)}) collective-permute-start(f32[32,2048]{1,0:T(8,128)S(1)} %get-tuple-element.26), channel_id=1, source_target_pairs={{0,1},{1,0},{2,3},{3,2},{4,5},{5,4},{6,7},{7,6},{8,9},{9,8},{10,11... | collective-permute-start | bytes 786440 | tf_op jit(solution)/shard_map/ppermute | solution.py:436
  38.3 12.1 %all-to-all-start = ((bf16[8,4,2560]{2,1,0:T(4,128)(2,1)}), bf16[8,4,2560]{2,1,0:T(4,128)(2,1)S(1)}, u32[]{:S(2)}, u32[]{:S(2)}) async-start(bf16[8,4,2560]{2,1,0:T(4,128)(2,1)} %sum_of_cores.1.refs_2_), calls=%async_computation | async-start | bytes 327680 | tf_op jit(solution)/shard_map/all_to_all | solution.py:520
  52.1 6.6 %collective-permute-start.10 = (bf16[4,12288]{1,0:T(4,128)(2,1)S(1)}, bf16[4,12288]{1,0:T(4,128)(2,1)S(1)}, u32[]{:S(2)}, u32[]{:S(2)}) collective-permute-start(bf16[4,12288]{1,0:T(4,128)(2,1)S(1)} %attention.1.refs_1_.refs_2_), channel_id=1, source_target_pairs={{0,4},{2,6},{4,0},{6,2},{8,12},{10,14},{12,8},{14,10},{1,5},{3,7},... | collective-permute-start | bytes 294920 | tf_op jit(solution)/shard_map/ppermute | solution.py:436
  52.2 6.6 %collective-permute-start.11 = (bf16[4,12288]{1,0:T(4,128)(2,1)S(1)}, bf16[4,12288]{1,0:T(4,128)(2,1)S(1)}, u32[]{:S(2)}, u32[]{:S(2)}) collective-permute-start(bf16[4,12288]{1,0:T(4,128)(2,1)S(1)} %attention.1.refs_1_.refs_2_), channel_id=1, source_target_pairs={{0,8},{2,10},{4,12},{6,14},{8,0},{10,2},{12,4},{14,6},{1,9},{3,11}... | collective-permute-start | bytes 294920 | tf_op jit(solution)/shard_map/ppermute | solution.py:436
  53.5 5.2 %collective-permute-start.9 = (bf16[4,12288]{1,0:T(4,128)(2,1)S(1)}, bf16[4,12288]{1,0:T(4,128)(2,1)S(1)}, u32[]{:S(2)}, u32[]{:S(2)}) collective-permute-start(bf16[4,12288]{1,0:T(4,128)(2,1)S(1)} %attention.1.refs_1_.refs_2_), channel_id=1, source_target_pairs={{0,2},{2,0},{4,6},{6,4},{8,10},{10,8},{12,14},{14,12},{1,3},{3,1},... | collective-permute-start | bytes 294920 | tf_op jit(solution)/shard_map/ppermute | solution.py:436
  58.8 4.7 %collective-permute-start.14 = (bf16[4,12288]{1,0:T(4,128)(2,1)S(1)}, bf16[4,12288]{1,0:T(4,128)(2,1)S(1)}, u32[]{:S(2)}, u32[]{:S(2)}) collective-permute-start(bf16[4,12288]{1,0:T(4,128)(2,1)S(1)} %collective-permute-done.11.refs_1_.refs_6_), channel_id=1, source_target_pairs={{0,2},{2,0},{4,6},{6,4},{8,10},{10,8},{12,14},{14,12},{1,3},{3,1},... | collective-permute-start | bytes 294920 | tf_op jit(solution)/shard_map/ppermute | solution.py:436
  60.1 4.8 %collective-permute-start.12 = (bf16[4,12288]{1,0:T(4,128)(2,1)S(1)}, bf16[4,12288]{1,0:T(4,128)(2,1)S(1)}, u32[]{:S(2)}, u32[]{:S(2)}) collective-permute-start(bf16[4,12288]{1,0:T(4,128)(2,1)S(1)} %collective-permute-done.10.refs_4_), channel_id=1, source_target_pairs={{0,2},{2,0},{4,6},{6,4},{8,10},{10,8},{12,14},{14,12},{1,3},{3,1},... | collective-permute-start | bytes 294920 | tf_op jit(solution)/shard_map/ppermute | solution.py:436
  60.8 7.8 %collective-permute-start.13 = (bf16[4,12288]{1,0:T(4,128)(2,1)S(1)}, bf16[4,12288]{1,0:T(4,128)(2,1)S(1)}, u32[]{:S(2)}, u32[]{:S(2)}) collective-permute-start(bf16[4,12288]{1,0:T(4,128)(2,1)S(1)} %collective-permute-done.11.refs_1_.refs_6_), channel_id=1, source_target_pairs={{0,4},{2,6},{4,0},{6,2},{8,12},{10,14},{12,8},{14,10},{1,5},{3,7},... | collective-permute-start | bytes 294920 | tf_op jit(solution)/shard_map/ppermute | solution.py:436
  63.4 5.8 %collective-permute-start.15 = (bf16[4,12288]{1,0:T(4,128)(2,1)S(1)}, bf16[4,12288]{1,0:T(4,128)(2,1)S(1)}, u32[]{:S(2)}, u32[]{:S(2)}) collective-permute-start(bf16[4,12288]{1,0:T(4,128)(2,1)S(1)} %collective-permute-done.14.refs_7_), channel_id=1, source_target_pairs={{0,4},{2,6},{4,0},{6,2},{8,12},{10,14},{12,8},{14,10},{1,5},{3,7},... | collective-permute-start | bytes 294920 | tf_op jit(solution)/shard_map/ppermute | solution.py:436
  64.3 5.0 %collective-permute-start.16 = (bf16[4,12288]{1,0:T(4,128)(2,1)S(1)}, bf16[4,12288]{1,0:T(4,128)(2,1)S(1)}, u32[]{:S(2)}, u32[]{:S(2)}) collective-permute-start(bf16[4,12288]{1,0:T(4,128)(2,1)S(1)} %attention.1.refs_1_.refs_2_), channel_id=1, source_target_pairs={{0,1},{1,0},{2,3},{3,2},{4,5},{5,4},{6,7},{7,6},{8,9},{9,8},{10,11... | collective-permute-start | bytes 294920 | tf_op jit(solution)/shard_map/ppermute | solution.py:436
  64.3 5.4 %collective-permute-start.17 = (bf16[4,12288]{1,0:T(4,128)(2,1)S(1)}, bf16[4,12288]{1,0:T(4,128)(2,1)S(1)}, u32[]{:S(2)}, u32[]{:S(2)}) collective-permute-start(bf16[4,12288]{1,0:T(4,128)(2,1)S(1)} %collective-permute-done.9.refs_3_), channel_id=1, source_target_pairs={{0,1},{1,0},{2,3},{3,2},{4,5},{5,4},{6,7},{7,6},{8,9},{9,8},{10,11... | collective-permute-start | bytes 294920 | tf_op jit(solution)/shard_map/ppermute | solution.py:436
  64.8 5.0 %collective-permute-start.18 = (bf16[4,12288]{1,0:T(4,128)(2,1)S(1)}, bf16[4,12288]{1,0:T(4,128)(2,1)S(1)}, u32[]{:S(2)}, u32[]{:S(2)}) collective-permute-start(bf16[4,12288]{1,0:T(4,128)(2,1)S(1)} %collective-permute-done.10.refs_4_), channel_id=1, source_target_pairs={{0,1},{1,0},{2,3},{3,2},{4,5},{5,4},{6,7},{7,6},{8,9},{9,8},{10,11... | collective-permute-start | bytes 294920 | tf_op jit(solution)/shard_map/ppermute | solution.py:436
  68.6 1.6 %collective-permute-start.20 = (bf16[4,12288]{1,0:T(4,128)(2,1)S(1)}, bf16[4,12288]{1,0:T(4,128)(2,1)S(1)}, u32[]{:S(2)}, u32[]{:S(2)}) collective-permute-start(bf16[4,12288]{1,0:T(4,128)(2,1)S(1)} %collective-permute-done.11.refs_1_.refs_6_), channel_id=1, source_target_pairs={{0,1},{1,0},{2,3},{3,2},{4,5},{5,4},{6,7},{7,6},{8,9},{9,8},{10,11... | collective-permute-start | bytes 294920 | tf_op jit(solution)/shard_map/ppermute | solution.py:436
  69.2 1.3 %collective-permute-start.21 = (bf16[4,12288]{1,0:T(4,128)(2,1)S(1)}, bf16[4,12288]{1,0:T(4,128)(2,1)S(1)}, u32[]{:S(2)}, u32[]{:S(2)}) collective-permute-start(bf16[4,12288]{1,0:T(4,128)(2,1)S(1)} %collective-permute-done.14.refs_7_), channel_id=1, source_target_pairs={{0,1},{1,0},{2,3},{3,2},{4,5},{5,4},{6,7},{7,6},{8,9},{9,8},{10,11... | collective-permute-start | bytes 294920 | tf_op jit(solution)/shard_map/ppermute | solution.py:436
  69.3 1.4 %collective-permute-start.19 = (bf16[4,12288]{1,0:T(4,128)(2,1)S(1)}, bf16[4,12288]{1,0:T(4,128)(2,1)S(1)}, u32[]{:S(2)}, u32[]{:S(2)}) collective-permute-start(bf16[4,12288]{1,0:T(4,128)(2,1)S(1)} %collective-permute-done.12.refs_5_), channel_id=1, source_target_pairs={{0,1},{1,0},{2,3},{3,2},{4,5},{5,4},{6,7},{7,6},{8,9},{9,8},{10,11... | collective-permute-start | bytes 294920 | tf_op jit(solution)/shard_map/ppermute | solution.py:436
  69.7 1.3 %collective-permute-start.22 = (bf16[4,12288]{1,0:T(4,128)(2,1)S(1)}, bf16[4,12288]{1,0:T(4,128)(2,1)S(1)}, u32[]{:S(2)}, u32[]{:S(2)}) collective-permute-start(bf16[4,12288]{1,0:T(4,128)(2,1)S(1)} %collective-permute-done.13.refs_8_), channel_id=1, source_target_pairs={{0,1},{1,0},{2,3},{3,2},{4,5},{5,4},{6,7},{7,6},{8,9},{9,8},{10,11... | collective-permute-start | bytes 294920 | tf_op jit(solution)/shard_map/ppermute | solution.py:436
  69.8 1.4 %collective-permute-start.23 = (bf16[4,12288]{1,0:T(4,128)(2,1)S(1)}, bf16[4,12288]{1,0:T(4,128)(2,1)S(1)}, u32[]{:S(2)}, u32[]{:S(2)}) collective-permute-start(bf16[4,12288]{1,0:T(4,128)(2,1)S(1)} %collective-permute-done.15.refs_9_), channel_id=1, source_target_pairs={{0,1},{1,0},{2,3},{3,2},{4,5},{5,4},{6,7},{7,6},{8,9},{9,8},{10,11... | collective-permute-start | bytes 294920 | tf_op jit(solution)/shard_map/ppermute | solution.py:436

commit v7 on v6

--- a/solution.py
+++ b/solution.py
@@ -112,7 +112,7 @@
 
 MIB = 1 << 20
 EXTRA = 16
-OUT_PIECES = 8
+OUT_CUTS = (4, 7)
 IN_VMEM = pl.BlockSpec(memory_space=pltpu.VMEM)
 IN_SMEM = pl.BlockSpec(memory_space=pltpu.SMEM)
 IN_HBM = pl.BlockSpec(memory_space=pltpu.HBM)
@@ -213,7 +213,7 @@
 
 
 class Stream:
-    def __init__(self, copies, flight=5):
+    def __init__(self, copies, flight=16):
         self.copies, self.started, self.done = copies, 0, 0
         self.start(flight)
 
@@ -284,8 +284,8 @@
                 result[:, span] = product
             else:
                 result[:, span] += product
-            if weights is early and k in (2, 4, 6):
-                stream.take(k // 2 - 1)
+            if weights is early and k in (3, 6):
+                stream.take(k // 3 - 1)
     result[:, columns:] = jnp.dot(normed[0], w_keyval[...], preferred_element_type=jnp.float32)
     half = rows // steps // 2
     for step in range(steps):
@@ -385,42 +385,37 @@
         ].astype(jnp.bfloat16)
 
 
-def output_kernel(steps, place, w_out, *refs):
-    *blocks, out, joined, result, ordered, late, sems = refs
+def output_kernel(steps, depth, place, w_out, *refs):
+    *blocks, out, result, ordered, late, sems = refs
     parts, blocks = [*blocks[:2], late], blocks[2:]
     wide_at, narrow_at = place[0], place[1]
     batch = len(blocks)
     count = batch // 2
-    deep, depth = late.shape[0], joined.shape[1]
-    piece = deep // OUT_PIECES
+    pieces = sems.shape[0]
+    size = late.shape[0] // pieces
     stream = Stream(
         [
             pltpu.make_async_copy(
-                w_out.at[pl.ds(2 * deep + at * piece, piece)],
-                late.at[pl.ds(at * piece, piece)],
+                w_out.at[pl.ds(w_out.shape[0] - late.shape[0] + at * size, size)],
+                late.at[pl.ds(at * size, size)],
                 sems.at[at],
             )
-            for at in range(OUT_PIECES)
+            for at in range(pieces)
         ]
     )
-    for at in range(0, 3 * deep, depth):
-        for k, block in enumerate(blocks):
-            joined[k * steps : (k + 1) * steps, :] = block[:, at : at + depth].astype(jnp.float32)
-        rows = joined[...].astype(jnp.bfloat16)
-        inside = at % deep
-        if at >= 2 * deep:
-            stream.take((inside + depth) // piece - 1)
-        product = jnp.dot(
-            rows,
-            parts[at // deep][inside : inside + depth, :],
-            preferred_element_type=jnp.float32,
-        )
-        if at == 0:
+    chunks = [(part, at) for part in parts for at in range(0, part.shape[0], depth)]
+    for index, (part, inside) in enumerate(chunks):
+        span = slice(index * depth, (index + 1) * depth)
+        rows = jnp.concatenate([block[:, span] for block in blocks], axis=0)
+        if part is late:
+            stream.take((inside + depth) // size - 1)
+        product = jnp.dot(rows, part[inside : inside + depth, :], preferred_element_type=jnp.float32)
+        if index == 0:
             result[...] = product
         else:
             result[...] += product
-        if at in (3 * depth, 5 * depth, 7 * depth):
-            stream.take(at // depth // 2 - 1)
+        if index in (3, 5):
+            stream.take(index // 2 - 1)
     for core in range(2):
         for k in range(count):
             sequence = jnp.bitwise_xor(narrow_at, core) * count + jnp.bitwise_xor(wide_at, k)
@@ -544,30 +539,33 @@
         limit=16 * MIB,
         flops=4 * steps * H * size * slots,
     )
-    deep = w_out.shape[0] // 3
-    contexts, early_weights = gather_contexts(
-        context,
-        lambda at, block: load(
+    depth = w_out.shape[0] // 12
+    bounds = (0, OUT_CUTS[0] * depth, OUT_CUTS[1] * depth, w_out.shape[0])
+
+    def load_out(at, block):
+        size = bounds[at + 1] - bounds[at]
+        return load(
             "load_out_weights",
-            (deep, w_out.shape[1]),
-            boxes(pl.ds(at * deep, deep), pl.ds(0, w_out.shape[1]), 8),
+            (size, w_out.shape[1]),
+            boxes(pl.ds(bounds[at], size), pl.ds(0, w_out.shape[1]), 8),
             w_out,
             after=[block],
-        ),
-    )
+        )
+
+    contexts, early_weights = gather_contexts(context, load_out)
+    deep = bounds[3] - bounds[2]
     contexts = contexts + [swap(block, "narrow", 1) for block in contexts]
     return call(
-        functools.partial(output_kernel, steps),
+        functools.partial(output_kernel, steps, depth),
         "project_out",
         jax.ShapeDtypeStruct((steps, batch, w_out.shape[1]), bf16),
         [place, in_hbm(w_out), *early_weights, *contexts],
         in_specs=[IN_SMEM, IN_HBM] + [IN_VMEM] * (2 + batch),
         scratch=[
-            pltpu.VMEM((rows, deep // 4), f32),
             pltpu.VMEM((rows, w_out.shape[1]), f32),
             pltpu.VMEM((rows, w_out.shape[1]), f32),
             pltpu.VMEM((deep, w_out.shape[1]), bf16),
-            pltpu.SemaphoreType.DMA((OUT_PIECES,)),
+            pltpu.SemaphoreType.DMA((deep // depth * 2,)),
         ],
         limit=28 * MIB,
         flops=2 * rows * w_out.size,

time: 78.9 us -> 77.4 us (0.981)
  Pallas kernels: 32.6 us -> 31.2 us
    pallas_call x10, Pallas kernels: 32.6 us -> 31.2 us  [call(): pl.pallas_call(kernel, out_shape=out_shape, in_specs=in_specs or [IN_VMEM...]
where the time goes in v7:
time: 77.4 us; the launch traced here: 77.1 us
  Pallas kernels  31.2 us (40%)
  starting transfers between devices  26.7 us (34%)
  waiting for transfers between devices  16.7 us (22%)
  local copies, waits for them, and re-layouts  1.6 us (2%)
  between operations  0.78 us (1%)
    pallas_call x10, Pallas kernels, call(): pl.pallas_call(kernel, out_shape=out_shape, in_specs=in_specs or [IN_VMEM...  31.2 us
    ppermute x24, starting transfers between devices, swap(): return lax.ppermute(value, axis, [(at, at ^ bits) for at in range(size)])  22.4 us
    ppermute x24, waiting for transfers between devices, swap(): return lax.ppermute(value, axis, [(at, at ^ bits) for at in range(size)])  10.7 us
    all_to_all x1, waiting for transfers between devices, local_fast(): arrived = lax.all_to_all(outgoing, 'wide', 0, 0, tiled=True)  6.07 us
    all_to_all x1, starting transfers between devices, local_fast(): arrived = lax.all_to_all(outgoing, 'wide', 0, 0, tiled=True)  4.29 us
  transfers between devices with their start and end apart: 25, of which 11 were waited for; matrix products, arithmetic and copies ran while one was open for 1% of the time, Pallas kernels for 20%

profile of v7, /device:TPU:0, one launch (start us, length us, event | category | flops | bytes accessed | tf_op | source)
XLA Modules:
  0.0 77.1 jit_solution(5443832122819428432)
XLA Ops:
  0.0 0.0 copy-start
  0.0 0.9 %copy-done = bf16[4,16,1152]{2,1,0:T(8,128)(2,1)S(1)} copy-done((bf16[4,16,1152]{2,1,0:T(8,128)(2,1)S(1)}, bf16[4,16,1152]{2,1,0:T(8,128)(2,1)}, u32[]{:S(2)}) %copy-start) | copy-done | bytes 147480
  0.9 0.1 row_sums.1.mine
  1.0 0.5 collective-permute-start
  1.6 0.7 broadcast_in_dim.2.gain
  2.2 0.1 collective-permute-done.theirs
  2.4 4.0 %collective-permute-start.1 = (bf16[592,128]{1,0:T(8,128)(2,1)S(1)}, bf16[592,128]{1,0:T(8,128)(2,1)S(1)}, u32[]{:S(2)}, u32[]{:S(2)}) collective-permute-start(bf16[592,128]{1,0:T(8,128)(2,1)S(1)} %payload.1.refs_0_), channel_id=1, source_target_pairs={{0,8},{2,10},{4,12},{6,14},{8,0},{10,2},{12,4},{14,6},{1,9},{3,11}... | collective-permute-start | bytes 454664 | tf_op jit(solution)/shard_map/ppermute | solution.py:431
  6.4 1.6 %collective-permute-start.2 = (bf16[592,128]{1,0:T(8,128)(2,1)S(1)}, bf16[592,128]{1,0:T(8,128)(2,1)S(1)}, u32[]{:S(2)}, u32[]{:S(2)}) collective-permute-start(bf16[592,128]{1,0:T(8,128)(2,1)S(1)} %payload.1.refs_0_), channel_id=1, source_target_pairs={{0,4},{2,6},{4,0},{6,2},{8,12},{10,14},{12,8},{14,10},{1,5},{3,7},... | collective-permute-start | bytes 454664 | tf_op jit(solution)/shard_map/ppermute | solution.py:431
  8.0 1.5 %collective-permute-start.3 = (bf16[592,128]{1,0:T(8,128)(2,1)S(1)}, bf16[592,128]{1,0:T(8,128)(2,1)S(1)}, u32[]{:S(2)}, u32[]{:S(2)}) collective-permute-start(bf16[592,128]{1,0:T(8,128)(2,1)S(1)} %payload.1.refs_0_), channel_id=1, source_target_pairs={{0,2},{2,0},{4,6},{6,4},{8,10},{10,8},{12,14},{14,12},{1,3},{3,1},... | collective-permute-start | bytes 454664 | tf_op jit(solution)/shard_map/ppermute | solution.py:431
  9.5 4.6 %collective-permute-done.1.refs_4_ = bf16[592,128]{1,0:T(8,128)(2,1)S(1)} collective-permute-done((bf16[592,128]{1,0:T(8,128)(2,1)S(1)}, bf16[592,128]{1,0:T(8,128)(2,1)S(1)}, u32[]{:S(2)}, u32[]{:S(2)}) %collective-permute-start.1) | collective-permute-done | bytes 151584 | tf_op jit(solution)/shard_map/ppermute | solution.py:431
  14.0 0.2 collective-permute-done.2.refs_2_
  14.2 0.0 collective-permute-done.3.refs_1_
  14.2 1.5 %collective-permute-start.4 = (bf16[592,128]{1,0:T(8,128)(2,1)S(1)}, bf16[592,128]{1,0:T(8,128)(2,1)S(1)}, u32[]{:S(2)}, u32[]{:S(2)}) collective-permute-start(bf16[592,128]{1,0:T(8,128)(2,1)S(1)} %collective-permute-done.1.refs_4_), channel_id=1, source_target_pairs={{0,2},{2,0},{4,6},{6,4},{8,10},{10,8},{12,14},{14,12},{1,3},{3,1},... | collective-permute-start | bytes 454664 | tf_op jit(solution)/shard_map/ppermute | solution.py:431
  15.8 1.4 %collective-permute-start.6 = (bf16[592,128]{1,0:T(8,128)(2,1)S(1)}, bf16[592,128]{1,0:T(8,128)(2,1)S(1)}, u32[]{:S(2)}, u32[]{:S(2)}) collective-permute-start(bf16[592,128]{1,0:T(8,128)(2,1)S(1)} %collective-permute-done.1.refs_4_), channel_id=1, source_target_pairs={{0,4},{2,6},{4,0},{6,2},{8,12},{10,14},{12,8},{14,10},{1,5},{3,7},... | collective-permute-start | bytes 454664 | tf_op jit(solution)/shard_map/ppermute | solution.py:431
  17.2 2.2 %collective-permute-done.4.refs_5_ = bf16[592,128]{1,0:T(8,128)(2,1)S(1)} collective-permute-done((bf16[592,128]{1,0:T(8,128)(2,1)S(1)}, bf16[592,128]{1,0:T(8,128)(2,1)S(1)}, u32[]{:S(2)}, u32[]{:S(2)}) %collective-permute-start.4) | collective-permute-done | bytes 151584 | tf_op jit(solution)/shard_map/ppermute | solution.py:431
  19.4 1.5 %collective-permute-start.5 = (bf16[592,128]{1,0:T(8,128)(2,1)S(1)}, bf16[592,128]{1,0:T(8,128)(2,1)S(1)}, u32[]{:S(2)}, u32[]{:S(2)}) collective-permute-start(bf16[592,128]{1,0:T(8,128)(2,1)S(1)} %collective-permute-done.2.refs_2_), channel_id=1, source_target_pairs={{0,2},{2,0},{4,6},{6,4},{8,10},{10,8},{12,14},{14,12},{1,3},{3,1},... | collective-permute-start | bytes 454664 | tf_op jit(solution)/shard_map/ppermute | solution.py:431
  21.0 1.4 %collective-permute-start.7 = (bf16[592,128]{1,0:T(8,128)(2,1)S(1)}, bf16[592,128]{1,0:T(8,128)(2,1)S(1)}, u32[]{:S(2)}, u32[]{:S(2)}) collective-permute-start(bf16[592,128]{1,0:T(8,128)(2,1)S(1)} %collective-permute-done.4.refs_5_), channel_id=1, source_target_pairs={{0,4},{2,6},{4,0},{6,2},{8,12},{10,14},{12,8},{14,10},{1,5},{3,7},... | collective-permute-start | bytes 454664 | tf_op jit(solution)/shard_map/ppermute | solution.py:431
  22.4 6.6 %load_query_weights.1.early = bf16[9216,1024]{1,0:T(8,128)(2,1)S(1)} custom-call(bf16[9216,1536]{1,0:T(8,128)(2,1)} %w_query.1), custom_call_target="tpu_custom_call" | custom-call | bytes 18874368 | tf_op jit(solution)/shard_map/load_query_weights/pallas_call | solution.py:124
  29.0 0.1 pad_add_fusion.place
  29.1 0.0 collective-permute-done.6.refs_6_
  29.1 0.0 collective-permute-done.5.refs_3_
  29.1 0.0 collective-permute-done.7.refs_7_
  29.1 6.2 %norm_and_project.1 = (f32[32,2048]{1,0:T(8,128)S(1)}, f32[32,2048]{1,0:T(8,128)S(1)}) custom-call(s32[2]{0:T(128)S(1)} %pad_add_fusion.place, bf16[1152,512]{1,0:T(8,128)(2,1)} %w_keyval_far.1, bf16[9216,1536]{1,0:T(8,128)(2,1)} %w_query.1, bf16[9216,1024]{1,0:T(8,128)(2,1)S(1)} %load_query_weights.1.early, bf16[592,128]{1,0:T(8,128)(2,1)S(1)} %payload.1.refs_0_, ...), custom_call_target="tpu_custom_call" | custom-call | flops 1811939328 | bytes 49577992 | tf_op jit(solution)/shard_map/norm_and_project/pallas_call | solution.py:124
  35.3 0.1 collective-permute-start.8
  36.1 0.9 %collective-permute-done.8.theirs = f32[32,2048]{1,0:T(8,128)S(1)} collective-permute-done((f32[32,2048]{1,0:T(8,128)S(1)}, f32[32,2048]{1,0:T(8,128)S(1)}, u32[]{:S(2)}, u32[]{:S(2)}) %collective-permute-start.8) | collective-permute-done | bytes 262176 | tf_op jit(solution)/shard_map/ppermute | solution.py:431
  36.9 0.8 %sum_of_cores.1.refs_2_ = bf16[8,4,2560]{2,1,0:T(4,128)(2,1)} custom-call(f32[32,2048]{1,0:T(8,128)S(1)} %get-tuple-element.25.mine, f32[32,2048]{1,0:T(8,128)S(1)} %collective-permute-done.8.theirs), custom_call_target="tpu_custom_call" | custom-call | bytes 524288 | tf_op jit(solution)/shard_map/sum_of_cores/pallas_call | solution.py:124
  37.7 4.3 %all-to-all-start = ((bf16[8,4,2560]{2,1,0:T(4,128)(2,1)}), bf16[8,4,2560]{2,1,0:T(4,128)(2,1)S(1)}, u32[]{:S(2)}, u32[]{:S(2)}) async-start(bf16[8,4,2560]{2,1,0:T(4,128)(2,1)} %sum_of_cores.1.refs_2_), calls=%async_computation | async-start | bytes 327680 | tf_op jit(solution)/shard_map/all_to_all | solution.py:515
  42.0 0.1 multiply_sine_fusion
  42.1 1.6 %load_cache.1.cache = bf16[4096,256]{1,0:T(8,128)(2,1)S(1)} custom-call(bf16[2048,256]{1,0:T(8,128)(2,1)} %bitcast.9, bf16[2048,256]{1,0:T(8,128)(2,1)} %bitcast.10, bf16[8,4,2560]{2,1,0:T(4,128)(2,1)} %sum_of_cores.1.refs_2_), custom_call_target="tpu_custom_call" | custom-call | bytes 2097152 | tf_op jit(solution)/shard_map/load_cache/pallas_call | solution.py:124
  43.7 6.1 %all-to-all-done.arrived = bf16[8,4,2560]{2,1,0:T(4,128)(2,1)S(1)} async-done(((bf16[8,4,2560]{2,1,0:T(4,128)(2,1)}), bf16[8,4,2560]{2,1,0:T(4,128)(2,1)S(1)}, u32[]{:S(2)}, u32[]{:S(2)}) %all-to-all-start) | async-done | bytes 163872 | tf_op jit(solution)/shard_map/all_to_all | solution.py:515
  49.8 1.7 %attention.1.refs_1_.refs_2_ = bf16[4,12288]{1,0:T(4,128)(2,1)S(1)} custom-call(s32[1]{0:T(128)} %copy.9.length, f32[4,128]{1,0:T(4,128)S(1)} %get-tuple-element.36.cosine, f32[4,128]{1,0:T(4,128)S(1)} %get-tuple-element.35.sine, bf16[8,4,2560]{2,1,0:T(4,128)(2,1)S(1)} %all-to-all-done.arrived, bf16[4096,256]{1,0:T(8,128)(2,1)S(1)} %load_cache.1.cache), custom_call_target="tpu_custom_call" | custom-call | flops 402653184 | bytes 2265092 | tf_op jit(solution)/shard_map/attention/pallas_call | solution.py:124
  51.5 0.1 collective-permute-start.10
  51.6 1.3 %collective-permute-start.11 = (bf16[4,12288]{1,0:T(4,128)(2,1)S(1)}, bf16[4,12288]{1,0:T(4,128)(2,1)S(1)}, u32[]{:S(2)}, u32[]{:S(2)}) collective-permute-start(bf16[4,12288]{1,0:T(4,128)(2,1)S(1)} %attention.1.refs_1_.refs_2_), channel_id=1, source_target_pairs={{0,8},{2,10},{4,12},{6,14},{8,0},{10,2},{12,4},{14,6},{1,9},{3,11}... | collective-permute-start | bytes 294920 | tf_op jit(solution)/shard_map/ppermute | solution.py:431
  52.9 1.4 %collective-permute-start.9 = (bf16[4,12288]{1,0:T(4,128)(2,1)S(1)}, bf16[4,12288]{1,0:T(4,128)(2,1)S(1)}, u32[]{:S(2)}, u32[]{:S(2)}) collective-permute-start(bf16[4,12288]{1,0:T(4,128)(2,1)S(1)} %attention.1.refs_1_.refs_2_), channel_id=1, source_target_pairs={{0,2},{2,0},{4,6},{6,4},{8,10},{10,8},{12,14},{14,12},{1,3},{3,1},... | collective-permute-start | bytes 294920 | tf_op jit(solution)/shard_map/ppermute | solution.py:431
  54.3 3.8 %load_out_weights.2.refs_0_ = bf16[4096,1152]{1,0:T(8,128)(2,1)S(1)} custom-call(bf16[12288,1152]{1,0:T(8,128)(2,1)} %w_out.1, bf16[4,12288]{1,0:T(4,128)(2,1)S(1)} %attention.1.refs_1_.refs_2_), custom_call_target="tpu_custom_call" | custom-call | bytes 9437184 | tf_op jit(solution)/shard_map/load_out_weights/pallas_call | solution.py:124
  58.1 0.0 collective-permute-done.10.refs_4_
  58.1 0.0 collective-permute-done.11.refs_1_.refs_6_
  58.1 0.0 collective-permute-done.9.refs_3_
  58.2 1.3 %collective-permute-start.14 = (bf16[4,12288]{1,0:T(4,128)(2,1)S(1)}, bf16[4,12288]{1,0:T(4,128)(2,1)S(1)}, u32[]{:S(2)}, u32[]{:S(2)}) collective-permute-start(bf16[4,12288]{1,0:T(4,128)(2,1)S(1)} %collective-permute-done.11.refs_1_.refs_6_), channel_id=1, source_target_pairs={{0,2},{2,0},{4,6},{6,4},{8,10},{10,8},{12,14},{14,12},{1,3},{3,1},... | collective-permute-start | bytes 294920 | tf_op jit(solution)/shard_map/ppermute | solution.py:431
  59.5 0.8 %collective-permute-start.12 = (bf16[4,12288]{1,0:T(4,128)(2,1)S(1)}, bf16[4,12288]{1,0:T(4,128)(2,1)S(1)}, u32[]{:S(2)}, u32[]{:S(2)}) collective-permute-start(bf16[4,12288]{1,0:T(4,128)(2,1)S(1)} %collective-permute-done.10.refs_4_), channel_id=1, source_target_pairs={{0,2},{2,0},{4,6},{6,4},{8,10},{10,8},{12,14},{14,12},{1,3},{3,1},... | collective-permute-start | bytes 294920 | tf_op jit(solution)/shard_map/ppermute | solution.py:431
  60.2 0.9 %collective-permute-start.13 = (bf16[4,12288]{1,0:T(4,128)(2,1)S(1)}, bf16[4,12288]{1,0:T(4,128)(2,1)S(1)}, u32[]{:S(2)}, u32[]{:S(2)}) collective-permute-start(bf16[4,12288]{1,0:T(4,128)(2,1)S(1)} %collective-permute-done.11.refs_1_.refs_6_), channel_id=1, source_target_pairs={{0,4},{2,6},{4,0},{6,2},{8,12},{10,14},{12,8},{14,10},{1,5},{3,7},... | collective-permute-start | bytes 294920 | tf_op jit(solution)/shard_map/ppermute | solution.py:431
  61.1 1.7 %collective-permute-done.14.refs_7_ = bf16[4,12288]{1,0:T(4,128)(2,1)S(1)} collective-permute-done((bf16[4,12288]{1,0:T(4,128)(2,1)S(1)}, bf16[4,12288]{1,0:T(4,128)(2,1)S(1)}, u32[]{:S(2)}, u32[]{:S(2)}) %collective-permute-start.14) | collective-permute-done | bytes 98336 | tf_op jit(solution)/shard_map/ppermute | solution.py:431
  62.8 0.9 %collective-permute-start.15 = (bf16[4,12288]{1,0:T(4,128)(2,1)S(1)}, bf16[4,12288]{1,0:T(4,128)(2,1)S(1)}, u32[]{:S(2)}, u32[]{:S(2)}) collective-permute-start(bf16[4,12288]{1,0:T(4,128)(2,1)S(1)} %collective-permute-done.14.refs_7_), channel_id=1, source_target_pairs={{0,4},{2,6},{4,0},{6,2},{8,12},{10,14},{12,8},{14,10},{1,5},{3,7},... | collective-permute-start | bytes 294920 | tf_op jit(solution)/shard_map/ppermute | solution.py:431
  63.7 0.0 collective-permute-start.16
  63.7 0.5 collective-permute-start.17
  64.2 0.0 collective-permute-done.12.refs_5_
  64.2 0.0 collective-permute-start.18
  64.2 3.1 %load_out_weights.3.refs_1_ = bf16[3072,1152]{1,0:T(8,128)(2,1)S(1)} custom-call(bf16[12288,1152]{1,0:T(8,128)(2,1)} %w_out.1, bf16[4,12288]{1,0:T(4,128)(2,1)S(1)} %collective-permute-done.11.refs_1_.refs_6_), custom_call_target="tpu_custom_call" | custom-call | bytes 7077888 | tf_op jit(solution)/shard_map/load_out_weights/pallas_call | solution.py:124
  67.3 0.0 collective-permute-done.13.refs_8_
  67.3 0.6 collective-permute-start.20
  67.9 0.0 collective-permute-done.15.refs_9_
  67.9 0.1 collective-permute-start.21
  68.0 0.0 collective-permute-done.16.refs_10_
  68.0 0.4 collective-permute-start.19
  68.4 0.0 collective-permute-done.17.refs_11_
  68.4 0.1 collective-permute-start.22
  68.5 0.0 collective-permute-done.18.refs_12_
  68.5 0.4 collective-permute-start.23
  68.9 0.0 collective-permute-done.20.refs_14_
  68.9 0.3 collective-permute-done.21.refs_15_
  69.2 0.2 collective-permute-done.19.refs_13_
  69.4 0.4 collective-permute-done.22.refs_16_
  69.7 0.2 collective-permute-done.23.refs_17_
  69.9 7.2 %project_out.1 = bf16[4,16,1152]{2,1,0:T(8,128)(2,1)} custom-call(s32[2]{0:T(128)S(1)} %pad_add_fusion.place, bf16[12288,1152]{1,0:T(8,128)(2,1)} %w_out.1, bf16[4096,1152]{1,0:T(8,128)(2,1)S(1)} %load_out_weights.2.refs_0_, bf16[3072,1152]{1,0:T(8,128)(2,1)S(1)} %load_out_weights.3.refs_1_, bf16[4,12288]{1,0:T(4,128)(2,1)S(1)} %attention.1.refs_1_.refs_2_, ...), custom_call_target="tpu_custom_call" | custom-call | flops 1811939328 | bytes 46399496 | tf_op jit(solution)/shard_map/project_out/pallas_call | solution.py:124
  (3 shorter events, 0.1 us)
Async XLA Ops:
  0.0 0.9 %copy-start = (bf16[4,16,1152]{2,1,0:T(8,128)(2,1)S(1)}, bf16[4,16,1152]{2,1,0:T(8,128)(2,1)}, u32[]{:S(2)}) copy-start(bf16[4,16,1152]{2,1,0:T(8,128)(2,1)} %param.8) | copy-start | bytes 442372
  1.0 1.3 %collective-permute-start = (f32[8,128]{1,0:T(8,128)S(1)}, f32[8,128]{1,0:T(8,128)S(1)}, u32[]{:S(2)}, u32[]{:S(2)}) collective-permute-start(f32[8,128]{1,0:T(8,128)S(1)} %row_sums.1.mine), channel_id=1, source_target_pairs={{0,1},{1,0},{2,3},{3,2},{4,5},{5,4},{6,7},{7,6},{8,9},{9,8},{10,11... | collective-permute-start | bytes 12296 | tf_op jit(solution)/shard_map/ppermute | solution.py:431
  2.4 11.6 %collective-permute-start.1 = (bf16[592,128]{1,0:T(8,128)(2,1)S(1)}, bf16[592,128]{1,0:T(8,128)(2,1)S(1)}, u32[]{:S(2)}, u32[]{:S(2)}) collective-permute-start(bf16[592,128]{1,0:T(8,128)(2,1)S(1)} %payload.1.refs_0_), channel_id=1, source_target_pairs={{0,8},{2,10},{4,12},{6,14},{8,0},{10,2},{12,4},{14,6},{1,9},{3,11}... | collective-permute-start | bytes 454664 | tf_op jit(solution)/shard_map/ppermute | solution.py:431
  6.4 7.8 %collective-permute-start.2 = (bf16[592,128]{1,0:T(8,128)(2,1)S(1)}, bf16[592,128]{1,0:T(8,128)(2,1)S(1)}, u32[]{:S(2)}, u32[]{:S(2)}) collective-permute-start(bf16[592,128]{1,0:T(8,128)(2,1)S(1)} %payload.1.refs_0_), channel_id=1, source_target_pairs={{0,4},{2,6},{4,0},{6,2},{8,12},{10,14},{12,8},{14,10},{1,5},{3,7},... | collective-permute-start | bytes 454664 | tf_op jit(solution)/shard_map/ppermute | solution.py:431
  8.0 6.2 %collective-permute-start.3 = (bf16[592,128]{1,0:T(8,128)(2,1)S(1)}, bf16[592,128]{1,0:T(8,128)(2,1)S(1)}, u32[]{:S(2)}, u32[]{:S(2)}) collective-permute-start(bf16[592,128]{1,0:T(8,128)(2,1)S(1)} %payload.1.refs_0_), channel_id=1, source_target_pairs={{0,2},{2,0},{4,6},{6,4},{8,10},{10,8},{12,14},{14,12},{1,3},{3,1},... | collective-permute-start | bytes 454664 | tf_op jit(solution)/shard_map/ppermute | solution.py:431
  14.2 5.2 %collective-permute-start.4 = (bf16[592,128]{1,0:T(8,128)(2,1)S(1)}, bf16[592,128]{1,0:T(8,128)(2,1)S(1)}, u32[]{:S(2)}, u32[]{:S(2)}) collective-permute-start(bf16[592,128]{1,0:T(8,128)(2,1)S(1)} %collective-permute-done.1.refs_4_), channel_id=1, source_target_pairs={{0,2},{2,0},{4,6},{6,4},{8,10},{10,8},{12,14},{14,12},{1,3},{3,1},... | collective-permute-start | bytes 454664 | tf_op jit(solution)/shard_map/ppermute | solution.py:431
  15.8 13.3 %collective-permute-start.6 = (bf16[592,128]{1,0:T(8,128)(2,1)S(1)}, bf16[592,128]{1,0:T(8,128)(2,1)S(1)}, u32[]{:S(2)}, u32[]{:S(2)}) collective-permute-start(bf16[592,128]{1,0:T(8,128)(2,1)S(1)} %collective-permute-done.1.refs_4_), channel_id=1, source_target_pairs={{0,4},{2,6},{4,0},{6,2},{8,12},{10,14},{12,8},{14,10},{1,5},{3,7},... | collective-permute-start | bytes 454664 | tf_op jit(solution)/shard_map/ppermute | solution.py:431
  19.4 9.7 %collective-permute-start.5 = (bf16[592,128]{1,0:T(8,128)(2,1)S(1)}, bf16[592,128]{1,0:T(8,128)(2,1)S(1)}, u32[]{:S(2)}, u32[]{:S(2)}) collective-permute-start(bf16[592,128]{1,0:T(8,128)(2,1)S(1)} %collective-permute-done.2.refs_2_), channel_id=1, source_target_pairs={{0,2},{2,0},{4,6},{6,4},{8,10},{10,8},{12,14},{14,12},{1,3},{3,1},... | collective-permute-start | bytes 454664 | tf_op jit(solution)/shard_map/ppermute | solution.py:431
  21.0 8.2 %collective-permute-start.7 = (bf16[592,128]{1,0:T(8,128)(2,1)S(1)}, bf16[592,128]{1,0:T(8,128)(2,1)S(1)}, u32[]{:S(2)}, u32[]{:S(2)}) collective-permute-start(bf16[592,128]{1,0:T(8,128)(2,1)S(1)} %collective-permute-done.4.refs_5_), channel_id=1, source_target_pairs={{0,4},{2,6},{4,0},{6,2},{8,12},{10,14},{12,8},{14,10},{1,5},{3,7},... | collective-permute-start | bytes 454664 | tf_op jit(solution)/shard_map/ppermute | solution.py:431
  35.3 1.6 %collective-permute-start.8 = (f32[32,2048]{1,0:T(8,128)S(1)}, f32[32,2048]{1,0:T(8,128)S(1)}, u32[]{:S(2)}, u32[]{:S(2)}) collective-permute-start(f32[32,2048]{1,0:T(8,128)S(1)} %get-tuple-element.26), channel_id=1, source_target_pairs={{0,1},{1,0},{2,3},{3,2},{4,5},{5,4},{6,7},{7,6},{8,9},{9,8},{10,11... | collective-permute-start | bytes 786440 | tf_op jit(solution)/shard_map/ppermute | solution.py:431
  37.7 12.1 %all-to-all-start = ((bf16[8,4,2560]{2,1,0:T(4,128)(2,1)}), bf16[8,4,2560]{2,1,0:T(4,128)(2,1)S(1)}, u32[]{:S(2)}, u32[]{:S(2)}) async-start(bf16[8,4,2560]{2,1,0:T(4,128)(2,1)} %sum_of_cores.1.refs_2_), calls=%async_computation | async-start | bytes 327680 | tf_op jit(solution)/shard_map/all_to_all | solution.py:515
  51.5 6.6 %collective-permute-start.10 = (bf16[4,12288]{1,0:T(4,128)(2,1)S(1)}, bf16[4,12288]{1,0:T(4,128)(2,1)S(1)}, u32[]{:S(2)}, u32[]{:S(2)}) collective-permute-start(bf16[4,12288]{1,0:T(4,128)(2,1)S(1)} %attention.1.refs_1_.refs_2_), channel_id=1, source_target_pairs={{0,4},{2,6},{4,0},{6,2},{8,12},{10,14},{12,8},{14,10},{1,5},{3,7},... | collective-permute-start | bytes 294920 | tf_op jit(solution)/shard_map/ppermute | solution.py:431
  51.6 6.6 %collective-permute-start.11 = (bf16[4,12288]{1,0:T(4,128)(2,1)S(1)}, bf16[4,12288]{1,0:T(4,128)(2,1)S(1)}, u32[]{:S(2)}, u32[]{:S(2)}) collective-permute-start(bf16[4,12288]{1,0:T(4,128)(2,1)S(1)} %attention.1.refs_1_.refs_2_), channel_id=1, source_target_pairs={{0,8},{2,10},{4,12},{6,14},{8,0},{10,2},{12,4},{14,6},{1,9},{3,11}... | collective-permute-start | bytes 294920 | tf_op jit(solution)/shard_map/ppermute | solution.py:431
  52.9 5.2 %collective-permute-start.9 = (bf16[4,12288]{1,0:T(4,128)(2,1)S(1)}, bf16[4,12288]{1,0:T(4,128)(2,1)S(1)}, u32[]{:S(2)}, u32[]{:S(2)}) collective-permute-start(bf16[4,12288]{1,0:T(4,128)(2,1)S(1)} %attention.1.refs_1_.refs_2_), channel_id=1, source_target_pairs={{0,2},{2,0},{4,6},{6,4},{8,10},{10,8},{12,14},{14,12},{1,3},{3,1},... | collective-permute-start | bytes 294920 | tf_op jit(solution)/shard_map/ppermute | solution.py:431
  58.2 4.7 %collective-permute-start.14 = (bf16[4,12288]{1,0:T(4,128)(2,1)S(1)}, bf16[4,12288]{1,0:T(4,128)(2,1)S(1)}, u32[]{:S(2)}, u32[]{:S(2)}) collective-permute-start(bf16[4,12288]{1,0:T(4,128)(2,1)S(1)} %collective-permute-done.11.refs_1_.refs_6_), channel_id=1, source_target_pairs={{0,2},{2,0},{4,6},{6,4},{8,10},{10,8},{12,14},{14,12},{1,3},{3,1},... | collective-permute-start | bytes 294920 | tf_op jit(solution)/shard_map/ppermute | solution.py:431
  59.5 4.8 %collective-permute-start.12 = (bf16[4,12288]{1,0:T(4,128)(2,1)S(1)}, bf16[4,12288]{1,0:T(4,128)(2,1)S(1)}, u32[]{:S(2)}, u32[]{:S(2)}) collective-permute-start(bf16[4,12288]{1,0:T(4,128)(2,1)S(1)} %collective-permute-done.10.refs_4_), channel_id=1, source_target_pairs={{0,2},{2,0},{4,6},{6,4},{8,10},{10,8},{12,14},{14,12},{1,3},{3,1},... | collective-permute-start | bytes 294920 | tf_op jit(solution)/shard_map/ppermute | solution.py:431
  60.2 7.1 %collective-permute-start.13 = (bf16[4,12288]{1,0:T(4,128)(2,1)S(1)}, bf16[4,12288]{1,0:T(4,128)(2,1)S(1)}, u32[]{:S(2)}, u32[]{:S(2)}) collective-permute-start(bf16[4,12288]{1,0:T(4,128)(2,1)S(1)} %collective-permute-done.11.refs_1_.refs_6_), channel_id=1, source_target_pairs={{0,4},{2,6},{4,0},{6,2},{8,12},{10,14},{12,8},{14,10},{1,5},{3,7},... | collective-permute-start | bytes 294920 | tf_op jit(solution)/shard_map/ppermute | solution.py:431
  62.8 5.1 %collective-permute-start.15 = (bf16[4,12288]{1,0:T(4,128)(2,1)S(1)}, bf16[4,12288]{1,0:T(4,128)(2,1)S(1)}, u32[]{:S(2)}, u32[]{:S(2)}) collective-permute-start(bf16[4,12288]{1,0:T(4,128)(2,1)S(1)} %collective-permute-done.14.refs_7_), channel_id=1, source_target_pairs={{0,4},{2,6},{4,0},{6,2},{8,12},{10,14},{12,8},{14,10},{1,5},{3,7},... | collective-permute-start | bytes 294920 | tf_op jit(solution)/shard_map/ppermute | solution.py:431
  63.7 4.3 %collective-permute-start.16 = (bf16[4,12288]{1,0:T(4,128)(2,1)S(1)}, bf16[4,12288]{1,0:T(4,128)(2,1)S(1)}, u32[]{:S(2)}, u32[]{:S(2)}) collective-permute-start(bf16[4,12288]{1,0:T(4,128)(2,1)S(1)} %attention.1.refs_1_.refs_2_), channel_id=1, source_target_pairs={{0,1},{1,0},{2,3},{3,2},{4,5},{5,4},{6,7},{7,6},{8,9},{9,8},{10,11... | collective-permute-start | bytes 294920 | tf_op jit(solution)/shard_map/ppermute | solution.py:431
  63.7 4.7 %collective-permute-start.17 = (bf16[4,12288]{1,0:T(4,128)(2,1)S(1)}, bf16[4,12288]{1,0:T(4,128)(2,1)S(1)}, u32[]{:S(2)}, u32[]{:S(2)}) collective-permute-start(bf16[4,12288]{1,0:T(4,128)(2,1)S(1)} %collective-permute-done.9.refs_3_), channel_id=1, source_target_pairs={{0,1},{1,0},{2,3},{3,2},{4,5},{5,4},{6,7},{7,6},{8,9},{9,8},{10,11... | collective-permute-start | bytes 294920 | tf_op jit(solution)/shard_map/ppermute | solution.py:431
  64.2 4.3 %collective-permute-start.18 = (bf16[4,12288]{1,0:T(4,128)(2,1)S(1)}, bf16[4,12288]{1,0:T(4,128)(2,1)S(1)}, u32[]{:S(2)}, u32[]{:S(2)}) collective-permute-start(bf16[4,12288]{1,0:T(4,128)(2,1)S(1)} %collective-permute-done.10.refs_4_), channel_id=1, source_target_pairs={{0,1},{1,0},{2,3},{3,2},{4,5},{5,4},{6,7},{7,6},{8,9},{9,8},{10,11... | collective-permute-start | bytes 294920 | tf_op jit(solution)/shard_map/ppermute | solution.py:431
  67.3 1.6 %collective-permute-start.20 = (bf16[4,12288]{1,0:T(4,128)(2,1)S(1)}, bf16[4,12288]{1,0:T(4,128)(2,1)S(1)}, u32[]{:S(2)}, u32[]{:S(2)}) collective-permute-start(bf16[4,12288]{1,0:T(4,128)(2,1)S(1)} %collective-permute-done.11.refs_1_.refs_6_), channel_id=1, source_target_pairs={{0,1},{1,0},{2,3},{3,2},{4,5},{5,4},{6,7},{7,6},{8,9},{9,8},{10,11... | collective-permute-start | bytes 294920 | tf_op jit(solution)/shard_map/ppermute | solution.py:431
  67.9 1.3 %collective-permute-start.21 = (bf16[4,12288]{1,0:T(4,128)(2,1)S(1)}, bf16[4,12288]{1,0:T(4,128)(2,1)S(1)}, u32[]{:S(2)}, u32[]{:S(2)}) collective-permute-start(bf16[4,12288]{1,0:T(4,128)(2,1)S(1)} %collective-permute-done.14.refs_7_), channel_id=1, source_target_pairs={{0,1},{1,0},{2,3},{3,2},{4,5},{5,4},{6,7},{7,6},{8,9},{9,8},{10,11... | collective-permute-start | bytes 294920 | tf_op jit(solution)/shard_map/ppermute | solution.py:431
  68.0 1.4 %collective-permute-start.19 = (bf16[4,12288]{1,0:T(4,128)(2,1)S(1)}, bf16[4,12288]{1,0:T(4,128)(2,1)S(1)}, u32[]{:S(2)}, u32[]{:S(2)}) collective-permute-start(bf16[4,12288]{1,0:T(4,128)(2,1)S(1)} %collective-permute-done.12.refs_5_), channel_id=1, source_target_pairs={{0,1},{1,0},{2,3},{3,2},{4,5},{5,4},{6,7},{7,6},{8,9},{9,8},{10,11... | collective-permute-start | bytes 294920 | tf_op jit(solution)/shard_map/ppermute | solution.py:431
  68.4 1.3 %collective-permute-start.22 = (bf16[4,12288]{1,0:T(4,128)(2,1)S(1)}, bf16[4,12288]{1,0:T(4,128)(2,1)S(1)}, u32[]{:S(2)}, u32[]{:S(2)}) collective-permute-start(bf16[4,12288]{1,0:T(4,128)(2,1)S(1)} %collective-permute-done.13.refs_8_), channel_id=1, source_target_pairs={{0,1},{1,0},{2,3},{3,2},{4,5},{5,4},{6,7},{7,6},{8,9},{9,8},{10,11... | collective-permute-start | bytes 294920 | tf_op jit(solution)/shard_map/ppermute | solution.py:431
  68.5 1.4 %collective-permute-start.23 = (bf16[4,12288]{1,0:T(4,128)(2,1)S(1)}, bf16[4,12288]{1,0:T(4,128)(2,1)S(1)}, u32[]{:S(2)}, u32[]{:S(2)}) collective-permute-start(bf16[4,12288]{1,0:T(4,128)(2,1)S(1)} %collective-permute-done.15.refs_9_), channel_id=1, source_target_pairs={{0,1},{1,0},{2,3},{3,2},{4,5},{5,4},{6,7},{7,6},{8,9},{9,8},{10,11... | collective-permute-start | bytes 294920 | tf_op jit(solution)/shard_map/ppermute | solution.py:431

commit v8 on v7

--- a/solution.py
+++ b/solution.py
@@ -449,7 +449,7 @@
     for bits in (4, 2, 1):
         near[bits] = swap(block, "wide", bits)
     first = loader(0, block)
-    near[1], near[2], near[4], first = lax.optimization_barrier((near[1], near[2], near[4], first))
+    near[2], near[4], near[1], first = lax.optimization_barrier((near[2], near[4], near[1], first))
     near[6] = swap(near[4], "wide", 2)
     near[5] = swap(near[4], "wide", 1)
     near[3] = swap(near[2], "wide", 1)
@@ -486,7 +486,7 @@
     early_weights = load(
         "load_query_weights",
         (deep, part),
-        boxes(pl.ds(0, deep), pl.ds(0, part), 8),
+        boxes(pl.ds(0, deep), pl.ds(0, part), 4),
         w_query,
     )
     keep, send = call(
@@ -547,7 +547,7 @@
         return load(
             "load_out_weights",
             (size, w_out.shape[1]),
-            boxes(pl.ds(bounds[at], size), pl.ds(0, w_out.shape[1]), 8),
+            boxes(pl.ds(bounds[at], size), pl.ds(0, w_out.shape[1]), 4),
             w_out,
             after=[block],
         )

time: 77.4 us -> 77.3 us (level)
  starting transfers between devices: 26.7 us -> 25.9 us
  transfers between devices with their start and end apart: 25 -> 25, of which waited for: 11 -> 12; matrix products, arithmetic and copies ran while one was open for 1% -> 1% of each run, Pallas kernels for 20% -> 20%
where the time goes in v8:
time: 77.3 us; the launch traced here: 77 us
  Pallas kernels  31.2 us (40%)
  starting transfers between devices  25.9 us (34%)
  waiting for transfers between devices  17.4 us (23%)
  local copies, waits for them, and re-layouts  1.6 us (2%)
    pallas_call x10, Pallas kernels, call(): pl.pallas_call(kernel, out_shape=out_shape, in_specs=in_specs or [IN_VMEM...  31.2 us
    ppermute x24, starting transfers between devices, swap(): return lax.ppermute(value, axis, [(at, at ^ bits) for at in range(size)])  21.6 us
    ppermute x24, waiting for transfers between devices, swap(): return lax.ppermute(value, axis, [(at, at ^ bits) for at in range(size)])  11.3 us
    all_to_all x1, waiting for transfers between devices, local_fast(): arrived = lax.all_to_all(outgoing, 'wide', 0, 0, tiled=True)  6.07 us
    all_to_all x1, starting transfers between devices, local_fast(): arrived = lax.all_to_all(outgoing, 'wide', 0, 0, tiled=True)  4.29 us
  transfers between devices with their start and end apart: 25, of which 12 were waited for; matrix products, arithmetic and copies ran while one was open for 1% of the time, Pallas kernels for 20%

profile of v8, /device:TPU:0, one launch (start us, length us, event | category | flops | bytes accessed | tf_op | source)
XLA Modules:
  0.0 77.0 jit_solution(98067492084674031)
XLA Ops:
  0.0 0.0 copy-start
  0.0 0.9 %copy-done = bf16[4,16,1152]{2,1,0:T(8,128)(2,1)S(1)} copy-done((bf16[4,16,1152]{2,1,0:T(8,128)(2,1)S(1)}, bf16[4,16,1152]{2,1,0:T(8,128)(2,1)}, u32[]{:S(2)}) %copy-start) | copy-done | bytes 147480
  0.9 0.1 row_sums.1.mine
  1.0 0.5 collective-permute-start
  1.6 0.7 broadcast_in_dim.2.gain
  2.2 0.1 collective-permute-done.theirs
  2.4 4.0 %collective-permute-start.1 = (bf16[592,128]{1,0:T(8,128)(2,1)S(1)}, bf16[592,128]{1,0:T(8,128)(2,1)S(1)}, u32[]{:S(2)}, u32[]{:S(2)}) collective-permute-start(bf16[592,128]{1,0:T(8,128)(2,1)S(1)} %payload.1.refs_0_), channel_id=1, source_target_pairs={{0,8},{2,10},{4,12},{6,14},{8,0},{10,2},{12,4},{14,6},{1,9},{3,11}... | collective-permute-start | bytes 454664 | tf_op jit(solution)/shard_map/ppermute | solution.py:431
  6.4 1.6 %collective-permute-start.2 = (bf16[592,128]{1,0:T(8,128)(2,1)S(1)}, bf16[592,128]{1,0:T(8,128)(2,1)S(1)}, u32[]{:S(2)}, u32[]{:S(2)}) collective-permute-start(bf16[592,128]{1,0:T(8,128)(2,1)S(1)} %payload.1.refs_0_), channel_id=1, source_target_pairs={{0,4},{2,6},{4,0},{6,2},{8,12},{10,14},{12,8},{14,10},{1,5},{3,7},... | collective-permute-start | bytes 454664 | tf_op jit(solution)/shard_map/ppermute | solution.py:431
  8.0 1.5 %collective-permute-start.3 = (bf16[592,128]{1,0:T(8,128)(2,1)S(1)}, bf16[592,128]{1,0:T(8,128)(2,1)S(1)}, u32[]{:S(2)}, u32[]{:S(2)}) collective-permute-start(bf16[592,128]{1,0:T(8,128)(2,1)S(1)} %payload.1.refs_0_), channel_id=1, source_target_pairs={{0,2},{2,0},{4,6},{6,4},{8,10},{10,8},{12,14},{14,12},{1,3},{3,1},... | collective-permute-start | bytes 454664 | tf_op jit(solution)/shard_map/ppermute | solution.py:431
  9.5 4.6 %collective-permute-done.1.refs_4_ = bf16[592,128]{1,0:T(8,128)(2,1)S(1)} collective-permute-done((bf16[592,128]{1,0:T(8,128)(2,1)S(1)}, bf16[592,128]{1,0:T(8,128)(2,1)S(1)}, u32[]{:S(2)}, u32[]{:S(2)}) %collective-permute-start.1) | collective-permute-done | bytes 151584 | tf_op jit(solution)/shard_map/ppermute | solution.py:431
  14.0 0.2 collective-permute-done.2.refs_2_
  14.2 0.0 collective-permute-done.3.refs_1_
  14.2 1.5 %collective-permute-start.4 = (bf16[592,128]{1,0:T(8,128)(2,1)S(1)}, bf16[592,128]{1,0:T(8,128)(2,1)S(1)}, u32[]{:S(2)}, u32[]{:S(2)}) collective-permute-start(bf16[592,128]{1,0:T(8,128)(2,1)S(1)} %collective-permute-done.1.refs_4_), channel_id=1, source_target_pairs={{0,2},{2,0},{4,6},{6,4},{8,10},{10,8},{12,14},{14,12},{1,3},{3,1},... | collective-permute-start | bytes 454664 | tf_op jit(solution)/shard_map/ppermute | solution.py:431
  15.8 1.4 %collective-permute-start.6 = (bf16[592,128]{1,0:T(8,128)(2,1)S(1)}, bf16[592,128]{1,0:T(8,128)(2,1)S(1)}, u32[]{:S(2)}, u32[]{:S(2)}) collective-permute-start(bf16[592,128]{1,0:T(8,128)(2,1)S(1)} %collective-permute-done.1.refs_4_), channel_id=1, source_target_pairs={{0,4},{2,6},{4,0},{6,2},{8,12},{10,14},{12,8},{14,10},{1,5},{3,7},... | collective-permute-start | bytes 454664 | tf_op jit(solution)/shard_map/ppermute | solution.py:431
  17.2 2.2 %collective-permute-done.4.refs_5_ = bf16[592,128]{1,0:T(8,128)(2,1)S(1)} collective-permute-done((bf16[592,128]{1,0:T(8,128)(2,1)S(1)}, bf16[592,128]{1,0:T(8,128)(2,1)S(1)}, u32[]{:S(2)}, u32[]{:S(2)}) %collective-permute-start.4) | collective-permute-done | bytes 151584 | tf_op jit(solution)/shard_map/ppermute | solution.py:431
  19.4 1.5 %collective-permute-start.5 = (bf16[592,128]{1,0:T(8,128)(2,1)S(1)}, bf16[592,128]{1,0:T(8,128)(2,1)S(1)}, u32[]{:S(2)}, u32[]{:S(2)}) collective-permute-start(bf16[592,128]{1,0:T(8,128)(2,1)S(1)} %collective-permute-done.2.refs_2_), channel_id=1, source_target_pairs={{0,2},{2,0},{4,6},{6,4},{8,10},{10,8},{12,14},{14,12},{1,3},{3,1},... | collective-permute-start | bytes 454664 | tf_op jit(solution)/shard_map/ppermute | solution.py:431
  21.0 1.4 %collective-permute-start.7 = (bf16[592,128]{1,0:T(8,128)(2,1)S(1)}, bf16[592,128]{1,0:T(8,128)(2,1)S(1)}, u32[]{:S(2)}, u32[]{:S(2)}) collective-permute-start(bf16[592,128]{1,0:T(8,128)(2,1)S(1)} %collective-permute-done.4.refs_5_), channel_id=1, source_target_pairs={{0,4},{2,6},{4,0},{6,2},{8,12},{10,14},{12,8},{14,10},{1,5},{3,7},... | collective-permute-start | bytes 454664 | tf_op jit(solution)/shard_map/ppermute | solution.py:431
  22.4 6.6 %load_query_weights.1.early = bf16[9216,1024]{1,0:T(8,128)(2,1)S(1)} custom-call(bf16[9216,1536]{1,0:T(8,128)(2,1)} %w_query.1), custom_call_target="tpu_custom_call" | custom-call | bytes 18874368 | tf_op jit(solution)/shard_map/load_query_weights/pallas_call | solution.py:124
  29.0 0.1 pad_add_fusion.place
  29.1 0.0 collective-permute-done.6.refs_6_
  29.1 0.0 collective-permute-done.5.refs_3_
  29.1 0.0 collective-permute-done.7.refs_7_
  29.1 6.2 %norm_and_project.1 = (f32[32,2048]{1,0:T(8,128)S(1)}, f32[32,2048]{1,0:T(8,128)S(1)}) custom-call(s32[2]{0:T(128)S(1)} %pad_add_fusion.place, bf16[1152,512]{1,0:T(8,128)(2,1)} %w_keyval_far.1, bf16[9216,1536]{1,0:T(8,128)(2,1)} %w_query.1, bf16[9216,1024]{1,0:T(8,128)(2,1)S(1)} %load_query_weights.1.early, bf16[592,128]{1,0:T(8,128)(2,1)S(1)} %payload.1.refs_0_, ...), custom_call_target="tpu_custom_call" | custom-call | flops 1811939328 | bytes 49577992 | tf_op jit(solution)/shard_map/norm_and_project/pallas_call | solution.py:124
  35.3 0.1 collective-permute-start.8
  36.0 0.9 %collective-permute-done.8.theirs = f32[32,2048]{1,0:T(8,128)S(1)} collective-permute-done((f32[32,2048]{1,0:T(8,128)S(1)}, f32[32,2048]{1,0:T(8,128)S(1)}, u32[]{:S(2)}, u32[]{:S(2)}) %collective-permute-start.8) | collective-permute-done | bytes 262176 | tf_op jit(solution)/shard_map/ppermute | solution.py:431
  36.9 0.8 %sum_of_cores.1.refs_2_ = bf16[8,4,2560]{2,1,0:T(4,128)(2,1)} custom-call(f32[32,2048]{1,0:T(8,128)S(1)} %get-tuple-element.25.mine, f32[32,2048]{1,0:T(8,128)S(1)} %collective-permute-done.8.theirs), custom_call_target="tpu_custom_call" | custom-call | bytes 524288 | tf_op jit(solution)/shard_map/sum_of_cores/pallas_call | solution.py:124
  37.7 4.3 %all-to-all-start = ((bf16[8,4,2560]{2,1,0:T(4,128)(2,1)}), bf16[8,4,2560]{2,1,0:T(4,128)(2,1)S(1)}, u32[]{:S(2)}, u32[]{:S(2)}) async-start(bf16[8,4,2560]{2,1,0:T(4,128)(2,1)} %sum_of_cores.1.refs_2_), calls=%async_computation | async-start | bytes 327680 | tf_op jit(solution)/shard_map/all_to_all | solution.py:515
  42.0 0.1 multiply_sine_fusion
  42.1 1.6 %load_cache.1.cache = bf16[4096,256]{1,0:T(8,128)(2,1)S(1)} custom-call(bf16[2048,256]{1,0:T(8,128)(2,1)} %bitcast.9, bf16[2048,256]{1,0:T(8,128)(2,1)} %bitcast.10, bf16[8,4,2560]{2,1,0:T(4,128)(2,1)} %sum_of_cores.1.refs_2_), custom_call_target="tpu_custom_call" | custom-call | bytes 2097152 | tf_op jit(solution)/shard_map/load_cache/pallas_call | solution.py:124
  43.7 6.1 %all-to-all-done.arrived = bf16[8,4,2560]{2,1,0:T(4,128)(2,1)S(1)} async-done(((bf16[8,4,2560]{2,1,0:T(4,128)(2,1)}), bf16[8,4,2560]{2,1,0:T(4,128)(2,1)S(1)}, u32[]{:S(2)}, u32[]{:S(2)}) %all-to-all-start) | async-done | bytes 163872 | tf_op jit(solution)/shard_map/all_to_all | solution.py:515
  49.7 1.7 %attention.1.refs_1_.refs_2_ = bf16[4,12288]{1,0:T(4,128)(2,1)S(1)} custom-call(s32[1]{0:T(128)} %copy.9.length, f32[4,128]{1,0:T(4,128)S(1)} %get-tuple-element.36.cosine, f32[4,128]{1,0:T(4,128)S(1)} %get-tuple-element.35.sine, bf16[8,4,2560]{2,1,0:T(4,128)(2,1)S(1)} %all-to-all-done.arrived, bf16[4096,256]{1,0:T(8,128)(2,1)S(1)} %load_cache.1.cache), custom_call_target="tpu_custom_call" | custom-call | flops 402653184 | bytes 2265092 | tf_op jit(solution)/shard_map/attention/pallas_call | solution.py:124
  51.4 0.6 collective-permute-start.10
  52.1 0.3 collective-permute-start.11
  52.4 1.9 %collective-permute-start.9 = (bf16[4,12288]{1,0:T(4,128)(2,1)S(1)}, bf16[4,12288]{1,0:T(4,128)(2,1)S(1)}, u32[]{:S(2)}, u32[]{:S(2)}) collective-permute-start(bf16[4,12288]{1,0:T(4,128)(2,1)S(1)} %attention.1.refs_1_.refs_2_), channel_id=1, source_target_pairs={{0,4},{2,6},{4,0},{6,2},{8,12},{10,14},{12,8},{14,10},{1,5},{3,7},... | collective-permute-start | bytes 294920 | tf_op jit(solution)/shard_map/ppermute | solution.py:431
  54.3 3.8 %load_out_weights.2.refs_0_ = bf16[4096,1152]{1,0:T(8,128)(2,1)S(1)} custom-call(bf16[12288,1152]{1,0:T(8,128)(2,1)} %w_out.1, bf16[4,12288]{1,0:T(4,128)(2,1)S(1)} %attention.1.refs_1_.refs_2_), custom_call_target="tpu_custom_call" | custom-call | bytes 9437184 | tf_op jit(solution)/shard_map/load_out_weights/pallas_call | solution.py:124
  58.1 0.0 collective-permute-done.10.refs_1_.refs_6_
  58.1 0.0 collective-permute-done.11.refs_3_
  58.1 0.3 collective-permute-done.9.refs_4_
  58.4 0.5 collective-permute-start.14
  58.9 1.5 %collective-permute-start.12 = (bf16[4,12288]{1,0:T(4,128)(2,1)S(1)}, bf16[4,12288]{1,0:T(4,128)(2,1)S(1)}, u32[]{:S(2)}, u32[]{:S(2)}) collective-permute-start(bf16[4,12288]{1,0:T(4,128)(2,1)S(1)} %collective-permute-done.9.refs_4_), channel_id=1, source_target_pairs={{0,2},{2,0},{4,6},{6,4},{8,10},{10,8},{12,14},{14,12},{1,3},{3,1},... | collective-permute-start | bytes 294920 | tf_op jit(solution)/shard_map/ppermute | solution.py:431
  60.4 0.5 collective-permute-start.13
  60.9 2.1 %collective-permute-done.14.refs_7_ = bf16[4,12288]{1,0:T(4,128)(2,1)S(1)} collective-permute-done((bf16[4,12288]{1,0:T(4,128)(2,1)S(1)}, bf16[4,12288]{1,0:T(4,128)(2,1)S(1)}, u32[]{:S(2)}, u32[]{:S(2)}) %collective-permute-start.14) | collective-permute-done | bytes 98336 | tf_op jit(solution)/shard_map/ppermute | solution.py:431
  63.0 0.5 collective-permute-start.15
  63.5 0.0 collective-permute-start.16
  63.5 0.5 collective-permute-start.17
  64.0 0.0 collective-permute-done.12.refs_5_
  64.1 0.0 collective-permute-start.18
  64.1 3.1 %load_out_weights.3.refs_1_ = bf16[3072,1152]{1,0:T(8,128)(2,1)S(1)} custom-call(bf16[12288,1152]{1,0:T(8,128)(2,1)} %w_out.1, bf16[4,12288]{1,0:T(4,128)(2,1)S(1)} %collective-permute-done.10.refs_1_.refs_6_), custom_call_target="tpu_custom_call" | custom-call | bytes 7077888 | tf_op jit(solution)/shard_map/load_out_weights/pallas_call | solution.py:124
  67.2 0.0 collective-permute-done.13.refs_8_
  67.2 0.6 collective-permute-start.20
  67.8 0.0 collective-permute-done.15.refs_9_
  67.8 0.1 collective-permute-start.21
  67.9 0.0 collective-permute-done.16.refs_10_
  67.9 0.4 collective-permute-start.19
  68.3 0.0 collective-permute-done.17.refs_11_
  68.3 0.1 collective-permute-start.22
  68.4 0.0 collective-permute-done.18.refs_12_
  68.4 0.4 collective-permute-start.23
  68.8 0.0 collective-permute-done.20.refs_14_
  68.8 0.3 collective-permute-done.21.refs_15_
  69.1 0.2 collective-permute-done.19.refs_13_
  69.2 0.4 collective-permute-done.22.refs_16_
  69.6 0.2 collective-permute-done.23.refs_17_
  69.7 7.2 %project_out.1 = bf16[4,16,1152]{2,1,0:T(8,128)(2,1)} custom-call(s32[2]{0:T(128)S(1)} %pad_add_fusion.place, bf16[12288,1152]{1,0:T(8,128)(2,1)} %w_out.1, bf16[4096,1152]{1,0:T(8,128)(2,1)S(1)} %load_out_weights.2.refs_0_, bf16[3072,1152]{1,0:T(8,128)(2,1)S(1)} %load_out_weights.3.refs_1_, bf16[4,12288]{1,0:T(4,128)(2,1)S(1)} %attention.1.refs_1_.refs_2_, ...), custom_call_target="tpu_custom_call" | custom-call | flops 1811939328 | bytes 46399496 | tf_op jit(solution)/shard_map/project_out/pallas_call | solution.py:124
  (3 shorter events, 0.1 us)
Async XLA Ops:
  0.0 0.9 %copy-start = (bf16[4,16,1152]{2,1,0:T(8,128)(2,1)S(1)}, bf16[4,16,1152]{2,1,0:T(8,128)(2,1)}, u32[]{:S(2)}) copy-start(bf16[4,16,1152]{2,1,0:T(8,128)(2,1)} %param.8) | copy-start | bytes 442372
  1.0 1.3 %collective-permute-start = (f32[8,128]{1,0:T(8,128)S(1)}, f32[8,128]{1,0:T(8,128)S(1)}, u32[]{:S(2)}, u32[]{:S(2)}) collective-permute-start(f32[8,128]{1,0:T(8,128)S(1)} %row_sums.1.mine), channel_id=1, source_target_pairs={{0,1},{1,0},{2,3},{3,2},{4,5},{5,4},{6,7},{7,6},{8,9},{9,8},{10,11... | collective-permute-start | bytes 12296 | tf_op jit(solution)/shard_map/ppermute | solution.py:431
  2.4 11.6 %collective-permute-start.1 = (bf16[592,128]{1,0:T(8,128)(2,1)S(1)}, bf16[592,128]{1,0:T(8,128)(2,1)S(1)}, u32[]{:S(2)}, u32[]{:S(2)}) collective-permute-start(bf16[592,128]{1,0:T(8,128)(2,1)S(1)} %payload.1.refs_0_), channel_id=1, source_target_pairs={{0,8},{2,10},{4,12},{6,14},{8,0},{10,2},{12,4},{14,6},{1,9},{3,11}... | collective-permute-start | bytes 454664 | tf_op jit(solution)/shard_map/ppermute | solution.py:431
  6.4 7.8 %collective-permute-start.2 = (bf16[592,128]{1,0:T(8,128)(2,1)S(1)}, bf16[592,128]{1,0:T(8,128)(2,1)S(1)}, u32[]{:S(2)}, u32[]{:S(2)}) collective-permute-start(bf16[592,128]{1,0:T(8,128)(2,1)S(1)} %payload.1.refs_0_), channel_id=1, source_target_pairs={{0,4},{2,6},{4,0},{6,2},{8,12},{10,14},{12,8},{14,10},{1,5},{3,7},... | collective-permute-start | bytes 454664 | tf_op jit(solution)/shard_map/ppermute | solution.py:431
  8.0 6.2 %collective-permute-start.3 = (bf16[592,128]{1,0:T(8,128)(2,1)S(1)}, bf16[592,128]{1,0:T(8,128)(2,1)S(1)}, u32[]{:S(2)}, u32[]{:S(2)}) collective-permute-start(bf16[592,128]{1,0:T(8,128)(2,1)S(1)} %payload.1.refs_0_), channel_id=1, source_target_pairs={{0,2},{2,0},{4,6},{6,4},{8,10},{10,8},{12,14},{14,12},{1,3},{3,1},... | collective-permute-start | bytes 454664 | tf_op jit(solution)/shard_map/ppermute | solution.py:431
  14.2 5.2 %collective-permute-start.4 = (bf16[592,128]{1,0:T(8,128)(2,1)S(1)}, bf16[592,128]{1,0:T(8,128)(2,1)S(1)}, u32[]{:S(2)}, u32[]{:S(2)}) collective-permute-start(bf16[592,128]{1,0:T(8,128)(2,1)S(1)} %collective-permute-done.1.refs_4_), channel_id=1, source_target_pairs={{0,2},{2,0},{4,6},{6,4},{8,10},{10,8},{12,14},{14,12},{1,3},{3,1},... | collective-permute-start | bytes 454664 | tf_op jit(solution)/shard_map/ppermute | solution.py:431
  15.8 13.3 %collective-permute-start.6 = (bf16[592,128]{1,0:T(8,128)(2,1)S(1)}, bf16[592,128]{1,0:T(8,128)(2,1)S(1)}, u32[]{:S(2)}, u32[]{:S(2)}) collective-permute-start(bf16[592,128]{1,0:T(8,128)(2,1)S(1)} %collective-permute-done.1.refs_4_), channel_id=1, source_target_pairs={{0,4},{2,6},{4,0},{6,2},{8,12},{10,14},{12,8},{14,10},{1,5},{3,7},... | collective-permute-start | bytes 454664 | tf_op jit(solution)/shard_map/ppermute | solution.py:431
  19.4 9.7 %collective-permute-start.5 = (bf16[592,128]{1,0:T(8,128)(2,1)S(1)}, bf16[592,128]{1,0:T(8,128)(2,1)S(1)}, u32[]{:S(2)}, u32[]{:S(2)}) collective-permute-start(bf16[592,128]{1,0:T(8,128)(2,1)S(1)} %collective-permute-done.2.refs_2_), channel_id=1, source_target_pairs={{0,2},{2,0},{4,6},{6,4},{8,10},{10,8},{12,14},{14,12},{1,3},{3,1},... | collective-permute-start | bytes 454664 | tf_op jit(solution)/shard_map/ppermute | solution.py:431
  21.0 8.1 %collective-permute-start.7 = (bf16[592,128]{1,0:T(8,128)(2,1)S(1)}, bf16[592,128]{1,0:T(8,128)(2,1)S(1)}, u32[]{:S(2)}, u32[]{:S(2)}) collective-permute-start(bf16[592,128]{1,0:T(8,128)(2,1)S(1)} %collective-permute-done.4.refs_5_), channel_id=1, source_target_pairs={{0,4},{2,6},{4,0},{6,2},{8,12},{10,14},{12,8},{14,10},{1,5},{3,7},... | collective-permute-start | bytes 454664 | tf_op jit(solution)/shard_map/ppermute | solution.py:431
  35.3 1.6 %collective-permute-start.8 = (f32[32,2048]{1,0:T(8,128)S(1)}, f32[32,2048]{1,0:T(8,128)S(1)}, u32[]{:S(2)}, u32[]{:S(2)}) collective-permute-start(f32[32,2048]{1,0:T(8,128)S(1)} %get-tuple-element.26), channel_id=1, source_target_pairs={{0,1},{1,0},{2,3},{3,2},{4,5},{5,4},{6,7},{7,6},{8,9},{9,8},{10,11... | collective-permute-start | bytes 786440 | tf_op jit(solution)/shard_map/ppermute | solution.py:431
  37.7 12.1 %all-to-all-start = ((bf16[8,4,2560]{2,1,0:T(4,128)(2,1)}), bf16[8,4,2560]{2,1,0:T(4,128)(2,1)S(1)}, u32[]{:S(2)}, u32[]{:S(2)}) async-start(bf16[8,4,2560]{2,1,0:T(4,128)(2,1)} %sum_of_cores.1.refs_2_), calls=%async_computation | async-start | bytes 327680 | tf_op jit(solution)/shard_map/all_to_all | solution.py:515
  51.4 6.7 %collective-permute-start.10 = (bf16[4,12288]{1,0:T(4,128)(2,1)S(1)}, bf16[4,12288]{1,0:T(4,128)(2,1)S(1)}, u32[]{:S(2)}, u32[]{:S(2)}) collective-permute-start(bf16[4,12288]{1,0:T(4,128)(2,1)S(1)} %attention.1.refs_1_.refs_2_), channel_id=1, source_target_pairs={{0,8},{2,10},{4,12},{6,14},{8,0},{10,2},{12,4},{14,6},{1,9},{3,11}... | collective-permute-start | bytes 294920 | tf_op jit(solution)/shard_map/ppermute | solution.py:431
  52.1 6.0 %collective-permute-start.11 = (bf16[4,12288]{1,0:T(4,128)(2,1)S(1)}, bf16[4,12288]{1,0:T(4,128)(2,1)S(1)}, u32[]{:S(2)}, u32[]{:S(2)}) collective-permute-start(bf16[4,12288]{1,0:T(4,128)(2,1)S(1)} %attention.1.refs_1_.refs_2_), channel_id=1, source_target_pairs={{0,2},{2,0},{4,6},{6,4},{8,10},{10,8},{12,14},{14,12},{1,3},{3,1},... | collective-permute-start | bytes 294920 | tf_op jit(solution)/shard_map/ppermute | solution.py:431
  52.4 6.0 %collective-permute-start.9 = (bf16[4,12288]{1,0:T(4,128)(2,1)S(1)}, bf16[4,12288]{1,0:T(4,128)(2,1)S(1)}, u32[]{:S(2)}, u32[]{:S(2)}) collective-permute-start(bf16[4,12288]{1,0:T(4,128)(2,1)S(1)} %attention.1.refs_1_.refs_2_), channel_id=1, source_target_pairs={{0,4},{2,6},{4,0},{6,2},{8,12},{10,14},{12,8},{14,10},{1,5},{3,7},... | collective-permute-start | bytes 294920 | tf_op jit(solution)/shard_map/ppermute | solution.py:431
  58.4 4.6 %collective-permute-start.14 = (bf16[4,12288]{1,0:T(4,128)(2,1)S(1)}, bf16[4,12288]{1,0:T(4,128)(2,1)S(1)}, u32[]{:S(2)}, u32[]{:S(2)}) collective-permute-start(bf16[4,12288]{1,0:T(4,128)(2,1)S(1)} %collective-permute-done.10.refs_1_.refs_6_), channel_id=1, source_target_pairs={{0,2},{2,0},{4,6},{6,4},{8,10},{10,8},{12,14},{14,12},{1,3},{3,1},... | collective-permute-start | bytes 294920 | tf_op jit(solution)/shard_map/ppermute | solution.py:431
  58.9 5.2 %collective-permute-start.12 = (bf16[4,12288]{1,0:T(4,128)(2,1)S(1)}, bf16[4,12288]{1,0:T(4,128)(2,1)S(1)}, u32[]{:S(2)}, u32[]{:S(2)}) collective-permute-start(bf16[4,12288]{1,0:T(4,128)(2,1)S(1)} %collective-permute-done.9.refs_4_), channel_id=1, source_target_pairs={{0,2},{2,0},{4,6},{6,4},{8,10},{10,8},{12,14},{14,12},{1,3},{3,1},... | collective-permute-start | bytes 294920 | tf_op jit(solution)/shard_map/ppermute | solution.py:431
  60.4 6.8 %collective-permute-start.13 = (bf16[4,12288]{1,0:T(4,128)(2,1)S(1)}, bf16[4,12288]{1,0:T(4,128)(2,1)S(1)}, u32[]{:S(2)}, u32[]{:S(2)}) collective-permute-start(bf16[4,12288]{1,0:T(4,128)(2,1)S(1)} %collective-permute-done.10.refs_1_.refs_6_), channel_id=1, source_target_pairs={{0,4},{2,6},{4,0},{6,2},{8,12},{10,14},{12,8},{14,10},{1,5},{3,7},... | collective-permute-start | bytes 294920 | tf_op jit(solution)/shard_map/ppermute | solution.py:431
  63.0 4.8 %collective-permute-start.15 = (bf16[4,12288]{1,0:T(4,128)(2,1)S(1)}, bf16[4,12288]{1,0:T(4,128)(2,1)S(1)}, u32[]{:S(2)}, u32[]{:S(2)}) collective-permute-start(bf16[4,12288]{1,0:T(4,128)(2,1)S(1)} %collective-permute-done.14.refs_7_), channel_id=1, source_target_pairs={{0,4},{2,6},{4,0},{6,2},{8,12},{10,14},{12,8},{14,10},{1,5},{3,7},... | collective-permute-start | bytes 294920 | tf_op jit(solution)/shard_map/ppermute | solution.py:431
  63.5 4.3 %collective-permute-start.16 = (bf16[4,12288]{1,0:T(4,128)(2,1)S(1)}, bf16[4,12288]{1,0:T(4,128)(2,1)S(1)}, u32[]{:S(2)}, u32[]{:S(2)}) collective-permute-start(bf16[4,12288]{1,0:T(4,128)(2,1)S(1)} %attention.1.refs_1_.refs_2_), channel_id=1, source_target_pairs={{0,1},{1,0},{2,3},{3,2},{4,5},{5,4},{6,7},{7,6},{8,9},{9,8},{10,11... | collective-permute-start | bytes 294920 | tf_op jit(solution)/shard_map/ppermute | solution.py:431
  63.5 4.8 %collective-permute-start.17 = (bf16[4,12288]{1,0:T(4,128)(2,1)S(1)}, bf16[4,12288]{1,0:T(4,128)(2,1)S(1)}, u32[]{:S(2)}, u32[]{:S(2)}) collective-permute-start(bf16[4,12288]{1,0:T(4,128)(2,1)S(1)} %collective-permute-done.11.refs_3_), channel_id=1, source_target_pairs={{0,1},{1,0},{2,3},{3,2},{4,5},{5,4},{6,7},{7,6},{8,9},{9,8},{10,11... | collective-permute-start | bytes 294920 | tf_op jit(solution)/shard_map/ppermute | solution.py:431
  64.1 4.3 %collective-permute-start.18 = (bf16[4,12288]{1,0:T(4,128)(2,1)S(1)}, bf16[4,12288]{1,0:T(4,128)(2,1)S(1)}, u32[]{:S(2)}, u32[]{:S(2)}) collective-permute-start(bf16[4,12288]{1,0:T(4,128)(2,1)S(1)} %collective-permute-done.9.refs_4_), channel_id=1, source_target_pairs={{0,1},{1,0},{2,3},{3,2},{4,5},{5,4},{6,7},{7,6},{8,9},{9,8},{10,11... | collective-permute-start | bytes 294920 | tf_op jit(solution)/shard_map/ppermute | solution.py:431
  67.2 1.6 %collective-permute-start.20 = (bf16[4,12288]{1,0:T(4,128)(2,1)S(1)}, bf16[4,12288]{1,0:T(4,128)(2,1)S(1)}, u32[]{:S(2)}, u32[]{:S(2)}) collective-permute-start(bf16[4,12288]{1,0:T(4,128)(2,1)S(1)} %collective-permute-done.10.refs_1_.refs_6_), channel_id=1, source_target_pairs={{0,1},{1,0},{2,3},{3,2},{4,5},{5,4},{6,7},{7,6},{8,9},{9,8},{10,11... | collective-permute-start | bytes 294920 | tf_op jit(solution)/shard_map/ppermute | solution.py:431
  67.8 1.3 %collective-permute-start.21 = (bf16[4,12288]{1,0:T(4,128)(2,1)S(1)}, bf16[4,12288]{1,0:T(4,128)(2,1)S(1)}, u32[]{:S(2)}, u32[]{:S(2)}) collective-permute-start(bf16[4,12288]{1,0:T(4,128)(2,1)S(1)} %collective-permute-done.14.refs_7_), channel_id=1, source_target_pairs={{0,1},{1,0},{2,3},{3,2},{4,5},{5,4},{6,7},{7,6},{8,9},{9,8},{10,11... | collective-permute-start | bytes 294920 | tf_op jit(solution)/shard_map/ppermute | solution.py:431
  67.9 1.4 %collective-permute-start.19 = (bf16[4,12288]{1,0:T(4,128)(2,1)S(1)}, bf16[4,12288]{1,0:T(4,128)(2,1)S(1)}, u32[]{:S(2)}, u32[]{:S(2)}) collective-permute-start(bf16[4,12288]{1,0:T(4,128)(2,1)S(1)} %collective-permute-done.12.refs_5_), channel_id=1, source_target_pairs={{0,1},{1,0},{2,3},{3,2},{4,5},{5,4},{6,7},{7,6},{8,9},{9,8},{10,11... | collective-permute-start | bytes 294920 | tf_op jit(solution)/shard_map/ppermute | solution.py:431
  68.3 1.3 %collective-permute-start.22 = (bf16[4,12288]{1,0:T(4,128)(2,1)S(1)}, bf16[4,12288]{1,0:T(4,128)(2,1)S(1)}, u32[]{:S(2)}, u32[]{:S(2)}) collective-permute-start(bf16[4,12288]{1,0:T(4,128)(2,1)S(1)} %collective-permute-done.13.refs_8_), channel_id=1, source_target_pairs={{0,1},{1,0},{2,3},{3,2},{4,5},{5,4},{6,7},{7,6},{8,9},{9,8},{10,11... | collective-permute-start | bytes 294920 | tf_op jit(solution)/shard_map/ppermute | solution.py:431
  68.4 1.4 %collective-permute-start.23 = (bf16[4,12288]{1,0:T(4,128)(2,1)S(1)}, bf16[4,12288]{1,0:T(4,128)(2,1)S(1)}, u32[]{:S(2)}, u32[]{:S(2)}) collective-permute-start(bf16[4,12288]{1,0:T(4,128)(2,1)S(1)} %collective-permute-done.15.refs_9_), channel_id=1, source_target_pairs={{0,1},{1,0},{2,3},{3,2},{4,5},{5,4},{6,7},{7,6},{8,9},{9,8},{10,11... | collective-permute-start | bytes 294920 | tf_op jit(solution)/shard_map/ppermute | solution.py:431

commit v9 on v8

--- a/solution.py
+++ b/solution.py
@@ -112,7 +112,7 @@
 
 MIB = 1 << 20
 EXTRA = 16
-OUT_CUTS = (4, 7)
+OUT_CUTS = (5, 7)
 IN_VMEM = pl.BlockSpec(memory_space=pltpu.VMEM)
 IN_SMEM = pl.BlockSpec(memory_space=pltpu.SMEM)
 IN_HBM = pl.BlockSpec(memory_space=pltpu.HBM)

time: 77.3 us -> 77.6 us (level)
  waiting for transfers between devices: 17.4 us -> 18.4 us
    ppermute x24, waiting for transfers between devices: 11.3 us -> 12.3 us  [swap(): return lax.ppermute(value, axis, [(at, at ^ bits) for at in range(size)])]
  transfers between devices with their start and end apart: 25 -> 25, of which waited for: 12 -> 13; matrix products, arithmetic and copies ran while one was open for 1% -> 1% of each run, Pallas kernels for 20% -> 19%
where the time goes in v9:
time: 77.6 us; the launch traced here: 77.3 us
  Pallas kernels  31.1 us (40%)
  starting transfers between devices  25.3 us (33%)
  waiting for transfers between devices  18.4 us (24%)
  local copies, waits for them, and re-layouts  1.6 us (2%)
    pallas_call x10, Pallas kernels, call(): pl.pallas_call(kernel, out_shape=out_shape, in_specs=in_specs or [IN_VMEM...  31.1 us
    ppermute x24, starting transfers between devices, swap(): return lax.ppermute(value, axis, [(at, at ^ bits) for at in range(size)])  21 us
    ppermute x24, waiting for transfers between devices, swap(): return lax.ppermute(value, axis, [(at, at ^ bits) for at in range(size)])  12.3 us
    all_to_all x1, waiting for transfers between devices, local_fast(): arrived = lax.all_to_all(outgoing, 'wide', 0, 0, tiled=True)  6.07 us
    all_to_all x1, starting transfers between devices, local_fast(): arrived = lax.all_to_all(outgoing, 'wide', 0, 0, tiled=True)  4.29 us
  transfers between devices with their start and end apart: 25, of which 13 were waited for; matrix products, arithmetic and copies ran while one was open for 1% of the time, Pallas kernels for 19%

profile of v9, /device:TPU:0, one launch (start us, length us, event | category | flops | bytes accessed | tf_op | source)
XLA Modules:
  0.0 77.3 jit_solution(12370903317918402971)
XLA Ops:
  0.0 0.0 copy-start
  0.0 0.9 %copy-done = bf16[4,16,1152]{2,1,0:T(8,128)(2,1)S(1)} copy-done((bf16[4,16,1152]{2,1,0:T(8,128)(2,1)S(1)}, bf16[4,16,1152]{2,1,0:T(8,128)(2,1)}, u32[]{:S(2)}) %copy-start) | copy-done | bytes 147480
  0.9 0.1 row_sums.1.mine
  1.0 0.5 collective-permute-start
  1.6 0.7 broadcast_in_dim.2.gain
  2.2 0.1 collective-permute-done.theirs
  2.4 4.0 %collective-permute-start.1 = (bf16[592,128]{1,0:T(8,128)(2,1)S(1)}, bf16[592,128]{1,0:T(8,128)(2,1)S(1)}, u32[]{:S(2)}, u32[]{:S(2)}) collective-permute-start(bf16[592,128]{1,0:T(8,128)(2,1)S(1)} %payload.1.refs_0_), channel_id=1, source_target_pairs={{0,8},{2,10},{4,12},{6,14},{8,0},{10,2},{12,4},{14,6},{1,9},{3,11}... | collective-permute-start | bytes 454664 | tf_op jit(solution)/shard_map/ppermute | solution.py:431
  6.4 1.6 %collective-permute-start.2 = (bf16[592,128]{1,0:T(8,128)(2,1)S(1)}, bf16[592,128]{1,0:T(8,128)(2,1)S(1)}, u32[]{:S(2)}, u32[]{:S(2)}) collective-permute-start(bf16[592,128]{1,0:T(8,128)(2,1)S(1)} %payload.1.refs_0_), channel_id=1, source_target_pairs={{0,4},{2,6},{4,0},{6,2},{8,12},{10,14},{12,8},{14,10},{1,5},{3,7},... | collective-permute-start | bytes 454664 | tf_op jit(solution)/shard_map/ppermute | solution.py:431
  8.0 1.5 %collective-permute-start.3 = (bf16[592,128]{1,0:T(8,128)(2,1)S(1)}, bf16[592,128]{1,0:T(8,128)(2,1)S(1)}, u32[]{:S(2)}, u32[]{:S(2)}) collective-permute-start(bf16[592,128]{1,0:T(8,128)(2,1)S(1)} %payload.1.refs_0_), channel_id=1, source_target_pairs={{0,2},{2,0},{4,6},{6,4},{8,10},{10,8},{12,14},{14,12},{1,3},{3,1},... | collective-permute-start | bytes 454664 | tf_op jit(solution)/shard_map/ppermute | solution.py:431
  9.5 4.6 %collective-permute-done.1.refs_4_ = bf16[592,128]{1,0:T(8,128)(2,1)S(1)} collective-permute-done((bf16[592,128]{1,0:T(8,128)(2,1)S(1)}, bf16[592,128]{1,0:T(8,128)(2,1)S(1)}, u32[]{:S(2)}, u32[]{:S(2)}) %collective-permute-start.1) | collective-permute-done | bytes 151584 | tf_op jit(solution)/shard_map/ppermute | solution.py:431
  14.0 0.2 collective-permute-done.2.refs_2_
  14.2 0.0 collective-permute-done.3.refs_1_
  14.2 1.5 %collective-permute-start.4 = (bf16[592,128]{1,0:T(8,128)(2,1)S(1)}, bf16[592,128]{1,0:T(8,128)(2,1)S(1)}, u32[]{:S(2)}, u32[]{:S(2)}) collective-permute-start(bf16[592,128]{1,0:T(8,128)(2,1)S(1)} %collective-permute-done.1.refs_4_), channel_id=1, source_target_pairs={{0,2},{2,0},{4,6},{6,4},{8,10},{10,8},{12,14},{14,12},{1,3},{3,1},... | collective-permute-start | bytes 454664 | tf_op jit(solution)/shard_map/ppermute | solution.py:431
  15.8 1.4 %collective-permute-start.6 = (bf16[592,128]{1,0:T(8,128)(2,1)S(1)}, bf16[592,128]{1,0:T(8,128)(2,1)S(1)}, u32[]{:S(2)}, u32[]{:S(2)}) collective-permute-start(bf16[592,128]{1,0:T(8,128)(2,1)S(1)} %collective-permute-done.1.refs_4_), channel_id=1, source_target_pairs={{0,4},{2,6},{4,0},{6,2},{8,12},{10,14},{12,8},{14,10},{1,5},{3,7},... | collective-permute-start | bytes 454664 | tf_op jit(solution)/shard_map/ppermute | solution.py:431
  17.2 2.2 %collective-permute-done.4.refs_5_ = bf16[592,128]{1,0:T(8,128)(2,1)S(1)} collective-permute-done((bf16[592,128]{1,0:T(8,128)(2,1)S(1)}, bf16[592,128]{1,0:T(8,128)(2,1)S(1)}, u32[]{:S(2)}, u32[]{:S(2)}) %collective-permute-start.4) | collective-permute-done | bytes 151584 | tf_op jit(solution)/shard_map/ppermute | solution.py:431
  19.4 1.5 %collective-permute-start.5 = (bf16[592,128]{1,0:T(8,128)(2,1)S(1)}, bf16[592,128]{1,0:T(8,128)(2,1)S(1)}, u32[]{:S(2)}, u32[]{:S(2)}) collective-permute-start(bf16[592,128]{1,0:T(8,128)(2,1)S(1)} %collective-permute-done.2.refs_2_), channel_id=1, source_target_pairs={{0,2},{2,0},{4,6},{6,4},{8,10},{10,8},{12,14},{14,12},{1,3},{3,1},... | collective-permute-start | bytes 454664 | tf_op jit(solution)/shard_map/ppermute | solution.py:431
  21.0 1.4 %collective-permute-start.7 = (bf16[592,128]{1,0:T(8,128)(2,1)S(1)}, bf16[592,128]{1,0:T(8,128)(2,1)S(1)}, u32[]{:S(2)}, u32[]{:S(2)}) collective-permute-start(bf16[592,128]{1,0:T(8,128)(2,1)S(1)} %collective-permute-done.4.refs_5_), channel_id=1, source_target_pairs={{0,4},{2,6},{4,0},{6,2},{8,12},{10,14},{12,8},{14,10},{1,5},{3,7},... | collective-permute-start | bytes 454664 | tf_op jit(solution)/shard_map/ppermute | solution.py:431
  22.4 6.6 %load_query_weights.1.early = bf16[9216,1024]{1,0:T(8,128)(2,1)S(1)} custom-call(bf16[9216,1536]{1,0:T(8,128)(2,1)} %w_query.1), custom_call_target="tpu_custom_call" | custom-call | bytes 18874368 | tf_op jit(solution)/shard_map/load_query_weights/pallas_call | solution.py:124
  29.0 0.1 pad_add_fusion.place
  29.1 0.0 collective-permute-done.6.refs_6_
  29.1 0.0 collective-permute-done.5.refs_3_
  29.1 0.0 collective-permute-done.7.refs_7_
  29.1 6.2 %norm_and_project.1 = (f32[32,2048]{1,0:T(8,128)S(1)}, f32[32,2048]{1,0:T(8,128)S(1)}) custom-call(s32[2]{0:T(128)S(1)} %pad_add_fusion.place, bf16[1152,512]{1,0:T(8,128)(2,1)} %w_keyval_far.1, bf16[9216,1536]{1,0:T(8,128)(2,1)} %w_query.1, bf16[9216,1024]{1,0:T(8,128)(2,1)S(1)} %load_query_weights.1.early, bf16[592,128]{1,0:T(8,128)(2,1)S(1)} %payload.1.refs_0_, ...), custom_call_target="tpu_custom_call" | custom-call | flops 1811939328 | bytes 49577992 | tf_op jit(solution)/shard_map/norm_and_project/pallas_call | solution.py:124
  35.3 0.1 collective-permute-start.8
  36.0 0.9 %collective-permute-done.8.theirs = f32[32,2048]{1,0:T(8,128)S(1)} collective-permute-done((f32[32,2048]{1,0:T(8,128)S(1)}, f32[32,2048]{1,0:T(8,128)S(1)}, u32[]{:S(2)}, u32[]{:S(2)}) %collective-permute-start.8) | collective-permute-done | bytes 262176 | tf_op jit(solution)/shard_map/ppermute | solution.py:431
  36.9 0.8 %sum_of_cores.1.refs_2_ = bf16[8,4,2560]{2,1,0:T(4,128)(2,1)} custom-call(f32[32,2048]{1,0:T(8,128)S(1)} %get-tuple-element.25.mine, f32[32,2048]{1,0:T(8,128)S(1)} %collective-permute-done.8.theirs), custom_call_target="tpu_custom_call" | custom-call | bytes 524288 | tf_op jit(solution)/shard_map/sum_of_cores/pallas_call | solution.py:124
  37.7 4.3 %all-to-all-start = ((bf16[8,4,2560]{2,1,0:T(4,128)(2,1)}), bf16[8,4,2560]{2,1,0:T(4,128)(2,1)S(1)}, u32[]{:S(2)}, u32[]{:S(2)}) async-start(bf16[8,4,2560]{2,1,0:T(4,128)(2,1)} %sum_of_cores.1.refs_2_), calls=%async_computation | async-start | bytes 327680 | tf_op jit(solution)/shard_map/all_to_all | solution.py:515
  42.0 0.1 multiply_sine_fusion
  42.1 1.6 %load_cache.1.cache = bf16[4096,256]{1,0:T(8,128)(2,1)S(1)} custom-call(bf16[2048,256]{1,0:T(8,128)(2,1)} %bitcast.9, bf16[2048,256]{1,0:T(8,128)(2,1)} %bitcast.10, bf16[8,4,2560]{2,1,0:T(4,128)(2,1)} %sum_of_cores.1.refs_2_), custom_call_target="tpu_custom_call" | custom-call | bytes 2097152 | tf_op jit(solution)/shard_map/load_cache/pallas_call | solution.py:124
  43.7 6.1 %all-to-all-done.arrived = bf16[8,4,2560]{2,1,0:T(4,128)(2,1)S(1)} async-done(((bf16[8,4,2560]{2,1,0:T(4,128)(2,1)}), bf16[8,4,2560]{2,1,0:T(4,128)(2,1)S(1)}, u32[]{:S(2)}, u32[]{:S(2)}) %all-to-all-start) | async-done | bytes 163872 | tf_op jit(solution)/shard_map/all_to_all | solution.py:515
  49.7 1.7 %attention.1.refs_1_.refs_2_ = bf16[4,12288]{1,0:T(4,128)(2,1)S(1)} custom-call(s32[1]{0:T(128)} %copy.9.length, f32[4,128]{1,0:T(4,128)S(1)} %get-tuple-element.36.cosine, f32[4,128]{1,0:T(4,128)S(1)} %get-tuple-element.35.sine, bf16[8,4,2560]{2,1,0:T(4,128)(2,1)S(1)} %all-to-all-done.arrived, bf16[4096,256]{1,0:T(8,128)(2,1)S(1)} %load_cache.1.cache), custom_call_target="tpu_custom_call" | custom-call | flops 402653184 | bytes 2265092 | tf_op jit(solution)/shard_map/attention/pallas_call | solution.py:124
  51.4 0.6 collective-permute-start.10
  52.1 0.3 collective-permute-start.11
  52.4 1.9 %collective-permute-start.9 = (bf16[4,12288]{1,0:T(4,128)(2,1)S(1)}, bf16[4,12288]{1,0:T(4,128)(2,1)S(1)}, u32[]{:S(2)}, u32[]{:S(2)}) collective-permute-start(bf16[4,12288]{1,0:T(4,128)(2,1)S(1)} %attention.1.refs_1_.refs_2_), channel_id=1, source_target_pairs={{0,4},{2,6},{4,0},{6,2},{8,12},{10,14},{12,8},{14,10},{1,5},{3,7},... | collective-permute-start | bytes 294920 | tf_op jit(solution)/shard_map/ppermute | solution.py:431
  54.3 4.5 %load_out_weights.2.refs_0_ = bf16[5120,1152]{1,0:T(8,128)(2,1)S(1)} custom-call(bf16[12288,1152]{1,0:T(8,128)(2,1)} %w_out.1, bf16[4,12288]{1,0:T(4,128)(2,1)S(1)} %attention.1.refs_1_.refs_2_), custom_call_target="tpu_custom_call" | custom-call | bytes 11796480 | tf_op jit(solution)/shard_map/load_out_weights/pallas_call | solution.py:124
  58.8 0.0 collective-permute-done.10.refs_1_.refs_6_
  58.8 0.0 collective-permute-done.11.refs_3_
  58.8 0.0 collective-permute-done.9.refs_4_
  58.8 0.7 collective-permute-start.14
  59.5 1.4 %collective-permute-start.12 = (bf16[4,12288]{1,0:T(4,128)(2,1)S(1)}, bf16[4,12288]{1,0:T(4,128)(2,1)S(1)}, u32[]{:S(2)}, u32[]{:S(2)}) collective-permute-start(bf16[4,12288]{1,0:T(4,128)(2,1)S(1)} %collective-permute-done.9.refs_4_), channel_id=1, source_target_pairs={{0,2},{2,0},{4,6},{6,4},{8,10},{10,8},{12,14},{14,12},{1,3},{3,1},... | collective-permute-start | bytes 294920 | tf_op jit(solution)/shard_map/ppermute | solution.py:431
  60.9 0.1 collective-permute-start.13
  61.0 2.5 %collective-permute-done.14.refs_7_ = bf16[4,12288]{1,0:T(4,128)(2,1)S(1)} collective-permute-done((bf16[4,12288]{1,0:T(4,128)(2,1)S(1)}, bf16[4,12288]{1,0:T(4,128)(2,1)S(1)}, u32[]{:S(2)}, u32[]{:S(2)}) %collective-permute-start.14) | collective-permute-done | bytes 98336 | tf_op jit(solution)/shard_map/ppermute | solution.py:431
  63.5 0.2 collective-permute-start.15
  63.7 0.0 collective-permute-start.16
  63.7 0.5 collective-permute-start.17
  64.2 0.3 collective-permute-done.12.refs_5_
  64.5 0.0 collective-permute-start.18
  64.5 2.4 %load_out_weights.3.refs_1_ = bf16[2048,1152]{1,0:T(8,128)(2,1)S(1)} custom-call(bf16[12288,1152]{1,0:T(8,128)(2,1)} %w_out.1, bf16[4,12288]{1,0:T(4,128)(2,1)S(1)} %collective-permute-done.10.refs_1_.refs_6_), custom_call_target="tpu_custom_call" | custom-call | bytes 4718592 | tf_op jit(solution)/shard_map/load_out_weights/pallas_call | solution.py:124
  66.9 0.0 collective-permute-done.13.refs_8_
  66.9 0.6 collective-permute-start.20
  67.5 0.6 collective-permute-done.15.refs_9_
  68.1 0.0 collective-permute-start.21
  68.1 0.0 collective-permute-done.16.refs_10_
  68.1 0.5 collective-permute-start.19
  68.6 0.0 collective-permute-done.17.refs_11_
  68.6 0.1 collective-permute-start.22
  68.7 0.0 collective-permute-done.18.refs_12_
  68.7 0.4 collective-permute-start.23
  69.1 0.0 collective-permute-done.20.refs_14_
  69.1 0.3 collective-permute-done.21.refs_15_
  69.4 0.2 collective-permute-done.19.refs_13_
  69.6 0.4 collective-permute-done.22.refs_16_
  69.9 0.2 collective-permute-done.23.refs_17_
  70.1 7.2 %project_out.1 = bf16[4,16,1152]{2,1,0:T(8,128)(2,1)} custom-call(s32[2]{0:T(128)S(1)} %pad_add_fusion.place, bf16[12288,1152]{1,0:T(8,128)(2,1)} %w_out.1, bf16[5120,1152]{1,0:T(8,128)(2,1)S(1)} %load_out_weights.2.refs_0_, bf16[2048,1152]{1,0:T(8,128)(2,1)S(1)} %load_out_weights.3.refs_1_, bf16[4,12288]{1,0:T(4,128)(2,1)S(1)} %attention.1.refs_1_.refs_2_, ...), custom_call_target="tpu_custom_call" | custom-call | flops 1811939328 | bytes 46399496 | tf_op jit(solution)/shard_map/project_out/pallas_call | solution.py:124
  (3 shorter events, 0.1 us)
Async XLA Ops:
  0.0 0.9 %copy-start = (bf16[4,16,1152]{2,1,0:T(8,128)(2,1)S(1)}, bf16[4,16,1152]{2,1,0:T(8,128)(2,1)}, u32[]{:S(2)}) copy-start(bf16[4,16,1152]{2,1,0:T(8,128)(2,1)} %param.8) | copy-start | bytes 442372
  1.0 1.3 %collective-permute-start = (f32[8,128]{1,0:T(8,128)S(1)}, f32[8,128]{1,0:T(8,128)S(1)}, u32[]{:S(2)}, u32[]{:S(2)}) collective-permute-start(f32[8,128]{1,0:T(8,128)S(1)} %row_sums.1.mine), channel_id=1, source_target_pairs={{0,1},{1,0},{2,3},{3,2},{4,5},{5,4},{6,7},{7,6},{8,9},{9,8},{10,11... | collective-permute-start | bytes 12296 | tf_op jit(solution)/shard_map/ppermute | solution.py:431
  2.4 11.6 %collective-permute-start.1 = (bf16[592,128]{1,0:T(8,128)(2,1)S(1)}, bf16[592,128]{1,0:T(8,128)(2,1)S(1)}, u32[]{:S(2)}, u32[]{:S(2)}) collective-permute-start(bf16[592,128]{1,0:T(8,128)(2,1)S(1)} %payload.1.refs_0_), channel_id=1, source_target_pairs={{0,8},{2,10},{4,12},{6,14},{8,0},{10,2},{12,4},{14,6},{1,9},{3,11}... | collective-permute-start | bytes 454664 | tf_op jit(solution)/shard_map/ppermute | solution.py:431
  6.4 7.8 %collective-permute-start.2 = (bf16[592,128]{1,0:T(8,128)(2,1)S(1)}, bf16[592,128]{1,0:T(8,128)(2,1)S(1)}, u32[]{:S(2)}, u32[]{:S(2)}) collective-permute-start(bf16[592,128]{1,0:T(8,128)(2,1)S(1)} %payload.1.refs_0_), channel_id=1, source_target_pairs={{0,4},{2,6},{4,0},{6,2},{8,12},{10,14},{12,8},{14,10},{1,5},{3,7},... | collective-permute-start | bytes 454664 | tf_op jit(solution)/shard_map/ppermute | solution.py:431
  8.0 6.2 %collective-permute-start.3 = (bf16[592,128]{1,0:T(8,128)(2,1)S(1)}, bf16[592,128]{1,0:T(8,128)(2,1)S(1)}, u32[]{:S(2)}, u32[]{:S(2)}) collective-permute-start(bf16[592,128]{1,0:T(8,128)(2,1)S(1)} %payload.1.refs_0_), channel_id=1, source_target_pairs={{0,2},{2,0},{4,6},{6,4},{8,10},{10,8},{12,14},{14,12},{1,3},{3,1},... | collective-permute-start | bytes 454664 | tf_op jit(solution)/shard_map/ppermute | solution.py:431
  14.2 5.2 %collective-permute-start.4 = (bf16[592,128]{1,0:T(8,128)(2,1)S(1)}, bf16[592,128]{1,0:T(8,128)(2,1)S(1)}, u32[]{:S(2)}, u32[]{:S(2)}) collective-permute-start(bf16[592,128]{1,0:T(8,128)(2,1)S(1)} %collective-permute-done.1.refs_4_), channel_id=1, source_target_pairs={{0,2},{2,0},{4,6},{6,4},{8,10},{10,8},{12,14},{14,12},{1,3},{3,1},... | collective-permute-start | bytes 454664 | tf_op jit(solution)/shard_map/ppermute | solution.py:431
  15.8 13.3 %collective-permute-start.6 = (bf16[592,128]{1,0:T(8,128)(2,1)S(1)}, bf16[592,128]{1,0:T(8,128)(2,1)S(1)}, u32[]{:S(2)}, u32[]{:S(2)}) collective-permute-start(bf16[592,128]{1,0:T(8,128)(2,1)S(1)} %collective-permute-done.1.refs_4_), channel_id=1, source_target_pairs={{0,4},{2,6},{4,0},{6,2},{8,12},{10,14},{12,8},{14,10},{1,5},{3,7},... | collective-permute-start | bytes 454664 | tf_op jit(solution)/shard_map/ppermute | solution.py:431
  19.4 9.7 %collective-permute-start.5 = (bf16[592,128]{1,0:T(8,128)(2,1)S(1)}, bf16[592,128]{1,0:T(8,128)(2,1)S(1)}, u32[]{:S(2)}, u32[]{:S(2)}) collective-permute-start(bf16[592,128]{1,0:T(8,128)(2,1)S(1)} %collective-permute-done.2.refs_2_), channel_id=1, source_target_pairs={{0,2},{2,0},{4,6},{6,4},{8,10},{10,8},{12,14},{14,12},{1,3},{3,1},... | collective-permute-start | bytes 454664 | tf_op jit(solution)/shard_map/ppermute | solution.py:431
  21.0 8.1 %collective-permute-start.7 = (bf16[592,128]{1,0:T(8,128)(2,1)S(1)}, bf16[592,128]{1,0:T(8,128)(2,1)S(1)}, u32[]{:S(2)}, u32[]{:S(2)}) collective-permute-start(bf16[592,128]{1,0:T(8,128)(2,1)S(1)} %collective-permute-done.4.refs_5_), channel_id=1, source_target_pairs={{0,4},{2,6},{4,0},{6,2},{8,12},{10,14},{12,8},{14,10},{1,5},{3,7},... | collective-permute-start | bytes 454664 | tf_op jit(solution)/shard_map/ppermute | solution.py:431
  35.3 1.6 %collective-permute-start.8 = (f32[32,2048]{1,0:T(8,128)S(1)}, f32[32,2048]{1,0:T(8,128)S(1)}, u32[]{:S(2)}, u32[]{:S(2)}) collective-permute-start(f32[32,2048]{1,0:T(8,128)S(1)} %get-tuple-element.26), channel_id=1, source_target_pairs={{0,1},{1,0},{2,3},{3,2},{4,5},{5,4},{6,7},{7,6},{8,9},{9,8},{10,11... | collective-permute-start | bytes 786440 | tf_op jit(solution)/shard_map/ppermute | solution.py:431
  37.7 12.1 %all-to-all-start = ((bf16[8,4,2560]{2,1,0:T(4,128)(2,1)}), bf16[8,4,2560]{2,1,0:T(4,128)(2,1)S(1)}, u32[]{:S(2)}, u32[]{:S(2)}) async-start(bf16[8,4,2560]{2,1,0:T(4,128)(2,1)} %sum_of_cores.1.refs_2_), calls=%async_computation | async-start | bytes 327680 | tf_op jit(solution)/shard_map/all_to_all | solution.py:515
  51.4 7.3 %collective-permute-start.10 = (bf16[4,12288]{1,0:T(4,128)(2,1)S(1)}, bf16[4,12288]{1,0:T(4,128)(2,1)S(1)}, u32[]{:S(2)}, u32[]{:S(2)}) collective-permute-start(bf16[4,12288]{1,0:T(4,128)(2,1)S(1)} %attention.1.refs_1_.refs_2_), channel_id=1, source_target_pairs={{0,8},{2,10},{4,12},{6,14},{8,0},{10,2},{12,4},{14,6},{1,9},{3,11}... | collective-permute-start | bytes 294920 | tf_op jit(solution)/shard_map/ppermute | solution.py:431
  52.1 6.7 %collective-permute-start.11 = (bf16[4,12288]{1,0:T(4,128)(2,1)S(1)}, bf16[4,12288]{1,0:T(4,128)(2,1)S(1)}, u32[]{:S(2)}, u32[]{:S(2)}) collective-permute-start(bf16[4,12288]{1,0:T(4,128)(2,1)S(1)} %attention.1.refs_1_.refs_2_), channel_id=1, source_target_pairs={{0,2},{2,0},{4,6},{6,4},{8,10},{10,8},{12,14},{14,12},{1,3},{3,1},... | collective-permute-start | bytes 294920 | tf_op jit(solution)/shard_map/ppermute | solution.py:431
  52.4 6.4 %collective-permute-start.9 = (bf16[4,12288]{1,0:T(4,128)(2,1)S(1)}, bf16[4,12288]{1,0:T(4,128)(2,1)S(1)}, u32[]{:S(2)}, u32[]{:S(2)}) collective-permute-start(bf16[4,12288]{1,0:T(4,128)(2,1)S(1)} %attention.1.refs_1_.refs_2_), channel_id=1, source_target_pairs={{0,4},{2,6},{4,0},{6,2},{8,12},{10,14},{12,8},{14,10},{1,5},{3,7},... | collective-permute-start | bytes 294920 | tf_op jit(solution)/shard_map/ppermute | solution.py:431
  58.8 4.7 %collective-permute-start.14 = (bf16[4,12288]{1,0:T(4,128)(2,1)S(1)}, bf16[4,12288]{1,0:T(4,128)(2,1)S(1)}, u32[]{:S(2)}, u32[]{:S(2)}) collective-permute-start(bf16[4,12288]{1,0:T(4,128)(2,1)S(1)} %collective-permute-done.10.refs_1_.refs_6_), channel_id=1, source_target_pairs={{0,2},{2,0},{4,6},{6,4},{8,10},{10,8},{12,14},{14,12},{1,3},{3,1},... | collective-permute-start | bytes 294920 | tf_op jit(solution)/shard_map/ppermute | solution.py:431
  59.5 5.1 %collective-permute-start.12 = (bf16[4,12288]{1,0:T(4,128)(2,1)S(1)}, bf16[4,12288]{1,0:T(4,128)(2,1)S(1)}, u32[]{:S(2)}, u32[]{:S(2)}) collective-permute-start(bf16[4,12288]{1,0:T(4,128)(2,1)S(1)} %collective-permute-done.9.refs_4_), channel_id=1, source_target_pairs={{0,2},{2,0},{4,6},{6,4},{8,10},{10,8},{12,14},{14,12},{1,3},{3,1},... | collective-permute-start | bytes 294920 | tf_op jit(solution)/shard_map/ppermute | solution.py:431
  60.9 6.0 %collective-permute-start.13 = (bf16[4,12288]{1,0:T(4,128)(2,1)S(1)}, bf16[4,12288]{1,0:T(4,128)(2,1)S(1)}, u32[]{:S(2)}, u32[]{:S(2)}) collective-permute-start(bf16[4,12288]{1,0:T(4,128)(2,1)S(1)} %collective-permute-done.10.refs_1_.refs_6_), channel_id=1, source_target_pairs={{0,4},{2,6},{4,0},{6,2},{8,12},{10,14},{12,8},{14,10},{1,5},{3,7},... | collective-permute-start | bytes 294920 | tf_op jit(solution)/shard_map/ppermute | solution.py:431
  63.5 4.6 %collective-permute-start.15 = (bf16[4,12288]{1,0:T(4,128)(2,1)S(1)}, bf16[4,12288]{1,0:T(4,128)(2,1)S(1)}, u32[]{:S(2)}, u32[]{:S(2)}) collective-permute-start(bf16[4,12288]{1,0:T(4,128)(2,1)S(1)} %collective-permute-done.14.refs_7_), channel_id=1, source_target_pairs={{0,4},{2,6},{4,0},{6,2},{8,12},{10,14},{12,8},{14,10},{1,5},{3,7},... | collective-permute-start | bytes 294920 | tf_op jit(solution)/shard_map/ppermute | solution.py:431
  63.7 4.4 %collective-permute-start.16 = (bf16[4,12288]{1,0:T(4,128)(2,1)S(1)}, bf16[4,12288]{1,0:T(4,128)(2,1)S(1)}, u32[]{:S(2)}, u32[]{:S(2)}) collective-permute-start(bf16[4,12288]{1,0:T(4,128)(2,1)S(1)} %attention.1.refs_1_.refs_2_), channel_id=1, source_target_pairs={{0,1},{1,0},{2,3},{3,2},{4,5},{5,4},{6,7},{7,6},{8,9},{9,8},{10,11... | collective-permute-start | bytes 294920 | tf_op jit(solution)/shard_map/ppermute | solution.py:431
  63.7 4.9 %collective-permute-start.17 = (bf16[4,12288]{1,0:T(4,128)(2,1)S(1)}, bf16[4,12288]{1,0:T(4,128)(2,1)S(1)}, u32[]{:S(2)}, u32[]{:S(2)}) collective-permute-start(bf16[4,12288]{1,0:T(4,128)(2,1)S(1)} %collective-permute-done.11.refs_3_), channel_id=1, source_target_pairs={{0,1},{1,0},{2,3},{3,2},{4,5},{5,4},{6,7},{7,6},{8,9},{9,8},{10,11... | collective-permute-start | bytes 294920 | tf_op jit(solution)/shard_map/ppermute | solution.py:431
  64.5 4.2 %collective-permute-start.18 = (bf16[4,12288]{1,0:T(4,128)(2,1)S(1)}, bf16[4,12288]{1,0:T(4,128)(2,1)S(1)}, u32[]{:S(2)}, u32[]{:S(2)}) collective-permute-start(bf16[4,12288]{1,0:T(4,128)(2,1)S(1)} %collective-permute-done.9.refs_4_), channel_id=1, source_target_pairs={{0,1},{1,0},{2,3},{3,2},{4,5},{5,4},{6,7},{7,6},{8,9},{9,8},{10,11... | collective-permute-start | bytes 294920 | tf_op jit(solution)/shard_map/ppermute | solution.py:431
  66.9 2.2 %collective-permute-start.20 = (bf16[4,12288]{1,0:T(4,128)(2,1)S(1)}, bf16[4,12288]{1,0:T(4,128)(2,1)S(1)}, u32[]{:S(2)}, u32[]{:S(2)}) collective-permute-start(bf16[4,12288]{1,0:T(4,128)(2,1)S(1)} %collective-permute-done.10.refs_1_.refs_6_), channel_id=1, source_target_pairs={{0,1},{1,0},{2,3},{3,2},{4,5},{5,4},{6,7},{7,6},{8,9},{9,8},{10,11... | collective-permute-start | bytes 294920 | tf_op jit(solution)/shard_map/ppermute | solution.py:431
  68.1 1.3 %collective-permute-start.21 = (bf16[4,12288]{1,0:T(4,128)(2,1)S(1)}, bf16[4,12288]{1,0:T(4,128)(2,1)S(1)}, u32[]{:S(2)}, u32[]{:S(2)}) collective-permute-start(bf16[4,12288]{1,0:T(4,128)(2,1)S(1)} %collective-permute-done.14.refs_7_), channel_id=1, source_target_pairs={{0,1},{1,0},{2,3},{3,2},{4,5},{5,4},{6,7},{7,6},{8,9},{9,8},{10,11... | collective-permute-start | bytes 294920 | tf_op jit(solution)/shard_map/ppermute | solution.py:431
  68.1 1.5 %collective-permute-start.19 = (bf16[4,12288]{1,0:T(4,128)(2,1)S(1)}, bf16[4,12288]{1,0:T(4,128)(2,1)S(1)}, u32[]{:S(2)}, u32[]{:S(2)}) collective-permute-start(bf16[4,12288]{1,0:T(4,128)(2,1)S(1)} %collective-permute-done.12.refs_5_), channel_id=1, source_target_pairs={{0,1},{1,0},{2,3},{3,2},{4,5},{5,4},{6,7},{7,6},{8,9},{9,8},{10,11... | collective-permute-start | bytes 294920 | tf_op jit(solution)/shard_map/ppermute | solution.py:431
  68.6 1.3 %collective-permute-start.22 = (bf16[4,12288]{1,0:T(4,128)(2,1)S(1)}, bf16[4,12288]{1,0:T(4,128)(2,1)S(1)}, u32[]{:S(2)}, u32[]{:S(2)}) collective-permute-start(bf16[4,12288]{1,0:T(4,128)(2,1)S(1)} %collective-permute-done.13.refs_8_), channel_id=1, source_target_pairs={{0,1},{1,0},{2,3},{3,2},{4,5},{5,4},{6,7},{7,6},{8,9},{9,8},{10,11... | collective-permute-start | bytes 294920 | tf_op jit(solution)/shard_map/ppermute | solution.py:431
  68.7 1.4 %collective-permute-start.23 = (bf16[4,12288]{1,0:T(4,128)(2,1)S(1)}, bf16[4,12288]{1,0:T(4,128)(2,1)S(1)}, u32[]{:S(2)}, u32[]{:S(2)}) collective-permute-start(bf16[4,12288]{1,0:T(4,128)(2,1)S(1)} %collective-permute-done.15.refs_9_), channel_id=1, source_target_pairs={{0,1},{1,0},{2,3},{3,2},{4,5},{5,4},{6,7},{7,6},{8,9},{9,8},{10,11... | collective-permute-start | bytes 294920 | tf_op jit(solution)/shard_map/ppermute | solution.py:431
